TPU v7x, 128 devices: a whole 4x4x4 slice. The times are simulated.
128 devices in a mesh: dp: 32 (over z, x, core), tensor: 4 (over y).
Axes of the slice: x: 4, y: 4, z: 4, core: 2. Of those that a mesh axis runs over, the one named last changes fastest.
Arguments:
- activations: bfloat16 [16384, 4096], P('dp'), may hold values from -6 to 6
- gate_up_grads: bfloat16 [2, 16384, 11008], P(None, 'dp', 'tensor'), may hold values from -60 to 60
- hidden_act: bfloat16 [16384, 11008], P('dp', 'tensor'), may hold values from -60 to 60
- down_out_grad: bfloat16 [16384, 4096], P('dp'), may hold values from -6 to 6
- bases: bfloat16 [3, 4096, 512], replicated, may hold values from -0.25 to 0.25
- first_moment: float32 [3, 4, 2752, 512], P(None, 'tensor', 'dp'), may hold values from -6 to 6
- second_moment: float32 [3, 4, 2752, 512], P(None, 'tensor', 'dp'), may hold values from 0.05 to 2
Outputs:
- gate_update: bfloat16 [4096, 11008], P('dp', 'tensor')
- up_update: bfloat16 [4096, 11008], P('dp', 'tensor')
- down_update: bfloat16 [11008, 4096], P('tensor', 'dp')
- new_first: float32 [3, 4, 2752, 512], P(None, 'tensor', 'dp')
- new_second: float32 [3, 4, 2752, 512], P(None, 'tensor', 'dp')
All inputs are finite; a program needn't handle non-finite values.
Results may differ from a plain program's by a relative error of at most 0.013.
Values may be sent and summed in bfloat16 or wider, within the bound.
No kernel may reach another device: no remote copies, remote signals or barrier semaphores. Data moves between devices by JAX's collectives and lax.ppermute only.
A program may use at most 192 MiB of HBM per device.

v0:
```python
import jax
import jax.numpy as jnp
from jax import lax
from jax.sharding import PartitionSpec as P

STEP = 10


def global_squares(values):
    return lax.psum(jnp.sum(values * values), ("dp", "tensor"))


def body(activations, gate_up_grads, hidden_act, down_out_grad, bases, first_moment, second_moment):
    unit_count = hidden_act.shape[1]
    rank_width = bases.shape[2]
    dp_rows = bases.shape[1] // lax.axis_size("dp")
    total_units = unit_count * lax.axis_size("tensor")
    gate_reduced = jnp.dot(activations, bases[0], preferred_element_type=jnp.float32).astype(
        jnp.bfloat16
    )
    up_reduced = jnp.dot(activations, bases[1], preferred_element_type=jnp.float32).astype(
        jnp.bfloat16
    )
    down_reduced = jnp.dot(down_out_grad, bases[2], preferred_element_type=jnp.float32).astype(
        jnp.bfloat16
    )
    out_grad = gate_up_grads[0]
    up_out_grad = gate_up_grads[1]
    every_term = jnp.stack(
        [
            jnp.dot(out_grad.T, gate_reduced, preferred_element_type=jnp.float32),
            jnp.dot(up_out_grad.T, up_reduced, preferred_element_type=jnp.float32),
            jnp.dot(hidden_act.T, down_reduced, preferred_element_type=jnp.float32),
        ]
    )
    owned_rows = lax.psum_scatter(
        every_term.astype(jnp.bfloat16), "dp", scatter_dimension=1, tiled=True
    ).astype(jnp.float32)
    square_sum = global_squares(owned_rows)
    clip_limit = jnp.sqrt(jnp.float32(3 * rank_width * total_units))
    factor = jnp.minimum(jnp.float32(1.0), clip_limit / jnp.sqrt(square_sum))
    clipped = owned_rows * factor
    moment_one = 0.9 * first_moment[:, 0] + 0.1 * clipped
    moment_two = 0.95 * second_moment[:, 0] + 0.05 * clipped * clipped
    direction = (
        moment_one / (1.0 - 0.9**STEP) / (jnp.sqrt(moment_two / (1.0 - 0.95**STEP)) + 1e-08)
    ).astype(jnp.bfloat16)
    gathered = lax.all_gather(direction, "dp", axis=1, tiled=True)
    local_basis = lax.dynamic_slice_in_dim(bases, lax.axis_index("dp") * dp_rows, dp_rows, 1)
    gate_and_up = jnp.einsum(
        "kdr,kfr->kdf", local_basis[:2], gathered[:2], preferred_element_type=jnp.float32
    ).astype(jnp.bfloat16)
    gate_update = gate_and_up[0]
    up_update = gate_and_up[1]
    down_update = jnp.dot(gathered[2], local_basis[2].T, preferred_element_type=jnp.float32).astype(
        jnp.bfloat16
    )
    return (gate_update, up_update, down_update, moment_one[:, None], moment_two[:, None])


def solution(mesh):
    placed = (
        P("dp", None),
        P(None, "dp", "tensor"),
        P("dp", "tensor"),
        P("dp", None),
        P(),
        P(None, "tensor", "dp", None),
        P(None, "tensor", "dp", None),
    )
    return jax.shard_map(
        body,
        mesh=mesh,
        in_specs=placed,
        out_specs=(
            P("dp", "tensor"),
            P("dp", "tensor"),
            P("tensor", "dp"),
            P(None, "tensor", "dp", None),
            P(None, "tensor", "dp", None),
        ),
        check_vma=False,
    )
```

profile of v0, /device:TPU:0, one launch (start us, length us, event | category | flops | bytes accessed | tf_op | source)
XLA Modules:
  0.0 317.4 jit_solution(8968801775634359531)
XLA Ops:
  7.2 0.0 copy-start
  7.2 0.0 all-reduce.3.cloned.1.call-start
  7.2 9.8 %fusion.11 = bf16[1,2752,512]{2,1,0:T(8,128)(2,1)} fusion(bf16[2,512,2752]{1,2,0:T(8,128)(2,1)} %param.8, bf16[512,4096]{1,0:T(8,128)(2,1)} %param.7, bf16[3,4096,512]{2,1,0:T(8,128)(2,1)} %param.11), kind=kOutput, calls=%fused_computation.15 | convolution fusion | flops 3591995392 | bytes 14024704 | tf_op jit(solution)/shard_map/dot_general | solution.py:31
  17.0 9.8 %fusion.12 = bf16[1,2752,512]{2,1,0:T(8,128)(2,1)} fusion(bf16[2,512,2752]{1,2,0:T(8,128)(2,1)} %param.8, bf16[512,4096]{1,0:T(8,128)(2,1)} %param.7, bf16[3,4096,512]{2,1,0:T(8,128)(2,1)} %param.11), kind=kOutput, calls=%fused_computation.16 | convolution fusion | flops 3591995392 | bytes 14024704 | tf_op jit(solution)/shard_map/dot_general | solution.py:32
  26.8 0.0 copy-done
  26.8 9.0 %fusion.13 = bf16[1,2752,512]{2,1,0:T(8,128)(2,1)} fusion(bf16[512,2752]{0,1:T(8,128)(2,1)S(1)} %copy-done, bf16[512,4096]{1,0:T(8,128)(2,1)} %param.10, bf16[3,4096,512]{2,1,0:T(8,128)(2,1)} %param.11), kind=kOutput, calls=%fused_computation.17 | convolution fusion | flops 3591995392 | bytes 14024704 | tf_op jit(solution)/shard_map/dot_general | solution.py:33
  35.8 7.2 %pad_maximum_fusion = bf16[3,2752,512]{2,1,0:T(8,128)(2,1)} fusion(bf16[1,2752,512]{2,1,0:T(8,128)(2,1)} %fusion.13, bf16[1,2752,512]{2,1,0:T(8,128)(2,1)} %fusion.12, bf16[1,2752,512]{2,1,0:T(8,128)(2,1)} %fusion.11), kind=kLoop, calls=%fused_computation | loop fusion | flops 8454144 | bytes 16908288 | tf_op jit(solution)/shard_map/stack | solution.py:29
  42.9 0.0 copy-start.5
  42.9 0.0 copy-start.3
  42.9 0.0 copy-start.4
  42.9 0.0 all-reduce.3.cloned.1.call-update
  43.0 0.0 all-gather.2.cloned.1.call-start
  43.0 0.6 copy-done.5
  43.6 0.6 dynamic-slice
  44.8 122.3 %all-reduce.3.cloned.1.call-done = bf16[3,2752,512]{2,1,0:T(8,128)(2,1)} async-done(((bf16[3,2752,512]{2,1,0:T(8,128)(2,1)}), bf16[3,2752,512]{2,1,0:T(8,128)(2,1)}) %all-reduce.3.cloned.1.call-update) | async-done | bytes 8454160
  167.1 1.7 fusion.38
  168.8 65.6 %psum.7 = f32[]{:T(128)} all-reduce(f32[]{:T(128)} %fusion.38), channel_id=1, replica_groups=mesh['dp'=32,'tensor'=4] {'dp','tensor'}, use_global_device_ids=true, to_apply=%region_2.0 | all-reduce | flops 1 | bytes 8 | tf_op jit(solution)/shard_map/psum | solution.py:10
  235.1 0.0 copy-done.3
  235.1 0.0 copy-done.4
  235.2 1.4 fusion.42
  236.6 0.9 copy.24
  237.5 0.0 all-gather.2.cloned.1.call-update
  237.5 1.3 copy.27
  238.9 1.3 copy.28
  240.2 54.0 %all-gather.2.cloned.1.call-done = bf16[3,2752,512]{2,0,1:T(4,128)(2,1)} async-done(((bf16[3,86,512]{2,0,1:T(4,128)(2,1)}), bf16[3,2752,512]{2,0,1:T(4,128)(2,1)}) %all-gather.2.cloned.1.call-update) | async-done | bytes 8454160 | tf_op jit(solution)/shard_map/all_gather | solution.py:48
  294.2 2.6 slice-done
  296.8 2.7 fusion.14
  299.5 1.2 slice_bitcast_fusion
  300.7 0.9 copy-done.2
  301.6 6.3 %slice.47 = bf16[1,2752,512]{2,0,1:T(2,128)(2,1)S(1)} slice(bf16[3,2752,512]{2,0,1:T(4,128)(2,1)S(1)} %copy-done.2), slice={[2:3], [0:2752], [0:512]} | slice | bytes 5636096 | tf_op jit(solution)/shard_map/slice | solution.py:55
  307.9 2.7 convolution_convert_fusion.3
  310.6 0.0 copy-done.1
  (3 shorter events, 0.0 us)
Async XLA Ops:
  7.2 19.6 %copy-start = (bf16[512,2752]{0,1:T(8,128)(2,1)S(1)}, bf16[512,2752]{0,1:T(8,128)(2,1)}, u32[]{:S(2)}) copy-start(bf16[512,2752]{0,1:T(8,128)(2,1)} %param.9) | copy-start | bytes 8454148
  7.2 159.9 %all-reduce.3.cloned.1.call-start = ((), (), s32[]{:S(2)}) async-start(), calls=%async_computation.1 | async-start | bytes 16908288
  42.9 0.7 copy-start.5
  42.9 192.2 %copy-start.3 = (f32[3,1,86,512]{3,1,2,0:T(1,128)S(1)}, f32[3,1,86,512]{3,1,2,0:T(1,128)}, u32[]{:S(2)}) copy-start(f32[3,1,86,512]{3,1,2,0:T(1,128)} %param.13) | copy-start | bytes 1585156
  42.9 192.2 %copy-start.4 = (f32[3,1,86,512]{3,1,2,0:T(1,128)S(1)}, f32[3,1,86,512]{3,1,2,0:T(1,128)}, u32[]{:S(2)}) copy-start(f32[3,1,86,512]{3,1,2,0:T(1,128)} %param.12) | copy-start | bytes 1585156
  43.0 251.3 %all-gather.2.cloned.1.call-start = ((), (), s32[]{:S(2)}) async-start(), calls=%async_computation | async-start | bytes 11624448 | tf_op jit(solution)/shard_map/all_gather | solution.py:48
  294.2 2.6 slice-start
  296.8 4.8 %copy-start.2 = (bf16[3,2752,512]{2,0,1:T(4,128)(2,1)S(1)}, bf16[3,2752,512]{2,0,1:T(4,128)(2,1)}, u32[]{:S(2)}) copy-start(bf16[3,2752,512]{2,0,1:T(4,128)(2,1)} %all-gather.2.cloned.1.call-done) | copy-start | bytes 25362436
  301.6 9.0 %copy-start.1 = (bf16[512,2752]{0,1:T(8,128)(2,1)S(1)}, bf16[512,2752]{0,1:T(8,128)(2,1)}, u32[]{:S(2)}) copy-start(bf16[512,2752]{0,1:T(8,128)(2,1)} %param.9) | copy-start | bytes 8454148
Sparse Core Ops, SparseCore 0:
  43.1 123.9 all-reduce.2
  237.6 56.5 all-gather.1
where the time goes:
time: 319 us; the launch traced here: 317 us
  waiting for transfers between devices  176 us (55%)
  blocking collectives  65.6 us (21%)
  matrix products  33.9 us (11%)
  local copies, waits for them, and re-layouts  15.8 us (5%)
  between operations  15.4 us (5%)
  other arithmetic  10.3 us (3%)
    unnamed x3, waiting for transfers between devices  122 us
    psum x1, blocking collectives, global_squares(): return lax.psum(jnp.sum(values * values), ('dp', 'tensor'))  65.6 us
    all_gather x1, waiting for transfers between devices, body(): gathered = lax.all_gather(direction, 'dp', axis=1, tiled=True)  54 us
    dot_general x1, matrix products, body(): jnp.dot(up_out_grad.T, up_reduced, preferred_element_type=jnp.float32)  9.8 us
    dot_general x1, matrix products, body(): jnp.dot(out_grad.T, gate_reduced, preferred_element_type=jnp.float32)  9.78 us
    dot_general x1, matrix products, body(): jnp.dot(hidden_act.T, down_reduced, preferred_element_type=jnp.float32)  8.96 us
    another operation x1, other arithmetic, body(): jnp.stack([jnp.dot(out_grad.T, gate_reduced, preferred_element_type=jnp.f...  7.16 us
  transfers between devices with their start and end apart: 2, of which 2 were waited for; matrix products, arithmetic and copies ran while one was open for 1% of the time, Pallas kernels for 0%

commit v1 on v0

v1 whole, which is shorter than its diff:
```python
import functools

import jax
import jax.numpy as jnp
from jax import lax
from jax.experimental import pallas as pl
from jax.experimental.pallas import tpu as pltpu
from jax.sharding import PartitionSpec as P

STEP = 10
N_Z, N_X, N_C = 4, 4, 2
N_DP = N_Z * N_X * N_C
UNITS = 86
PAD = 88
LANES = 128
BF16 = jnp.bfloat16
F32 = jnp.float32
MB = 1 << 20


def dp_index(z, x, c):
    return ((z % N_Z) * N_X + (x % N_X)) * N_C + c % N_C


def every_chip():
    return [(z, x, c) for z in range(N_Z) for x in range(N_X) for c in range(N_C)]


CORE_PAIRS = [(dp_index(z, x, c), dp_index(z, x, c + 1)) for z, x, c in every_chip()]


def along_x(s):
    return [(dp_index(z, x, c), dp_index(z, x + s, c)) for z, x, c in every_chip()]


def along_z(s):
    return [(dp_index(z, x, c), dp_index(z + s, x, c)) for z, x, c in every_chip()]


VMEM = pl.BlockSpec(memory_space=pltpu.VMEM)
SMEM = pl.BlockSpec(memory_space=pltpu.SMEM)


def params(mib, **more):
    return pltpu.CompilerParams(vmem_limit_bytes=mib * MB, **more)


def project_kernel(place, a_ref, b_ref, g_ref, keep_ref, send_ref, acc, terms):
    k = pl.program_id(0)
    part = jnp.dot(a_ref[...], b_ref[0], preferred_element_type=F32)

    @pl.when(k == 0)
    def _():
        acc[...] = part

    @pl.when(k > 0)
    def _():
        acc[...] += part

    @pl.when(k == pl.num_programs(0) - 1)
    def _():
        z0, x0, c0 = place[0], place[1], place[2]
        half = 2 * LANES
        mine = acc[:, pl.ds(pl.multiple_of(c0 * half, half), half)].astype(BF16)
        other = acc[:, pl.ds(pl.multiple_of((1 - c0) * half, half), half)].astype(BF16)
        reduced = jnp.concatenate([mine, other], axis=1)
        units = g_ref.shape[-1]

        def rows(at, count):
            g = g_ref[0, :, pl.ds(at, count)]
            terms[pl.ds(at, count), :] = lax.dot_general(
                g, reduced, (((0,), (0,)), ((), ())), preferred_element_type=F32
            )

        block = 256
        whole = units // block

        @pl.loop(0, whole)
        def _(j):
            rows(pl.multiple_of(j * block, block), block)

        if units % block:
            rows(whole * block, units % block)
        terms[units:, :] = jnp.zeros((terms.shape[0] - units, terms.shape[1]), F32)

        for z in range(N_Z):
            for x in range(N_X):
                sz = lax.rem(z - z0 + N_Z, N_Z)
                sx = lax.rem(x - x0 + N_X, N_X)
                for c in range(N_C):
                    own = lax.rem(c + c0, 2)
                    at = dp_index(z, x, c) * UNITS
                    chunk = terms[at : at + PAD, :].astype(BF16)
                    keep_ref[0, sx, sz, own] = chunk[:, 0:128]
                    keep_ref[1, sz, sx, own] = chunk[:, 128:256]
                    send_ref[0, sx, sz, 1 - own] = chunk[:, 256:384]
                    send_ref[1, sz, sx, 1 - own] = chunk[:, 384:512]


def project(place, a, bases, matrix, g, g_at):
    tokens, width = a.shape
    rank = bases.shape[2]
    units = g.shape[2]
    steps = 8
    wide = width // steps
    shape = (2, 4, 4, N_C, PAD, LANES)
    whole = pl.BlockSpec(shape, lambda k, s: (0,) * 6)
    return pl.pallas_call(
        project_kernel,
        grid_spec=pltpu.PrefetchScalarGridSpec(
            num_scalar_prefetch=1,
            grid=(steps,),
            in_specs=[
                pl.BlockSpec((tokens, wide), lambda k, s: (0, k)),
                pl.BlockSpec((1, wide, rank), lambda k, s: (matrix, k, 0)),
                pl.BlockSpec((1, tokens, units), lambda k, s: (g_at, 0, 0)),
            ],
            out_specs=[whole, whole],
            scratch_shapes=[
                pltpu.VMEM((tokens, rank), F32),
                pltpu.VMEM((N_DP * UNITS + 8, rank), F32),
            ],
        ),
        out_shape=[jax.ShapeDtypeStruct(shape, BF16)] * 2,
        compiler_params=params(40),
        cost_estimate=pl.CostEstimate(
            flops=2 * tokens * rank * (width + units),
            bytes_accessed=2 * (tokens * width + width * rank + tokens * units + units * rank),
            transcendentals=0,
        ),
        name="project",
    )(place, a, bases, g)


def pair_kernel(*refs):
    keep, recv, outs = refs[0:3], refs[3:6], refs[6:]
    step = pl.program_id(0)
    for i, out in enumerate(outs):

        @pl.when(step == i)
        def _(out=out):
            for m in range(3):
                out[:, m] = (keep[m][0].astype(F32) + recv[m][0].astype(F32)).astype(BF16)


def pair_sum(keep, recv):
    flat = [t.reshape(8, 4, N_C, PAD, LANES) for t in (*keep, *recv)]
    shape = (4, 3, N_C, PAD, LANES)
    return pl.pallas_call(
        pair_kernel,
        grid=(8,),
        in_specs=[pl.BlockSpec((1, 4, N_C, PAD, LANES), lambda i: (i, 0, 0, 0, 0))] * 6,
        out_specs=[pl.BlockSpec(shape, lambda i: (0,) * 5)] * 8,
        out_shape=[jax.ShapeDtypeStruct(shape, BF16)] * 8,
        compiler_params=params(32),
        name="pair_sum",
    )(*flat)


def stage_kernel(own, r1, r2, r3, *outs):
    for i, out in enumerate(outs):
        total = own[i].astype(F32) + r1[i].astype(F32)
        total = total + (r2[i].astype(F32) + r3[i].astype(F32))
        out[...] = total.astype(BF16)


def stage_sum(terms):
    shape = terms[0].shape[1:]
    return pl.pallas_call(
        stage_kernel,
        in_specs=[VMEM] * 4,
        out_specs=[VMEM] * 4,
        out_shape=[jax.ShapeDtypeStruct(shape, BF16)] * 4,
        compiler_params=params(16),
        name="stage_sum",
    )(*terms)


def owned_kernel(*refs):
    parts, (mine, fix, squares) = refs[:8], refs[8:]
    inside = lax.broadcasted_iota(jnp.int32, (PAD, LANES), 0) < UNITS
    total_sq = jnp.zeros((PAD, LANES), F32)
    for half in range(2):
        t = parts[4 * half : 4 * half + 4]
        lanes = slice(half * LANES, half * LANES + LANES)
        for m in range(3):
            for c in range(N_C):
                v = t[0][m, c].astype(F32) + t[1][m, c].astype(F32)
                v = v + (t[2][m, c].astype(F32) + t[3][m, c].astype(F32))
                total_sq += jnp.where(inside, v * v, 0.0)
                if c == 0:
                    mine[m, :, lanes] = v
                else:
                    fix[m, :, lanes] = v.astype(BF16)
    row = jnp.sum(total_sq, axis=0, keepdims=True)
    squares[...] = jnp.broadcast_to(row, squares.shape)


def owned_sum(first, second, peers):
    return pl.pallas_call(
        owned_kernel,
        in_specs=[VMEM] * 8,
        out_specs=[VMEM] * 3,
        out_shape=[
            jax.ShapeDtypeStruct((3, PAD, 2 * LANES), F32),
            jax.ShapeDtypeStruct((3, PAD, 2 * LANES), BF16),
            jax.ShapeDtypeStruct((peers, LANES), F32),
        ],
        compiler_params=params(16),
        name="owned_sum",
    )(*first, *second)


def adam_kernel(limit_sq, place, squares, mine, recv, first, second, new_first, new_second, direction):
    total = jnp.sum(squares[...])
    clip_limit = jnp.sqrt(jnp.full((1, 1), limit_sq, F32))
    factor = jnp.minimum(1.0, clip_limit / jnp.sqrt(jnp.full((1, 1), total, F32)))
    low = place[2] == 0
    for m in range(3):
        here = mine[m]
        there = recv[m].astype(F32)
        lower = jnp.where(low, here, there)
        upper = jnp.where(low, there, here)
        clipped = jnp.concatenate([lower, upper], axis=1)[:UNITS] * factor
        one = 0.9 * first[m] + 0.1 * clipped
        two = 0.95 * second[m] + 0.05 * clipped * clipped
        new_first[m] = one
        new_second[m] = two
        way = one / (1.0 - 0.9**STEP) / (jnp.sqrt(two / (1.0 - 0.95**STEP)) + 1e-08)
        padded = jnp.concatenate([way, jnp.zeros((PAD - UNITS, way.shape[1]), F32)], axis=0)
        direction[m] = padded.astype(BF16)


def adam(limit_sq, place, squares, mine, recv, first, second):
    rank = first.shape[-1]
    moment = jax.ShapeDtypeStruct((3, UNITS, rank), F32)
    return pl.pallas_call(
        functools.partial(adam_kernel, limit_sq),
        in_specs=[SMEM] + [VMEM] * 5,
        out_specs=[VMEM] * 3,
        out_shape=[moment, moment, jax.ShapeDtypeStruct((3, PAD, rank), BF16)],
        compiler_params=params(16),
        name="adam",
    )(place, squares, mine, recv, first, second)


def update_kernel(way, bases, out):
    for m in range(3):
        full = lax.dot_general(
            way[m], bases[m], (((1,), (1,)), ((), ())), preferred_element_type=F32
        ).astype(BF16)
        for j in range(out.shape[0]):
            out[j, m] = full[:, j * LANES : (j + 1) * LANES]


def updates(way, bases):
    width, rank = bases.shape[1:]
    wide = 512
    shape = (width // LANES, 3, PAD, LANES)
    return pl.pallas_call(
        update_kernel,
        grid=(width // wide,),
        in_specs=[
            pl.BlockSpec((3, PAD, rank), lambda i: (0, 0, 0)),
            pl.BlockSpec((3, wide, rank), lambda i: (0, i, 0)),
        ],
        out_specs=pl.BlockSpec((wide // LANES, 3, PAD, LANES), lambda i: (i, 0, 0, 0)),
        out_shape=jax.ShapeDtypeStruct(shape, BF16),
        compiler_params=params(24),
        name="updates",
    )(way, bases)


def layout_kernel(pieces, gate, up, down, rows):
    units = N_DP * UNITS
    for m, out in enumerate((gate, up, down)):
        for k in range(N_DP):
            rows[k * UNITS : k * UNITS + PAD, :] = pieces[k, m].astype(F32)
        if m == 2:
            out[...] = rows[:units, :].astype(BF16)
            continue
        for at in range(0, units, LANES):
            count = min(LANES, units - at)
            out[:, at : at + count] = rows[at : at + count, :].T.astype(BF16)


def layout(pieces):
    units = N_DP * UNITS
    return pl.pallas_call(
        layout_kernel,
        in_specs=[VMEM],
        out_specs=[VMEM] * 3,
        out_shape=[
            jax.ShapeDtypeStruct((LANES, units), BF16),
            jax.ShapeDtypeStruct((LANES, units), BF16),
            jax.ShapeDtypeStruct((units, LANES), BF16),
        ],
        scratch_shapes=[pltpu.VMEM((units + 8, LANES), F32)],
        compiler_params=params(24),
        name="layout",
    )(pieces)


def body(activations, gate_up_grads, hidden_act, down_out_grad, bases, first_moment, second_moment):
    devices = lax.axis_size("dp") * lax.axis_size("tensor")
    total_units = hidden_act.shape[1] * lax.axis_size("tensor")
    me = lax.axis_index("dp")
    place = jnp.stack([me // (N_X * N_C), (me // N_C) % N_X, me % N_C]).astype(jnp.int32)

    keep, recv = [], []
    for m, (a, g, at) in enumerate(
        (
            (activations, gate_up_grads, 0),
            (activations, gate_up_grads, 1),
            (down_out_grad, hidden_act[None], 0),
        )
    ):
        kept, sent = project(place, a, bases, m, g, at)
        keep.append(kept)
        recv.append(lax.ppermute(sent, "dp", CORE_PAIRS))

    cut = pair_sum(keep, recv)
    by_x, by_z = cut[:4], cut[4:]
    by_x = [by_x[0]] + [lax.ppermute(by_x[s], "dp", along_x(s)) for s in (1, 2, 3)]
    by_z = [by_z[0]] + [lax.ppermute(by_z[s], "dp", along_z(s)) for s in (1, 2, 3)]
    by_x = stage_sum(by_x)
    by_z = stage_sum(by_z)
    first = [by_x[0]] + [lax.ppermute(by_x[s], "dp", along_z(s)) for s in (1, 2, 3)]
    second = [by_z[0]] + [lax.ppermute(by_z[s], "dp", along_x(s)) for s in (1, 2, 3)]
    mine, fix, squares = owned_sum(first, second, devices)
    fix = lax.ppermute(fix, "dp", CORE_PAIRS)
    squares = lax.all_to_all(squares, ("dp", "tensor"), 0, 0, tiled=True)

    limit_sq = float(3 * bases.shape[2] * total_units)
    new_first, new_second, way = adam(
        limit_sq, place, squares, mine, fix, first_moment[:, 0], second_moment[:, 0]
    )
    pieces = lax.all_to_all(updates(way, bases), "dp", 0, 0, tiled=True)
    gate_update, up_update, down_update = layout(pieces)
    return (gate_update, up_update, down_update, new_first[:, None], new_second[:, None])


def solution(mesh):
    placed = (
        P("dp", None),
        P(None, "dp", "tensor"),
        P("dp", "tensor"),
        P("dp", None),
        P(),
        P(None, "tensor", "dp", None),
        P(None, "tensor", "dp", None),
    )
    return jax.shard_map(
        body,
        mesh=mesh,
        in_specs=placed,
        out_specs=(
            P("dp", "tensor"),
            P("dp", "tensor"),
            P("tensor", "dp"),
            P(None, "tensor", "dp", None),
            P(None, "tensor", "dp", None),
        ),
        check_vma=False,
    )
```

time: 319 us -> 186 us (0.58)
  waiting for transfers between devices: 176 us -> 60.8 us
  blocking collectives: 65.6 us -> 0 us
  Pallas kernels: 0 us -> 54.2 us
  starting transfers between devices: 0.08 us -> 36.6 us
  matrix products: 33.9 us -> 0 us
  local copies, waits for them, and re-layouts: 15.8 us -> 32.2 us
  between operations: 15.4 us -> 0.84 us
  other arithmetic: 10.3 us -> 0.08 us
    unnamed x3 -> x0, waiting for transfers between devices: 122 us -> none
    psum x1 -> x0, blocking collectives: 65.6 us -> none  [global_squares(): return lax.psum(jnp.sum(values * values), ('dp', 'tensor'))]
    pallas_call x0 -> x10, Pallas kernels: none -> 54.2 us  [the longest x3 38.6 us: project(): pl.pallas_call(project_kernel, grid_spec=pltpu.PrefetchScalarGridSpec(num...]
    all_gather x1 -> x0, waiting for transfers between devices: 54 us -> none  [body(): gathered = lax.all_gather(direction, 'dp', axis=1, tiled=True)]
    all_to_all x0 -> x2, waiting for transfers between devices: none -> 37.2 us  [the longest x1 28.1 us: body(): pieces = lax.all_to_all(updates(way, bases), 'dp', 0, 0, tiled=True)]
    dot_general x5 -> x0, matrix products: 33.9 us -> none  [the longest x1 9.8 us: body(): jnp.dot(up_out_grad.T, up_reduced, preferred_element_type=jnp.float32)]
    unnamed x15 -> x29, local copies, waits for them, and re-layouts: 4.74 us -> 32.2 us
    ppermute x0 -> x16, starting transfers between devices: none -> 24.5 us  [the longest x3 6.95 us: body(): lax.ppermute(by_x[s], 'dp', along_x(s))]
  transfers between devices with their start and end apart: 2 -> 18, of which waited for: 2 -> 7; matrix products, arithmetic and copies ran while one was open for 1% -> 3% of each run, Pallas kernels for 0% -> 14%
where the time goes in v1:
time: 186 us; the launch traced here: 185 us
  waiting for transfers between devices  60.8 us (33%)
  Pallas kernels  54.2 us (29%)
  starting transfers between devices  36.6 us (20%)
  local copies, waits for them, and re-layouts  32.2 us (17%)
    pallas_call x3, Pallas kernels, project(): pl.pallas_call(project_kernel, grid_spec=pltpu.PrefetchScalarGridSpec(num...  38.6 us
    unnamed x29, local copies, waits for them, and re-layouts  32.2 us
    all_to_all x1, waiting for transfers between devices, body(): pieces = lax.all_to_all(updates(way, bases), 'dp', 0, 0, tiled=True)  28.1 us
    ppermute x3, waiting for transfers between devices, body(): lax.ppermute(by_z[s], 'dp', along_z(s))  15.9 us
    all_to_all x1, waiting for transfers between devices, body(): squares = lax.all_to_all(squares, ('dp', 'tensor'), 0, 0, tiled=True)  9.11 us
    all_to_all x1, starting transfers between devices, body(): squares = lax.all_to_all(squares, ('dp', 'tensor'), 0, 0, tiled=True)  7.99 us
    ppermute x3, starting transfers between devices, body(): lax.ppermute(by_x[s], 'dp', along_x(s))  6.95 us
    pallas_call x1, Pallas kernels, updates(): pl.pallas_call(update_kernel, grid=(width // wide,), in_specs=[pl.BlockSp...  6.47 us
  transfers between devices with their start and end apart: 18, of which 7 were waited for; matrix products, arithmetic and copies ran while one was open for 3% of the time, Pallas kernels for 14%

profile of v1, /device:TPU:0, one launch (start us, length us, event | category | flops | bytes accessed | tf_op | source)
XLA Modules:
  0.0 184.8 jit_solution(3794828457059540571)
XLA Ops:
  0.7 8.3 %copy.19.g_ref = bf16[2,512,2752]{2,1,0:T(8,128)(2,1)} copy(bf16[2,512,2752]{1,2,0:T(8,128)(2,1)} %param.8) | data formatting | bytes 11272192 | tf_op args[1]
  9.1 2.6 %copy-done.1 = bf16[2,512,2752]{2,1,0:T(8,128)(2,1)S(1)} copy-done((bf16[2,512,2752]{2,1,0:T(8,128)(2,1)S(1)}, bf16[2,512,2752]{2,1,0:T(8,128)(2,1)}, u32[]{:S(2)}) %copy-start.1) | copy-done | bytes 5636120
  11.7 2.2 %copy-done.2 = bf16[512,4096]{1,0:T(8,128)(2,1)S(1)} copy-done((bf16[512,4096]{1,0:T(8,128)(2,1)S(1)}, bf16[512,4096]{1,0:T(8,128)(2,1)}, u32[]{:S(2)}) %copy-start.2) | copy-done | bytes 4194328
  13.9 13.1 %project.3 = (bf16[2,4,4,2,88,128]{5,4,3,2,1,0:T(8,128)(2,1)S(1)}, bf16[2,4,4,2,88,128]{5,4,3,2,1,0:T(8,128)(2,1)}) custom-call(s32[3]{0:T(128)S(1)} %pad_add_fusion.place, bf16[512,4096]{1,0:T(8,128)(2,1)S(1)} %copy-done.2, bf16[3,4096,512]{2,1,0:T(8,128)(2,1)} %bases.1, bf16[2,512,2752]{2,1,0:T(8,128)(2,1)S(1)} %copy-done.1), custom_call_target="tpu_custom_call" | custom-call | flops 3590324224 | bytes 14024704 | tf_op jit(solution)/shard_map/project/pallas_call | solution.py:108
  28.1 13.2 %project.4 = (bf16[2,4,4,2,88,128]{5,4,3,2,1,0:T(8,128)(2,1)S(1)}, bf16[2,4,4,2,88,128]{5,4,3,2,1,0:T(8,128)(2,1)}) custom-call(s32[3]{0:T(128)S(1)} %pad_add_fusion.place, bf16[512,4096]{1,0:T(8,128)(2,1)S(1)} %copy-done.2, bf16[3,4096,512]{2,1,0:T(8,128)(2,1)} %bases.1, bf16[2,512,2752]{2,1,0:T(8,128)(2,1)S(1)} %copy-done.1), custom_call_target="tpu_custom_call" | custom-call | flops 3590324224 | bytes 14024704 | tf_op jit(solution)/shard_map/project/pallas_call | solution.py:108
  42.9 3.1 %copy.21 = bf16[512,2752]{1,0:T(8,128)(2,1)S(1)} copy(bf16[512,2752]{0,1:T(8,128)(2,1)} %param.9) | data formatting | bytes 5636096 | tf_op args[2]
  46.0 2.2 %copy-done.3 = bf16[512,4096]{1,0:T(8,128)(2,1)S(1)} copy-done((bf16[512,4096]{1,0:T(8,128)(2,1)S(1)}, bf16[512,4096]{1,0:T(8,128)(2,1)}, u32[]{:S(2)}) %copy-start.3) | copy-done | bytes 4194328
  48.2 12.3 %project.5 = (bf16[2,4,4,2,88,128]{5,4,3,2,1,0:T(8,128)(2,1)S(1)}, bf16[2,4,4,2,88,128]{5,4,3,2,1,0:T(8,128)(2,1)S(1)}) custom-call(s32[3]{0:T(128)S(1)} %pad_add_fusion.place, bf16[512,4096]{1,0:T(8,128)(2,1)S(1)} %copy-done.3, bf16[3,4096,512]{2,1,0:T(8,128)(2,1)} %bases.1, bf16[1,512,2752]{2,1,0:T(8,128)(2,1)S(1)} %bitcast.20), custom_call_target="tpu_custom_call" | custom-call | flops 3590324224 | bytes 14024704 | tf_op jit(solution)/shard_map/project/pallas_call | solution.py:108
  60.6 3.2 %collective-permute-done.2 = bf16[2,4,4,2,88,128]{5,4,3,2,1,0:T(8,128)(2,1)S(1)} collective-permute-done((bf16[2,4,4,2,88,128]{5,4,3,2,1,0:T(8,128)(2,1)S(1)}, bf16[2,4,4,2,88,128]{5,4,3,2,1,0:T(8,128)(2,1)S(1)}, u32[]{:S(2)}, u32[]{:S(2)}) %collective-permute-start.2) | collective-permute-done | bytes 1441824 | tf_op jit(solution)/shard_map/ppermute | solution.py:320
  63.8 5.0 %pair_sum.1 = (bf16[4,3,2,88,128]{4,3,2,1,0:T(8,128)(2,1)S(1)}, bf16[4,3,2,88,128]{4,3,2,1,0:T(8,128)(2,1)S(1)}, bf16[4,3,2,88,128]{4,3,2,1,0:T(8,128)(2,1)S(1)}...) custom-call(bf16[8,4,2,88,128]{4,3,2,1,0:T(8,128)(2,1)S(1)} %bitcast, ...), custom_call_target="tpu_custom_call" | custom-call | tf_op jit(solution)/shard_map/pair_sum/pallas_call | solution.py:149
  68.8 4.0 %collective-permute-start.10 = (bf16[4,3,2,88,128]{4,3,2,1,0:T(8,128)(2,1)S(1)}, bf16[4,3,2,88,128]{4,3,2,1,0:T(8,128)(2,1)S(1)}, u32[]{:S(2)}, u32[]{:S(2)}) collective-permute-start(bf16[4,3,2,88,128]{4,3,2,1,0:T(8,128)(2,1)S(1)} %get-tuple-element.52), channel_id=1, source_target_pairs={{0,64},{4,68},{8,72},{12,76},{16,80},{20,84},{24,88},{28,92},{32,9... | collective-permute-start | bytes 1622024 | tf_op jit(solution)/shard_map/ppermute | solution.py:325
  74.9 1.5 collective-permute-start.3
  76.4 2.7 %collective-permute-start.4 = (bf16[4,3,2,88,128]{4,3,2,1,0:T(8,128)(2,1)S(1)}, bf16[4,3,2,88,128]{4,3,2,1,0:T(8,128)(2,1)S(1)}, u32[]{:S(2)}, u32[]{:S(2)}) collective-permute-start(bf16[4,3,2,88,128]{4,3,2,1,0:T(8,128)(2,1)S(1)} %get-tuple-element.44), channel_id=1, source_target_pairs={{0,16},{4,20},{8,24},{12,28},{16,0},{20,4},{24,8},{28,12},{32,48},... | collective-permute-start | bytes 1622024 | tf_op jit(solution)/shard_map/ppermute | solution.py:324
  79.1 6.9 %collective-permute-done.10.r2 = bf16[4,3,2,88,128]{4,3,2,1,0:T(8,128)(2,1)S(1)} collective-permute-done((bf16[4,3,2,88,128]{4,3,2,1,0:T(8,128)(2,1)S(1)}, bf16[4,3,2,88,128]{4,3,2,1,0:T(8,128)(2,1)S(1)}, u32[]{:S(2)}, u32[]{:S(2)}) %collective-permute-start.10) | collective-permute-done | bytes 540704 | tf_op jit(solution)/shard_map/ppermute | solution.py:325
  86.0 2.7 %collective-permute-start.5 = (bf16[4,3,2,88,128]{4,3,2,1,0:T(8,128)(2,1)S(1)}, bf16[4,3,2,88,128]{4,3,2,1,0:T(8,128)(2,1)S(1)}, u32[]{:S(2)}, u32[]{:S(2)}) collective-permute-start(bf16[4,3,2,88,128]{4,3,2,1,0:T(8,128)(2,1)S(1)} %get-tuple-element.45), channel_id=1, source_target_pairs={{0,24},{4,28},{8,0},{12,4},{16,8},{20,12},{24,16},{28,20},{32,56},... | collective-permute-start | bytes 1622024 | tf_op jit(solution)/shard_map/ppermute | solution.py:324
  88.7 9.1 %collective-permute-done.11.r3 = bf16[4,3,2,88,128]{4,3,2,1,0:T(8,128)(2,1)S(1)} collective-permute-done((bf16[4,3,2,88,128]{4,3,2,1,0:T(8,128)(2,1)S(1)}, bf16[4,3,2,88,128]{4,3,2,1,0:T(8,128)(2,1)S(1)}, u32[]{:S(2)}, u32[]{:S(2)}) %collective-permute-start.11) | collective-permute-done | bytes 540704 | tf_op jit(solution)/shard_map/ppermute | solution.py:325
  98.1 1.6 collective-permute-start.12
  99.6 2.7 %collective-permute-start.13 = (bf16[3,2,88,128]{3,2,1,0:T(8,128)(2,1)S(1)}, bf16[3,2,88,128]{3,2,1,0:T(8,128)(2,1)S(1)}, u32[]{:S(2)}, u32[]{:S(2)}) collective-permute-start(bf16[3,2,88,128]{3,2,1,0:T(8,128)(2,1)S(1)} %get-tuple-element.56), channel_id=1, source_target_pairs={{0,16},{4,20},{8,24},{12,28},{16,0},{20,4},{24,8},{28,12},{32,48},... | collective-permute-start | bytes 405512 | tf_op jit(solution)/shard_map/ppermute | solution.py:329
  102.3 1.5 collective-permute-start.14
  105.1 3.1 %collective-permute-start.7 = (bf16[3,2,88,128]{3,2,1,0:T(8,128)(2,1)S(1)}, bf16[3,2,88,128]{3,2,1,0:T(8,128)(2,1)S(1)}, u32[]{:S(2)}, u32[]{:S(2)}) collective-permute-start(bf16[3,2,88,128]{3,2,1,0:T(8,128)(2,1)S(1)} %get-tuple-element.48), channel_id=1, source_target_pairs={{0,64},{4,68},{8,72},{12,76},{16,80},{20,84},{24,88},{28,92},{32,9... | collective-permute-start | bytes 405512 | tf_op jit(solution)/shard_map/ppermute | solution.py:328
  109.3 2.6 %collective-permute-done.6.refs_1_ = bf16[3,2,88,128]{3,2,1,0:T(8,128)(2,1)S(1)} collective-permute-done((bf16[3,2,88,128]{3,2,1,0:T(8,128)(2,1)S(1)}, bf16[3,2,88,128]{3,2,1,0:T(8,128)(2,1)S(1)}, u32[]{:S(2)}, u32[]{:S(2)}) %collective-permute-start.6) | collective-permute-done | bytes 135200 | tf_op jit(solution)/shard_map/ppermute | solution.py:328
  111.8 1.9 %collective-permute-done.7.refs_2_ = bf16[3,2,88,128]{3,2,1,0:T(8,128)(2,1)S(1)} collective-permute-done((bf16[3,2,88,128]{3,2,1,0:T(8,128)(2,1)S(1)}, bf16[3,2,88,128]{3,2,1,0:T(8,128)(2,1)S(1)}, u32[]{:S(2)}, u32[]{:S(2)}) %collective-permute-start.7) | collective-permute-done | bytes 135200 | tf_op jit(solution)/shard_map/ppermute | solution.py:328
  114.6 8.0 %all-to-all-start = ((f32[128,1,128]{2,1,0:T(1,128)}), f32[128,1,128]{2,1,0:T(1,128)S(1)}, u32[]{:S(2)}, u32[]{:S(2)}) async-start(f32[128,1,128]{2,1,0:T(1,128)} %bitcast.11), calls=%async_computation | async-start | bytes 131072 | tf_op jit(solution)/shard_map/all_to_all | solution.py:332
  122.7 9.1 %all-to-all-done = f32[128,1,128]{2,1,0:T(1,128)S(1)} async-done(((f32[128,1,128]{2,1,0:T(1,128)}), f32[128,1,128]{2,1,0:T(1,128)S(1)}, u32[]{:S(2)}, u32[]{:S(2)}) %all-to-all-start) | async-done | bytes 65568 | tf_op jit(solution)/shard_map/all_to_all | solution.py:332
  133.1 4.6 %copy-done = bf16[3,4096,512]{2,1,0:T(8,128)(2,1)S(1)} copy-done((bf16[3,4096,512]{2,1,0:T(8,128)(2,1)S(1)}, bf16[3,4096,512]{2,1,0:T(8,128)(2,1)}, u32[]{:S(2)}) %copy-start) | copy-done | bytes 12582936
  137.7 6.5 %updates.1 = bf16[32,3,88,128]{3,2,1,0:T(8,128)(2,1)} custom-call(bf16[3,88,512]{2,1,0:T(8,128)(2,1)S(1)} %get-tuple-element.61.way, bf16[3,4096,512]{2,1,0:T(8,128)(2,1)S(1)} %copy-done), custom_call_target="tpu_custom_call" | custom-call | tf_op jit(solution)/shard_map/updates/pallas_call | solution.py:260
  144.2 4.1 %all-to-all-start.1 = ((bf16[32,3,88,128]{3,2,1,0:T(8,128)(2,1)}), bf16[32,3,88,128]{3,2,1,0:T(8,128)(2,1)S(1)}, u32[]{:S(2)}, u32[]{:S(2)}) async-start(bf16[32,3,88,128]{3,2,1,0:T(8,128)(2,1)} %updates.1), calls=%async_computation.1 | async-start | bytes 4325376 | tf_op jit(solution)/shard_map/all_to_all | solution.py:338
  148.2 1.3 copy.25
  149.6 1.3 copy.26
  150.9 28.1 %all-to-all-done.1.pieces = bf16[32,3,88,128]{3,2,1,0:T(8,128)(2,1)S(1)} async-done(((bf16[32,3,88,128]{3,2,1,0:T(8,128)(2,1)}), bf16[32,3,88,128]{3,2,1,0:T(8,128)(2,1)S(1)}, u32[]{:S(2)}, u32[]{:S(2)}) %all-to-all-start.1) | async-done | bytes 2162720 | tf_op jit(solution)/shard_map/all_to_all | solution.py:338
  179.0 1.5 layout.1
  181.4 2.2 %copy.23 = bf16[128,2752]{0,1:T(8,128)(2,1)} copy(bf16[128,2752]{1,0:T(8,128)(2,1)} %copy-done.8) | data formatting | bytes 1409024
  (44 shorter events, 11.8 us)
Async XLA Ops:
  9.1 2.6 %copy-start.1 = (bf16[2,512,2752]{2,1,0:T(8,128)(2,1)S(1)}, bf16[2,512,2752]{2,1,0:T(8,128)(2,1)}, u32[]{:S(2)}) copy-start(bf16[2,512,2752]{2,1,0:T(8,128)(2,1)} %copy.19.g_ref) | copy-start | bytes 16908292
  11.7 2.2 %copy-start.2 = (bf16[512,4096]{1,0:T(8,128)(2,1)S(1)}, bf16[512,4096]{1,0:T(8,128)(2,1)}, u32[]{:S(2)}) copy-start(bf16[512,4096]{1,0:T(8,128)(2,1)} %a_ref.4) | copy-start | bytes 12582916
  27.0 1.1 copy-start.4
  28.1 32.5 %collective-permute-start = (bf16[2,4,4,2,88,128]{5,4,3,2,1,0:T(8,128)(2,1)}, bf16[2,4,4,2,88,128]{5,4,3,2,1,0:T(8,128)(2,1)}, u32[]{:S(2)}, u32[]{:S(2)}) collective-permute-start(bf16[2,4,4,2,88,128]{5,4,3,2,1,0:T(8,128)(2,1)} %get-tuple-element.39), channel_id=1, source_target_pairs={{0,4},{4,0},{8,12},{12,8},{16,20},{20,16},{24,28},{28,24},{32,36},... | collective-permute-start | bytes 4325384 | tf_op jit(solution)/shard_map/ppermute | solution.py:320
  41.3 1.1 copy-start.6
  42.4 18.2 %collective-permute-start.1 = (bf16[2,4,4,2,88,128]{5,4,3,2,1,0:T(8,128)(2,1)}, bf16[2,4,4,2,88,128]{5,4,3,2,1,0:T(8,128)(2,1)}, u32[]{:S(2)}, u32[]{:S(2)}) collective-permute-start(bf16[2,4,4,2,88,128]{5,4,3,2,1,0:T(8,128)(2,1)} %get-tuple-element.40), channel_id=1, source_target_pairs={{0,4},{4,0},{8,12},{12,8},{16,20},{20,16},{24,28},{28,24},{32,36},... | collective-permute-start | bytes 4325384 | tf_op jit(solution)/shard_map/ppermute | solution.py:320
  46.0 2.2 %copy-start.3 = (bf16[512,4096]{1,0:T(8,128)(2,1)S(1)}, bf16[512,4096]{1,0:T(8,128)(2,1)}, u32[]{:S(2)}) copy-start(bf16[512,4096]{1,0:T(8,128)(2,1)} %a_ref.5) | copy-start | bytes 12582916
  48.2 15.6 %copy-start.5 = (bf16[2,4,4,2,88,128]{5,4,3,2,1,0:T(8,128)(2,1)S(1)}, bf16[2,4,4,2,88,128]{5,4,3,2,1,0:T(8,128)(2,1)}, u32[]{:S(2)}) copy-start(bf16[2,4,4,2,88,128]{5,4,3,2,1,0:T(8,128)(2,1)} %copy-done.4) | copy-start | bytes 4325380
  48.2 15.6 %copy-start.7 = (bf16[2,4,4,2,88,128]{5,4,3,2,1,0:T(8,128)(2,1)S(1)}, bf16[2,4,4,2,88,128]{5,4,3,2,1,0:T(8,128)(2,1)}, u32[]{:S(2)}) copy-start(bf16[2,4,4,2,88,128]{5,4,3,2,1,0:T(8,128)(2,1)} %copy-done.6) | copy-start | bytes 4325380
  60.5 3.3 %collective-permute-start.2 = (bf16[2,4,4,2,88,128]{5,4,3,2,1,0:T(8,128)(2,1)S(1)}, bf16[2,4,4,2,88,128]{5,4,3,2,1,0:T(8,128)(2,1)S(1)}, u32[]{:S(2)}, u32[]{:S(2)}) collective-permute-start(bf16[2,4,4,2,88,128]{5,4,3,2,1,0:T(8,128)(2,1)S(1)} %get-tuple-element.41), channel_id=1, source_target_pairs={{0,4},{4,0},{8,12},{12,8},{16,20},{20,16},{24,28},{28,24},{32,36},... | collective-permute-start | bytes 4325384 | tf_op jit(solution)/shard_map/ppermute | solution.py:320
  68.8 17.2 %collective-permute-start.10 = (bf16[4,3,2,88,128]{4,3,2,1,0:T(8,128)(2,1)S(1)}, bf16[4,3,2,88,128]{4,3,2,1,0:T(8,128)(2,1)S(1)}, u32[]{:S(2)}, u32[]{:S(2)}) collective-permute-start(bf16[4,3,2,88,128]{4,3,2,1,0:T(8,128)(2,1)S(1)} %get-tuple-element.52), channel_id=1, source_target_pairs={{0,64},{4,68},{8,72},{12,76},{16,80},{20,84},{24,88},{28,92},{32,9... | collective-permute-start | bytes 1622024 | tf_op jit(solution)/shard_map/ppermute | solution.py:325
  72.9 24.9 %collective-permute-start.11 = (bf16[4,3,2,88,128]{4,3,2,1,0:T(8,128)(2,1)S(1)}, bf16[4,3,2,88,128]{4,3,2,1,0:T(8,128)(2,1)S(1)}, u32[]{:S(2)}, u32[]{:S(2)}) collective-permute-start(bf16[4,3,2,88,128]{4,3,2,1,0:T(8,128)(2,1)S(1)} %get-tuple-element.53), channel_id=1, source_target_pairs={{0,96},{4,100},{8,104},{12,108},{16,112},{20,116},{24,120},{28,124... | collective-permute-start | bytes 1622024 | tf_op jit(solution)/shard_map/ppermute | solution.py:325
  73.6 24.2 %collective-permute-start.9 = (bf16[4,3,2,88,128]{4,3,2,1,0:T(8,128)(2,1)S(1)}, bf16[4,3,2,88,128]{4,3,2,1,0:T(8,128)(2,1)S(1)}, u32[]{:S(2)}, u32[]{:S(2)}) collective-permute-start(bf16[4,3,2,88,128]{4,3,2,1,0:T(8,128)(2,1)S(1)} %get-tuple-element.51), channel_id=1, source_target_pairs={{0,32},{4,36},{8,40},{12,44},{16,48},{20,52},{24,56},{28,60},{32,6... | collective-permute-start | bytes 1622024 | tf_op jit(solution)/shard_map/ppermute | solution.py:325
  74.9 27.5 %collective-permute-start.3 = (bf16[4,3,2,88,128]{4,3,2,1,0:T(8,128)(2,1)S(1)}, bf16[4,3,2,88,128]{4,3,2,1,0:T(8,128)(2,1)S(1)}, u32[]{:S(2)}, u32[]{:S(2)}) collective-permute-start(bf16[4,3,2,88,128]{4,3,2,1,0:T(8,128)(2,1)S(1)} %get-tuple-element.43), channel_id=1, source_target_pairs={{0,8},{4,12},{8,16},{12,20},{16,24},{20,28},{24,0},{28,4},{32,40},... | collective-permute-start | bytes 1622024 | tf_op jit(solution)/shard_map/ppermute | solution.py:324
  76.4 27.5 %collective-permute-start.4 = (bf16[4,3,2,88,128]{4,3,2,1,0:T(8,128)(2,1)S(1)}, bf16[4,3,2,88,128]{4,3,2,1,0:T(8,128)(2,1)S(1)}, u32[]{:S(2)}, u32[]{:S(2)}) collective-permute-start(bf16[4,3,2,88,128]{4,3,2,1,0:T(8,128)(2,1)S(1)} %get-tuple-element.44), channel_id=1, source_target_pairs={{0,16},{4,20},{8,24},{12,28},{16,0},{20,4},{24,8},{28,12},{32,48},... | collective-permute-start | bytes 1622024 | tf_op jit(solution)/shard_map/ppermute | solution.py:324
  86.0 17.9 %collective-permute-start.5 = (bf16[4,3,2,88,128]{4,3,2,1,0:T(8,128)(2,1)S(1)}, bf16[4,3,2,88,128]{4,3,2,1,0:T(8,128)(2,1)S(1)}, u32[]{:S(2)}, u32[]{:S(2)}) collective-permute-start(bf16[4,3,2,88,128]{4,3,2,1,0:T(8,128)(2,1)S(1)} %get-tuple-element.45), channel_id=1, source_target_pairs={{0,24},{4,28},{8,0},{12,4},{16,8},{20,12},{24,16},{28,20},{32,56},... | collective-permute-start | bytes 1622024 | tf_op jit(solution)/shard_map/ppermute | solution.py:324
  98.0 24.5 %copy-start.9 = (f32[3,1,86,512]{3,1,2,0:T(1,128)S(1)}, f32[3,1,86,512]{3,1,2,0:T(1,128)}, u32[]{:S(2)}) copy-start(f32[3,1,86,512]{3,1,2,0:T(1,128)} %param.13) | copy-start | bytes 1585156
  98.0 24.5 %copy-start.10 = (f32[3,1,86,512]{3,1,2,0:T(1,128)S(1)}, f32[3,1,86,512]{3,1,2,0:T(1,128)}, u32[]{:S(2)}) copy-start(f32[3,1,86,512]{3,1,2,0:T(1,128)} %param.12) | copy-start | bytes 1585156
  98.1 10.2 %collective-permute-start.12 = (bf16[3,2,88,128]{3,2,1,0:T(8,128)(2,1)S(1)}, bf16[3,2,88,128]{3,2,1,0:T(8,128)(2,1)S(1)}, u32[]{:S(2)}, u32[]{:S(2)}) collective-permute-start(bf16[3,2,88,128]{3,2,1,0:T(8,128)(2,1)S(1)} %get-tuple-element.55), channel_id=1, source_target_pairs={{0,8},{4,12},{8,16},{12,20},{16,24},{20,28},{24,0},{28,4},{32,40},... | collective-permute-start | bytes 405512 | tf_op jit(solution)/shard_map/ppermute | solution.py:329
  99.6 9.6 %collective-permute-start.13 = (bf16[3,2,88,128]{3,2,1,0:T(8,128)(2,1)S(1)}, bf16[3,2,88,128]{3,2,1,0:T(8,128)(2,1)S(1)}, u32[]{:S(2)}, u32[]{:S(2)}) collective-permute-start(bf16[3,2,88,128]{3,2,1,0:T(8,128)(2,1)S(1)} %get-tuple-element.56), channel_id=1, source_target_pairs={{0,16},{4,20},{8,24},{12,28},{16,0},{20,4},{24,8},{28,12},{32,48},... | collective-permute-start | bytes 405512 | tf_op jit(solution)/shard_map/ppermute | solution.py:329
  102.3 6.9 %collective-permute-start.14 = (bf16[3,2,88,128]{3,2,1,0:T(8,128)(2,1)S(1)}, bf16[3,2,88,128]{3,2,1,0:T(8,128)(2,1)S(1)}, u32[]{:S(2)}, u32[]{:S(2)}) collective-permute-start(bf16[3,2,88,128]{3,2,1,0:T(8,128)(2,1)S(1)} %get-tuple-element.57), channel_id=1, source_target_pairs={{0,24},{4,28},{8,0},{12,4},{16,8},{20,12},{24,16},{28,20},{32,56},... | collective-permute-start | bytes 405512 | tf_op jit(solution)/shard_map/ppermute | solution.py:329
  104.1 7.7 %collective-permute-start.6 = (bf16[3,2,88,128]{3,2,1,0:T(8,128)(2,1)S(1)}, bf16[3,2,88,128]{3,2,1,0:T(8,128)(2,1)S(1)}, u32[]{:S(2)}, u32[]{:S(2)}) collective-permute-start(bf16[3,2,88,128]{3,2,1,0:T(8,128)(2,1)S(1)} %get-tuple-element.47), channel_id=1, source_target_pairs={{0,32},{4,36},{8,40},{12,44},{16,48},{20,52},{24,56},{28,60},{32,6... | collective-permute-start | bytes 405512 | tf_op jit(solution)/shard_map/ppermute | solution.py:328
  105.1 8.6 %collective-permute-start.7 = (bf16[3,2,88,128]{3,2,1,0:T(8,128)(2,1)S(1)}, bf16[3,2,88,128]{3,2,1,0:T(8,128)(2,1)S(1)}, u32[]{:S(2)}, u32[]{:S(2)}) collective-permute-start(bf16[3,2,88,128]{3,2,1,0:T(8,128)(2,1)S(1)} %get-tuple-element.48), channel_id=1, source_target_pairs={{0,64},{4,68},{8,72},{12,76},{16,80},{20,84},{24,88},{28,92},{32,9... | collective-permute-start | bytes 405512 | tf_op jit(solution)/shard_map/ppermute | solution.py:328
  108.2 5.5 %collective-permute-start.8 = (bf16[3,2,88,128]{3,2,1,0:T(8,128)(2,1)S(1)}, bf16[3,2,88,128]{3,2,1,0:T(8,128)(2,1)S(1)}, u32[]{:S(2)}, u32[]{:S(2)}) collective-permute-start(bf16[3,2,88,128]{3,2,1,0:T(8,128)(2,1)S(1)} %get-tuple-element.49), channel_id=1, source_target_pairs={{0,96},{4,100},{8,104},{12,108},{16,112},{20,116},{24,120},{28,124... | collective-permute-start | bytes 405512 | tf_op jit(solution)/shard_map/ppermute | solution.py:328
  114.6 17.2 %collective-permute-start.15 = (bf16[3,88,256]{2,1,0:T(8,128)(2,1)S(1)}, bf16[3,88,256]{2,1,0:T(8,128)(2,1)S(1)}, u32[]{:S(2)}, u32[]{:S(2)}) collective-permute-start(bf16[3,88,256]{2,1,0:T(8,128)(2,1)S(1)} %get-tuple-element.60), channel_id=1, source_target_pairs={{0,4},{4,0},{8,12},{12,8},{16,20},{20,16},{24,28},{28,24},{32,36},... | collective-permute-start | bytes 405512 | tf_op jit(solution)/shard_map/ppermute | solution.py:331
  114.6 17.2 %all-to-all-start = ((f32[128,1,128]{2,1,0:T(1,128)}), f32[128,1,128]{2,1,0:T(1,128)S(1)}, u32[]{:S(2)}, u32[]{:S(2)}) async-start(f32[128,1,128]{2,1,0:T(1,128)} %bitcast.11), calls=%async_computation | async-start | bytes 131072 | tf_op jit(solution)/shard_map/all_to_all | solution.py:332
  133.1 4.6 %copy-start = (bf16[3,4096,512]{2,1,0:T(8,128)(2,1)S(1)}, bf16[3,4096,512]{2,1,0:T(8,128)(2,1)}, u32[]{:S(2)}) copy-start(bf16[3,4096,512]{2,1,0:T(8,128)(2,1)} %bases.1) | copy-start | bytes 37748740
  144.2 34.8 %all-to-all-start.1 = ((bf16[32,3,88,128]{3,2,1,0:T(8,128)(2,1)}), bf16[32,3,88,128]{3,2,1,0:T(8,128)(2,1)S(1)}, u32[]{:S(2)}, u32[]{:S(2)}) async-start(bf16[32,3,88,128]{3,2,1,0:T(8,128)(2,1)} %updates.1), calls=%async_computation.1 | async-start | bytes 4325376 | tf_op jit(solution)/shard_map/all_to_all | solution.py:338
  180.5 0.9 copy-start.8

commit v2 on v1

--- a/solution.py
+++ b/solution.py
@@ -45,116 +45,151 @@
     return pltpu.CompilerParams(vmem_limit_bytes=mib * MB, **more)
 
 
-def project_kernel(place, a_ref, b_ref, g_ref, keep_ref, send_ref, acc, terms):
+def project_kernel(b_steps, a_ref, b_ref, g_ref, send_ref, kept_ref, acc, other, terms):
     k = pl.program_id(0)
-    part = jnp.dot(a_ref[...], b_ref[0], preferred_element_type=F32)
-
-    @pl.when(k == 0)
+    count = b_ref.shape[0]
+    half = kept_ref.shape[2]
+
+    @pl.when(k < b_steps)
     def _():
-        acc[...] = part
-
-    @pl.when(k > 0)
+        for m in range(count):
+            part = jnp.dot(a_ref[...], b_ref[m], preferred_element_type=F32)
+
+            @pl.when(k == 0)
+            def _(m=m, part=part):
+                acc[m] = part
+
+            @pl.when(k > 0)
+            def _(m=m, part=part):
+                acc[m] += part
+
+    @pl.when(k == b_steps)
     def _():
-        acc[...] += part
-
-    @pl.when(k == pl.num_programs(0) - 1)
+        terms[...] = jnp.zeros(terms.shape, F32)
+        core = lax.rem(lax.axis_index("dp"), 2)
+        for m in range(count):
+            low, high = acc[m, :, :half].astype(BF16), acc[m, :, half:].astype(BF16)
+            kept_ref[m] = jnp.where(core == 0, low, high)
+            other[m] = jnp.where(core == 0, high, low)
+
+    @pl.when(k >= b_steps)
     def _():
-        z0, x0, c0 = place[0], place[1], place[2]
-        half = 2 * LANES
-        mine = acc[:, pl.ds(pl.multiple_of(c0 * half, half), half)].astype(BF16)
-        other = acc[:, pl.ds(pl.multiple_of((1 - c0) * half, half), half)].astype(BF16)
-        reduced = jnp.concatenate([mine, other], axis=1)
-        units = g_ref.shape[-1]
-
-        def rows(at, count):
-            g = g_ref[0, :, pl.ds(at, count)]
-            terms[pl.ds(at, count), :] = lax.dot_general(
-                g, reduced, (((0,), (0,)), ((), ())), preferred_element_type=F32
-            )
-
-        block = 256
-        whole = units // block
-
-        @pl.loop(0, whole)
-        def _(j):
-            rows(pl.multiple_of(j * block, block), block)
-
-        if units % block:
-            rows(whole * block, units % block)
-        terms[units:, :] = jnp.zeros((terms.shape[0] - units, terms.shape[1]), F32)
-
-        for z in range(N_Z):
-            for x in range(N_X):
-                sz = lax.rem(z - z0 + N_Z, N_Z)
-                sx = lax.rem(x - x0 + N_X, N_X)
-                for c in range(N_C):
-                    own = lax.rem(c + c0, 2)
-                    at = dp_index(z, x, c) * UNITS
-                    chunk = terms[at : at + PAD, :].astype(BF16)
-                    keep_ref[0, sx, sz, own] = chunk[:, 0:128]
-                    keep_ref[1, sz, sx, own] = chunk[:, 128:256]
-                    send_ref[0, sx, sz, 1 - own] = chunk[:, 256:384]
-                    send_ref[1, sz, sx, 1 - own] = chunk[:, 384:512]
-
-
-def project(place, a, bases, matrix, g, g_at):
+        block = g_ref.shape[1]
+        for m in range(count):
+            terms[m, :block] = jnp.dot(g_ref[m], other[m], preferred_element_type=F32)
+            for d in range(block // UNITS):
+                send_ref[m, 0, d] = terms[m, d * UNITS : d * UNITS + PAD].astype(BF16)
+
+
+def project(a, bases, first, g):
     tokens, width = a.shape
     rank = bases.shape[2]
-    units = g.shape[2]
+    count, units, _ = g.shape
+    half = rank // 2
     steps = 8
     wide = width // steps
-    shape = (2, 4, 4, N_C, PAD, LANES)
-    whole = pl.BlockSpec(shape, lambda k, s: (0,) * 6)
-    return pl.pallas_call(
-        project_kernel,
-        grid_spec=pltpu.PrefetchScalarGridSpec(
-            num_scalar_prefetch=1,
-            grid=(steps,),
-            in_specs=[
-                pl.BlockSpec((tokens, wide), lambda k, s: (0, k)),
-                pl.BlockSpec((1, wide, rank), lambda k, s: (matrix, k, 0)),
-                pl.BlockSpec((1, tokens, units), lambda k, s: (g_at, 0, 0)),
-            ],
-            out_specs=[whole, whole],
-            scratch_shapes=[
-                pltpu.VMEM((tokens, rank), F32),
-                pltpu.VMEM((N_DP * UNITS + 8, rank), F32),
-            ],
-        ),
-        out_shape=[jax.ShapeDtypeStruct(shape, BF16)] * 2,
-        compiler_params=params(40),
+    block = units // N_Z
+    chunks = block // UNITS
+    last = lambda k: jnp.minimum(k, steps - 1)
+    after = lambda k: jnp.maximum(k - steps, 0)
+    return pl.pallas_call(
+        functools.partial(project_kernel, steps),
+        grid=(steps + N_Z,),
+        in_specs=[
+            pl.BlockSpec((tokens, wide), lambda k: (0, last(k))),
+            pl.BlockSpec((count, wide, rank), lambda k: (first // count, last(k), 0)),
+            pl.BlockSpec((count, block, tokens), lambda k: (0, after(k), 0)),
+        ],
+        out_specs=[
+            pl.BlockSpec((count, 1, chunks, PAD, half), lambda k: (0, after(k), 0, 0, 0)),
+            pl.BlockSpec((count, tokens, half), lambda k: (0, 0, 0)),
+        ],
+        out_shape=[
+            jax.ShapeDtypeStruct((count, N_Z, chunks, PAD, half), BF16),
+            jax.ShapeDtypeStruct((count, tokens, half), BF16),
+        ],
+        scratch_shapes=[
+            pltpu.VMEM((count, tokens, rank), F32),
+            pltpu.VMEM((count, tokens, half), BF16),
+            pltpu.VMEM((count, block + 8, half), F32),
+        ],
+        compiler_params=params(56),
         cost_estimate=pl.CostEstimate(
-            flops=2 * tokens * rank * (width + units),
-            bytes_accessed=2 * (tokens * width + width * rank + tokens * units + units * rank),
+            flops=2 * count * tokens * rank * (width + units // 2),
+            bytes_accessed=2 * (tokens * width + count * (width * rank + tokens * units + units * half)),
             transcendentals=0,
         ),
         name="project",
-    )(place, a, bases, g)
-
-
-def pair_kernel(*refs):
-    keep, recv, outs = refs[0:3], refs[3:6], refs[6:]
+    )(a, bases, g)
+
+
+def collect_kernel(old, place, g_ref, kept_ref, recv_ref, *refs):
+    by_x, by_z = refs[old : old + 4], refs[old + 4 : old + 8]
+    terms, cut = refs[old + 8 :]
     step = pl.program_id(0)
-    for i, out in enumerate(outs):
-
-        @pl.when(step == i)
-        def _(out=out):
-            for m in range(3):
-                out[:, m] = (keep[m][0].astype(F32) + recv[m][0].astype(F32)).astype(BF16)
-
-
-def pair_sum(keep, recv):
-    flat = [t.reshape(8, 4, N_C, PAD, LANES) for t in (*keep, *recv)]
+    x0, c0 = place[1], place[2]
+    count, block, _ = g_ref.shape
+
+    @pl.when(step == 0)
+    def _():
+        terms[...] = jnp.zeros(terms.shape, F32)
+
+    for m in range(count):
+        terms[m, :block] = jnp.dot(g_ref[m], kept_ref[m], preferred_element_type=F32)
+        for x in range(N_X):
+            sx = lax.rem(x - x0 + N_X, N_X)
+            for c in range(N_C):
+                own = lax.rem(c + c0, 2)
+                d = x * N_C + c
+                both = terms[m, d * UNITS : d * UNITS + PAD] + recv_ref[m, 0, d].astype(F32)
+                both = both.astype(BF16)
+                cut[0, sx, m, own] = both[:, :LANES]
+                cut[1, sx, m, own] = both[:, LANES:]
+    for s in range(N_X):
+        by_x[s][0] = cut[0, s]
+    for s in range(N_Z):
+
+        @pl.when(step == s)
+        def _(s=s):
+            by_z[s][...] = cut[1]
+
+
+def collect(place, g, kept, recv, first, old=()):
+    count, units, tokens = g.shape
+    half = kept.shape[2]
+    block = units // N_Z
+    chunks = block // UNITS
     shape = (4, 3, N_C, PAD, LANES)
-    return pl.pallas_call(
-        pair_kernel,
-        grid=(8,),
-        in_specs=[pl.BlockSpec((1, 4, N_C, PAD, LANES), lambda i: (i, 0, 0, 0, 0))] * 6,
-        out_specs=[pl.BlockSpec(shape, lambda i: (0,) * 5)] * 8,
+    at = first // count
+    ring = lambda i, s: lax.rem(s[0] + i, N_Z)
+    return pl.pallas_call(
+        functools.partial(collect_kernel, len(old)),
+        grid_spec=pltpu.PrefetchScalarGridSpec(
+            num_scalar_prefetch=1,
+            grid=(N_Z,),
+            in_specs=[
+                pl.BlockSpec((count, block, tokens), lambda i, s: (0, ring(i, s), 0)),
+                pl.BlockSpec((count, tokens, half), lambda i, s: (0, 0, 0)),
+                pl.BlockSpec((count, 1, chunks, PAD, half), lambda i, s: (0, ring(i, s), 0, 0, 0)),
+            ]
+            + [pl.BlockSpec(memory_space=pl.ANY)] * len(old),
+            out_specs=[pl.BlockSpec((1, count, N_C, PAD, LANES), lambda i, s: (i, at, 0, 0, 0))] * 4
+            + [pl.BlockSpec((4, count, N_C, PAD, LANES), lambda i, s: (0, at, 0, 0, 0))] * 4,
+            scratch_shapes=[
+                pltpu.VMEM((count, block + 8, half), F32),
+                pltpu.VMEM((2, 4, count, N_C, PAD, LANES), BF16),
+            ],
+        ),
         out_shape=[jax.ShapeDtypeStruct(shape, BF16)] * 8,
+        input_output_aliases={4 + i: i for i in range(len(old))},
         compiler_params=params(32),
-        name="pair_sum",
-    )(*flat)
+        cost_estimate=pl.CostEstimate(
+            flops=2 * count * tokens * units * half,
+            bytes_accessed=2 * count * units * (tokens + 2 * half),
+            transcendentals=0,
+        ),
+        name="collect",
+    )(place, g, kept, recv, *old)
 
 
 def stage_kernel(own, r1, r2, r3, *outs):
@@ -266,7 +301,7 @@
         ],
         out_specs=pl.BlockSpec((wide // LANES, 3, PAD, LANES), lambda i: (i, 0, 0, 0)),
         out_shape=jax.ShapeDtypeStruct(shape, BF16),
-        compiler_params=params(24),
+        compiler_params=params(56),
         name="updates",
     )(way, bases)
 
@@ -275,13 +310,8 @@
     units = N_DP * UNITS
     for m, out in enumerate((gate, up, down)):
         for k in range(N_DP):
-            rows[k * UNITS : k * UNITS + PAD, :] = pieces[k, m].astype(F32)
-        if m == 2:
-            out[...] = rows[:units, :].astype(BF16)
-            continue
-        for at in range(0, units, LANES):
-            count = min(LANES, units - at)
-            out[:, at : at + count] = rows[at : at + count, :].T.astype(BF16)
+            rows[m, k * UNITS : k * UNITS + PAD, :] = pieces[k, m].astype(F32)
+        out[...] = rows[m, :units, :].astype(BF16)
 
 
 def layout(pieces):
@@ -290,12 +320,8 @@
         layout_kernel,
         in_specs=[VMEM],
         out_specs=[VMEM] * 3,
-        out_shape=[
-            jax.ShapeDtypeStruct((LANES, units), BF16),
-            jax.ShapeDtypeStruct((LANES, units), BF16),
-            jax.ShapeDtypeStruct((units, LANES), BF16),
-        ],
-        scratch_shapes=[pltpu.VMEM((units + 8, LANES), F32)],
+        out_shape=[jax.ShapeDtypeStruct((units, LANES), BF16)] * 3,
+        scratch_shapes=[pltpu.VMEM((3, units + 8, LANES), F32)],
         compiler_params=params(24),
         name="layout",
     )(pieces)
@@ -307,19 +333,14 @@
     me = lax.axis_index("dp")
     place = jnp.stack([me // (N_X * N_C), (me // N_C) % N_X, me % N_C]).astype(jnp.int32)
 
-    keep, recv = [], []
-    for m, (a, g, at) in enumerate(
-        (
-            (activations, gate_up_grads, 0),
-            (activations, gate_up_grads, 1),
-            (down_out_grad, hidden_act[None], 0),
-        )
-    ):
-        kept, sent = project(place, a, bases, m, g, at)
-        keep.append(kept)
-        recv.append(lax.ppermute(sent, "dp", CORE_PAIRS))
-
-    cut = pair_sum(keep, recv)
+    gate_up = jnp.swapaxes(gate_up_grads, 1, 2)
+    hidden = hidden_act.T[None]
+    sent_two, kept_two = project(activations, bases, 0, gate_up)
+    recv_two = lax.ppermute(sent_two, "dp", CORE_PAIRS)
+    sent_one, kept_one = project(down_out_grad, bases, 2, hidden)
+    recv_one = lax.ppermute(sent_one, "dp", CORE_PAIRS)
+    cut = collect(place, gate_up, kept_two, recv_two, 0)
+    cut = collect(place, hidden, kept_one, recv_one, 2, cut)
     by_x, by_z = cut[:4], cut[4:]
     by_x = [by_x[0]] + [lax.ppermute(by_x[s], "dp", along_x(s)) for s in (1, 2, 3)]
     by_z = [by_z[0]] + [lax.ppermute(by_z[s], "dp", along_z(s)) for s in (1, 2, 3)]
@@ -337,7 +358,7 @@
     )
     pieces = lax.all_to_all(updates(way, bases), "dp", 0, 0, tiled=True)
     gate_update, up_update, down_update = layout(pieces)
-    return (gate_update, up_update, down_update, new_first[:, None], new_second[:, None])
+    return (gate_update.T, up_update.T, down_update, new_first[:, None], new_second[:, None])
 
 
 def solution(mesh):

time: 186 us -> 166 us (0.89)
  local copies, waits for them, and re-layouts: 32.2 us -> 6.1 us
  waiting for transfers between devices: 60.8 us -> 68.5 us
  Pallas kernels: 54.2 us -> 51.9 us
    unnamed x29 -> x17, local copies, waits for them, and re-layouts: 32.2 us -> 6.1 us
    ppermute x3, waiting for transfers between devices: 0.01 us -> 8.48 us  [body(): lax.ppermute(by_x[s], 'dp', along_x(s))]
    pallas_call x4, Pallas kernels: 43.6 us -> 37.7 us  [the longest x2 29 us: project(): pl.pallas_call(functools.partial(project_kernel, steps), grid=(steps + N_...]
    pallas_call x1, Pallas kernels: 6.47 us -> 10.1 us  [updates(): pl.pallas_call(update_kernel, grid=(width // wide,), in_specs=[pl.BlockSp...]
    ppermute x3 -> x2, waiting for transfers between devices: 3.19 us -> 0.01 us  [the longest x1 0.01 us: body(): recv_two = lax.ppermute(sent_two, 'dp', CORE_PAIRS)]
    ppermute x3, waiting for transfers between devices: 15.9 us -> 17.9 us  [body(): lax.ppermute(by_z[s], 'dp', along_z(s))]
  transfers between devices with their start and end apart: 18 -> 17, of which waited for: 7 -> 8; matrix products, arithmetic and copies ran while one was open for 3% -> 2% of each run, Pallas kernels for 14% -> 11%
where the time goes in v2:
time: 166 us; the launch traced here: 165 us
  waiting for transfers between devices  68.5 us (41%)
  Pallas kernels  51.9 us (31%)
  starting transfers between devices  38 us (23%)
  local copies, waits for them, and re-layouts  6.1 us (4%)
    pallas_call x2, Pallas kernels, project(): pl.pallas_call(functools.partial(project_kernel, steps), grid=(steps + N_...  29 us
    all_to_all x1, waiting for transfers between devices, body(): pieces = lax.all_to_all(updates(way, bases), 'dp', 0, 0, tiled=True)  28.1 us
    ppermute x3, waiting for transfers between devices, body(): lax.ppermute(by_z[s], 'dp', along_z(s))  17.9 us
    pallas_call x1, Pallas kernels, updates(): pl.pallas_call(update_kernel, grid=(width // wide,), in_specs=[pl.BlockSp...  10.1 us
    all_to_all x1, starting transfers between devices, body(): squares = lax.all_to_all(squares, ('dp', 'tensor'), 0, 0, tiled=True)  9.34 us
    all_to_all x1, waiting for transfers between devices, body(): squares = lax.all_to_all(squares, ('dp', 'tensor'), 0, 0, tiled=True)  9.11 us
    pallas_call x2, Pallas kernels, collect(): pl.pallas_call(functools.partial(collect_kernel, len(old)), grid_spec=plt...  8.73 us
    ppermute x3, waiting for transfers between devices, body(): lax.ppermute(by_x[s], 'dp', along_x(s))  8.48 us
  transfers between devices with their start and end apart: 17, of which 8 were waited for; matrix products, arithmetic and copies ran while one was open for 2% of the time, Pallas kernels for 11%

profile of v2, /device:TPU:0, one launch (start us, length us, event | category | flops | bytes accessed | tf_op | source)
XLA Modules:
  0.0 165.4 jit_solution(9079552617875289634)
XLA Ops:
  0.6 16.9 %project.3 = (bf16[2,4,8,88,256]{4,3,2,1,0:T(8,128)(2,1)}, bf16[2,512,256]{2,1,0:T(8,128)(2,1)}) custom-call(bf16[512,4096]{1,0:T(8,128)(2,1)} %a_ref.3, bf16[3,4096,512]{2,1,0:T(8,128)(2,1)} %bases.1, bf16[2,2752,512]{2,1,0:T(8,128)(2,1)} %bitcast.19), custom_call_target="tpu_custom_call" | custom-call | flops 5737807872 | bytes 21037056 | tf_op jit(solution)/shard_map/project/pallas_call | solution.py:95
  17.5 12.1 %project.2 = (bf16[1,4,8,88,256]{4,3,2,1,0:T(8,128)(2,1)}, bf16[1,512,256]{2,1,0:T(8,128)(2,1)}) custom-call(bf16[512,4096]{1,0:T(8,128)(2,1)} %a_ref.2, bf16[3,4096,512]{2,1,0:T(8,128)(2,1)} %bases.1, bf16[1,2752,512]{2,1,0:T(8,128)(2,1)} %bitcast.21), custom_call_target="tpu_custom_call" | custom-call | flops 2868903936 | bytes 12615680 | tf_op jit(solution)/shard_map/project/pallas_call | solution.py:95
  29.6 0.5 collective-permute-start
  30.2 2.6 %copy-done = bf16[2,512,2752]{1,2,0:T(8,128)(2,1)S(1)} copy-done((bf16[2,512,2752]{1,2,0:T(8,128)(2,1)S(1)}, bf16[2,512,2752]{1,2,0:T(8,128)(2,1)}, u32[]{:S(2)}) %copy-start) | copy-done | bytes 5636120
  32.8 4.8 %collect.2 = (bf16[4,3,2,88,128]{4,3,2,1,0:T(8,128)(2,1)S(1)}, bf16[4,3,2,88,128]{4,3,2,1,0:T(8,128)(2,1)S(1)}, bf16[4,3,2,88,128]{4,3,2,1,0:T(8,128)(2,1)S(1)},...) custom-call(s32[3]{0:T(128)S(1)} %pad_add_fusion.place, ...), custom_call_target="tpu_custom_call" | custom-call | flops 1442840576 | bytes 11272192 | tf_op jit(solution)/shard_map/collect/pallas_call | solution.py:165
  37.6 3.9 %collect.3 = (bf16[4,3,2,88,128]{4,3,2,1,0:T(8,128)(2,1)S(1)}, bf16[4,3,2,88,128]{4,3,2,1,0:T(8,128)(2,1)S(1)}, bf16[4,3,2,88,128]{4,3,2,1,0:T(8,128)(2,1)S(1)},...) custom-call(s32[3]{0:T(128)S(1)} %pad_add_fusion.place, ...), custom_call_target="tpu_custom_call", output_to_operand_aliasing={{0}: (4, {}), {1}: (5, {}), {2}: (6, {}), {3}: (7, {}), {4}... | custom-call | flops 721420288 | bytes 5636096 | tf_op jit(solution)/shard_map/collect/pallas_call | solution.py:165
  41.6 4.2 %collective-permute-start.10 = (bf16[4,3,2,88,128]{4,3,2,1,0:T(8,128)(2,1)S(1)}, bf16[4,3,2,88,128]{4,3,2,1,0:T(8,128)(2,1)S(1)}, u32[]{:S(2)}, u32[]{:S(2)}) collective-permute-start(bf16[4,3,2,88,128]{4,3,2,1,0:T(8,128)(2,1)S(1)} %get-tuple-element.65), channel_id=1, source_target_pairs={{0,96},{4,100},{8,104},{12,108},{16,112},{20,116},{24,120},{28,124... | collective-permute-start | bytes 1622024 | tf_op jit(solution)/shard_map/ppermute | solution.py:346
  45.8 1.9 %collective-permute-start.9 = (bf16[4,3,2,88,128]{4,3,2,1,0:T(8,128)(2,1)S(1)}, bf16[4,3,2,88,128]{4,3,2,1,0:T(8,128)(2,1)S(1)}, u32[]{:S(2)}, u32[]{:S(2)}) collective-permute-start(bf16[4,3,2,88,128]{4,3,2,1,0:T(8,128)(2,1)S(1)} %get-tuple-element.64), channel_id=1, source_target_pairs={{0,64},{4,68},{8,72},{12,76},{16,80},{20,84},{24,88},{28,92},{32,9... | collective-permute-start | bytes 1622024 | tf_op jit(solution)/shard_map/ppermute | solution.py:346
  47.6 1.5 collective-permute-start.2
  49.1 2.7 %collective-permute-start.3 = (bf16[4,3,2,88,128]{4,3,2,1,0:T(8,128)(2,1)S(1)}, bf16[4,3,2,88,128]{4,3,2,1,0:T(8,128)(2,1)S(1)}, u32[]{:S(2)}, u32[]{:S(2)}) collective-permute-start(bf16[4,3,2,88,128]{4,3,2,1,0:T(8,128)(2,1)S(1)} %get-tuple-element.56), channel_id=1, source_target_pairs={{0,16},{4,20},{8,24},{12,28},{16,0},{20,4},{24,8},{28,12},{32,48},... | collective-permute-start | bytes 1622024 | tf_op jit(solution)/shard_map/ppermute | solution.py:345
  51.9 17.2 %collective-permute-done.10.r3 = bf16[4,3,2,88,128]{4,3,2,1,0:T(8,128)(2,1)S(1)} collective-permute-done((bf16[4,3,2,88,128]{4,3,2,1,0:T(8,128)(2,1)S(1)}, bf16[4,3,2,88,128]{4,3,2,1,0:T(8,128)(2,1)S(1)}, u32[]{:S(2)}, u32[]{:S(2)}) %collective-permute-start.10) | collective-permute-done | bytes 540704 | tf_op jit(solution)/shard_map/ppermute | solution.py:346
  69.1 2.8 %collective-permute-start.4 = (bf16[4,3,2,88,128]{4,3,2,1,0:T(8,128)(2,1)S(1)}, bf16[4,3,2,88,128]{4,3,2,1,0:T(8,128)(2,1)S(1)}, u32[]{:S(2)}, u32[]{:S(2)}) collective-permute-start(bf16[4,3,2,88,128]{4,3,2,1,0:T(8,128)(2,1)S(1)} %get-tuple-element.57), channel_id=1, source_target_pairs={{0,24},{4,28},{8,0},{12,4},{16,8},{20,12},{24,16},{28,20},{32,56},... | collective-permute-start | bytes 1622024 | tf_op jit(solution)/shard_map/ppermute | solution.py:345
  71.8 0.6 collective-permute-done.8.r1
  72.8 1.6 collective-permute-start.11
  74.3 2.7 %collective-permute-start.12 = (bf16[3,2,88,128]{3,2,1,0:T(8,128)(2,1)S(1)}, bf16[3,2,88,128]{3,2,1,0:T(8,128)(2,1)S(1)}, u32[]{:S(2)}, u32[]{:S(2)}) collective-permute-start(bf16[3,2,88,128]{3,2,1,0:T(8,128)(2,1)S(1)} %get-tuple-element.68), channel_id=1, source_target_pairs={{0,16},{4,20},{8,24},{12,28},{16,0},{20,4},{24,8},{28,12},{32,48},... | collective-permute-start | bytes 405512 | tf_op jit(solution)/shard_map/ppermute | solution.py:350
  77.1 1.4 collective-permute-start.13
  78.5 8.5 %collective-permute-done.4.r3 = bf16[4,3,2,88,128]{4,3,2,1,0:T(8,128)(2,1)S(1)} collective-permute-done((bf16[4,3,2,88,128]{4,3,2,1,0:T(8,128)(2,1)S(1)}, bf16[4,3,2,88,128]{4,3,2,1,0:T(8,128)(2,1)S(1)}, u32[]{:S(2)}, u32[]{:S(2)}) %collective-permute-start.4) | collective-permute-done | bytes 540704 | tf_op jit(solution)/shard_map/ppermute | solution.py:345
  87.3 5.3 %collective-permute-start.6 = (bf16[3,2,88,128]{3,2,1,0:T(8,128)(2,1)S(1)}, bf16[3,2,88,128]{3,2,1,0:T(8,128)(2,1)S(1)}, u32[]{:S(2)}, u32[]{:S(2)}) collective-permute-start(bf16[3,2,88,128]{3,2,1,0:T(8,128)(2,1)S(1)} %get-tuple-element.60), channel_id=1, source_target_pairs={{0,64},{4,68},{8,72},{12,76},{16,80},{20,84},{24,88},{28,92},{32,9... | collective-permute-start | bytes 405512 | tf_op jit(solution)/shard_map/ppermute | solution.py:349
  92.6 1.5 collective-permute-done.5.refs_1_
  94.1 2.9 %collective-permute-done.6.refs_2_ = bf16[3,2,88,128]{3,2,1,0:T(8,128)(2,1)S(1)} collective-permute-done((bf16[3,2,88,128]{3,2,1,0:T(8,128)(2,1)S(1)}, bf16[3,2,88,128]{3,2,1,0:T(8,128)(2,1)S(1)}, u32[]{:S(2)}, u32[]{:S(2)}) %collective-permute-start.6) | collective-permute-done | bytes 135200 | tf_op jit(solution)/shard_map/ppermute | solution.py:349
  97.0 0.6 collective-permute-done.7.refs_3_
  97.6 0.8 owned_sum.1
  98.4 9.3 %all-to-all-start = ((f32[128,1,128]{2,1,0:T(1,128)}), f32[128,1,128]{2,1,0:T(1,128)S(1)}, u32[]{:S(2)}, u32[]{:S(2)}) async-start(f32[128,1,128]{2,1,0:T(1,128)} %bitcast.8), calls=%async_computation | async-start | bytes 131072 | tf_op jit(solution)/shard_map/all_to_all | solution.py:353
  107.9 9.1 %all-to-all-done = f32[128,1,128]{2,1,0:T(1,128)S(1)} async-done(((f32[128,1,128]{2,1,0:T(1,128)}), f32[128,1,128]{2,1,0:T(1,128)S(1)}, u32[]{:S(2)}, u32[]{:S(2)}) %all-to-all-start) | async-done | bytes 65568 | tf_op jit(solution)/shard_map/all_to_all | solution.py:353
  117.0 1.3 adam.1
  118.4 0.7 copy-done.3
  119.1 10.1 %updates.1 = bf16[32,3,88,128]{3,2,1,0:T(8,128)(2,1)} custom-call(bf16[3,88,512]{2,1,0:T(8,128)(2,1)} %copy-done.3, bf16[3,4096,512]{2,1,0:T(8,128)(2,1)} %bases.1), custom_call_target="tpu_custom_call" | custom-call | tf_op jit(solution)/shard_map/updates/pallas_call | solution.py:295
  129.2 4.1 %all-to-all-start.1 = ((bf16[32,3,88,128]{3,2,1,0:T(8,128)(2,1)}), bf16[32,3,88,128]{3,2,1,0:T(8,128)(2,1)S(1)}, u32[]{:S(2)}, u32[]{:S(2)}) async-start(bf16[32,3,88,128]{3,2,1,0:T(8,128)(2,1)} %updates.1), calls=%async_computation.1 | async-start | bytes 4325376 | tf_op jit(solution)/shard_map/all_to_all | solution.py:359
  133.2 1.3 copy.23
  134.6 1.3 copy.24
  135.9 28.1 %all-to-all-done.1.pieces = bf16[32,3,88,128]{3,2,1,0:T(8,128)(2,1)S(1)} async-done(((bf16[32,3,88,128]{3,2,1,0:T(8,128)(2,1)}), bf16[32,3,88,128]{3,2,1,0:T(8,128)(2,1)S(1)}, u32[]{:S(2)}, u32[]{:S(2)}) %all-to-all-start.1) | async-done | bytes 2162720 | tf_op jit(solution)/shard_map/all_to_all | solution.py:359
  164.0 1.5 layout.1
  (30 shorter events, 0.8 us)
Async XLA Ops:
  17.5 12.7 %collective-permute-start.1 = (bf16[2,4,8,88,256]{4,3,2,1,0:T(8,128)(2,1)}, bf16[2,4,8,88,256]{4,3,2,1,0:T(8,128)(2,1)S(1)}, u32[]{:S(2)}, u32[]{:S(2)}) collective-permute-start(bf16[2,4,8,88,256]{4,3,2,1,0:T(8,128)(2,1)} %get-tuple-element.45), channel_id=1, source_target_pairs={{0,4},{4,0},{8,12},{12,8},{16,20},{20,16},{24,28},{28,24},{32,36},... | collective-permute-start | bytes 8650760 | tf_op jit(solution)/shard_map/ppermute | solution.py:339
  17.5 12.7 %copy-start.2 = (bf16[2,512,256]{2,1,0:T(8,128)(2,1)S(1)}, bf16[2,512,256]{2,1,0:T(8,128)(2,1)}, u32[]{:S(2)}) copy-start(bf16[2,512,256]{2,1,0:T(8,128)(2,1)} %get-tuple-element.44.kept_ref) | copy-start | bytes 1572868
  29.6 8.0 %collective-permute-start = (bf16[1,4,8,88,256]{4,3,2,1,0:T(8,128)(2,1)}, bf16[1,4,8,88,256]{4,3,2,1,0:T(8,128)(2,1)}, u32[]{:S(2)}, u32[]{:S(2)}) collective-permute-start(bf16[1,4,8,88,256]{4,3,2,1,0:T(8,128)(2,1)} %get-tuple-element.43), channel_id=1, source_target_pairs={{0,4},{4,0},{8,12},{12,8},{16,20},{20,16},{24,28},{28,24},{32,36},... | collective-permute-start | bytes 4325384 | tf_op jit(solution)/shard_map/ppermute | solution.py:341
  30.2 2.6 %copy-start = (bf16[2,512,2752]{1,2,0:T(8,128)(2,1)S(1)}, bf16[2,512,2752]{1,2,0:T(8,128)(2,1)}, u32[]{:S(2)}) copy-start(bf16[2,512,2752]{1,2,0:T(8,128)(2,1)} %param.8) | copy-start | bytes 16908292
  32.8 4.8 %copy-start.1 = (bf16[512,2752]{0,1:T(8,128)(2,1)S(1)}, bf16[512,2752]{0,1:T(8,128)(2,1)}, u32[]{:S(2)}) copy-start(bf16[512,2752]{0,1:T(8,128)(2,1)} %param.9) | copy-start | bytes 8454148
  32.8 4.8 %copy-start.4 = (bf16[1,512,256]{2,1,0:T(8,128)(2,1)S(1)}, bf16[1,512,256]{2,1,0:T(8,128)(2,1)}, u32[]{:S(2)}) copy-start(bf16[1,512,256]{2,1,0:T(8,128)(2,1)} %get-tuple-element.42.kept_ref) | copy-start | bytes 786436
  41.5 66.2 %copy-start.5 = (f32[3,1,86,512]{3,1,2,0:T(1,128)S(1)}, f32[3,1,86,512]{3,1,2,0:T(1,128)}, u32[]{:S(2)}) copy-start(f32[3,1,86,512]{3,1,2,0:T(1,128)} %param.13) | copy-start | bytes 1585156
  41.6 66.2 %copy-start.6 = (f32[3,1,86,512]{3,1,2,0:T(1,128)S(1)}, f32[3,1,86,512]{3,1,2,0:T(1,128)}, u32[]{:S(2)}) copy-start(f32[3,1,86,512]{3,1,2,0:T(1,128)} %param.12) | copy-start | bytes 1585156
  41.6 27.5 %collective-permute-start.10 = (bf16[4,3,2,88,128]{4,3,2,1,0:T(8,128)(2,1)S(1)}, bf16[4,3,2,88,128]{4,3,2,1,0:T(8,128)(2,1)S(1)}, u32[]{:S(2)}, u32[]{:S(2)}) collective-permute-start(bf16[4,3,2,88,128]{4,3,2,1,0:T(8,128)(2,1)S(1)} %get-tuple-element.65), channel_id=1, source_target_pairs={{0,96},{4,100},{8,104},{12,108},{16,112},{20,116},{24,120},{28,124... | collective-permute-start | bytes 1622024 | tf_op jit(solution)/shard_map/ppermute | solution.py:346
  45.8 26.7 %collective-permute-start.8 = (bf16[4,3,2,88,128]{4,3,2,1,0:T(8,128)(2,1)S(1)}, bf16[4,3,2,88,128]{4,3,2,1,0:T(8,128)(2,1)S(1)}, u32[]{:S(2)}, u32[]{:S(2)}) collective-permute-start(bf16[4,3,2,88,128]{4,3,2,1,0:T(8,128)(2,1)S(1)} %get-tuple-element.63), channel_id=1, source_target_pairs={{0,32},{4,36},{8,40},{12,44},{16,48},{20,52},{24,56},{28,60},{32,6... | collective-permute-start | bytes 1622024 | tf_op jit(solution)/shard_map/ppermute | solution.py:346
  45.8 26.7 %collective-permute-start.9 = (bf16[4,3,2,88,128]{4,3,2,1,0:T(8,128)(2,1)S(1)}, bf16[4,3,2,88,128]{4,3,2,1,0:T(8,128)(2,1)S(1)}, u32[]{:S(2)}, u32[]{:S(2)}) collective-permute-start(bf16[4,3,2,88,128]{4,3,2,1,0:T(8,128)(2,1)S(1)} %get-tuple-element.64), channel_id=1, source_target_pairs={{0,64},{4,68},{8,72},{12,76},{16,80},{20,84},{24,88},{28,92},{32,9... | collective-permute-start | bytes 1622024 | tf_op jit(solution)/shard_map/ppermute | solution.py:346
  47.6 29.4 %collective-permute-start.2 = (bf16[4,3,2,88,128]{4,3,2,1,0:T(8,128)(2,1)S(1)}, bf16[4,3,2,88,128]{4,3,2,1,0:T(8,128)(2,1)S(1)}, u32[]{:S(2)}, u32[]{:S(2)}) collective-permute-start(bf16[4,3,2,88,128]{4,3,2,1,0:T(8,128)(2,1)S(1)} %get-tuple-element.55), channel_id=1, source_target_pairs={{0,8},{4,12},{8,16},{12,20},{16,24},{20,28},{24,0},{28,4},{32,40},... | collective-permute-start | bytes 1622024 | tf_op jit(solution)/shard_map/ppermute | solution.py:345
  49.1 29.4 %collective-permute-start.3 = (bf16[4,3,2,88,128]{4,3,2,1,0:T(8,128)(2,1)S(1)}, bf16[4,3,2,88,128]{4,3,2,1,0:T(8,128)(2,1)S(1)}, u32[]{:S(2)}, u32[]{:S(2)}) collective-permute-start(bf16[4,3,2,88,128]{4,3,2,1,0:T(8,128)(2,1)S(1)} %get-tuple-element.56), channel_id=1, source_target_pairs={{0,16},{4,20},{8,24},{12,28},{16,0},{20,4},{24,8},{28,12},{32,48},... | collective-permute-start | bytes 1622024 | tf_op jit(solution)/shard_map/ppermute | solution.py:345
  69.1 17.9 %collective-permute-start.4 = (bf16[4,3,2,88,128]{4,3,2,1,0:T(8,128)(2,1)S(1)}, bf16[4,3,2,88,128]{4,3,2,1,0:T(8,128)(2,1)S(1)}, u32[]{:S(2)}, u32[]{:S(2)}) collective-permute-start(bf16[4,3,2,88,128]{4,3,2,1,0:T(8,128)(2,1)S(1)} %get-tuple-element.57), channel_id=1, source_target_pairs={{0,24},{4,28},{8,0},{12,4},{16,8},{20,12},{24,16},{28,20},{32,56},... | collective-permute-start | bytes 1622024 | tf_op jit(solution)/shard_map/ppermute | solution.py:345
  72.8 19.8 %collective-permute-start.11 = (bf16[3,2,88,128]{3,2,1,0:T(8,128)(2,1)S(1)}, bf16[3,2,88,128]{3,2,1,0:T(8,128)(2,1)S(1)}, u32[]{:S(2)}, u32[]{:S(2)}) collective-permute-start(bf16[3,2,88,128]{3,2,1,0:T(8,128)(2,1)S(1)} %get-tuple-element.67), channel_id=1, source_target_pairs={{0,8},{4,12},{8,16},{12,20},{16,24},{20,28},{24,0},{28,4},{32,40},... | collective-permute-start | bytes 405512 | tf_op jit(solution)/shard_map/ppermute | solution.py:350
  74.3 18.3 %collective-permute-start.12 = (bf16[3,2,88,128]{3,2,1,0:T(8,128)(2,1)S(1)}, bf16[3,2,88,128]{3,2,1,0:T(8,128)(2,1)S(1)}, u32[]{:S(2)}, u32[]{:S(2)}) collective-permute-start(bf16[3,2,88,128]{3,2,1,0:T(8,128)(2,1)S(1)} %get-tuple-element.68), channel_id=1, source_target_pairs={{0,16},{4,20},{8,24},{12,28},{16,0},{20,4},{24,8},{28,12},{32,48},... | collective-permute-start | bytes 405512 | tf_op jit(solution)/shard_map/ppermute | solution.py:350
  77.1 15.6 %collective-permute-start.13 = (bf16[3,2,88,128]{3,2,1,0:T(8,128)(2,1)S(1)}, bf16[3,2,88,128]{3,2,1,0:T(8,128)(2,1)S(1)}, u32[]{:S(2)}, u32[]{:S(2)}) collective-permute-start(bf16[3,2,88,128]{3,2,1,0:T(8,128)(2,1)S(1)} %get-tuple-element.69), channel_id=1, source_target_pairs={{0,24},{4,28},{8,0},{12,4},{16,8},{20,12},{24,16},{28,20},{32,56},... | collective-permute-start | bytes 405512 | tf_op jit(solution)/shard_map/ppermute | solution.py:350
  87.2 6.9 %collective-permute-start.5 = (bf16[3,2,88,128]{3,2,1,0:T(8,128)(2,1)S(1)}, bf16[3,2,88,128]{3,2,1,0:T(8,128)(2,1)S(1)}, u32[]{:S(2)}, u32[]{:S(2)}) collective-permute-start(bf16[3,2,88,128]{3,2,1,0:T(8,128)(2,1)S(1)} %get-tuple-element.59), channel_id=1, source_target_pairs={{0,32},{4,36},{8,40},{12,44},{16,48},{20,52},{24,56},{28,60},{32,6... | collective-permute-start | bytes 405512 | tf_op jit(solution)/shard_map/ppermute | solution.py:349
  87.3 9.7 %collective-permute-start.6 = (bf16[3,2,88,128]{3,2,1,0:T(8,128)(2,1)S(1)}, bf16[3,2,88,128]{3,2,1,0:T(8,128)(2,1)S(1)}, u32[]{:S(2)}, u32[]{:S(2)}) collective-permute-start(bf16[3,2,88,128]{3,2,1,0:T(8,128)(2,1)S(1)} %get-tuple-element.60), channel_id=1, source_target_pairs={{0,64},{4,68},{8,72},{12,76},{16,80},{20,84},{24,88},{28,92},{32,9... | collective-permute-start | bytes 405512 | tf_op jit(solution)/shard_map/ppermute | solution.py:349
  92.6 5.0 %collective-permute-start.7 = (bf16[3,2,88,128]{3,2,1,0:T(8,128)(2,1)S(1)}, bf16[3,2,88,128]{3,2,1,0:T(8,128)(2,1)S(1)}, u32[]{:S(2)}, u32[]{:S(2)}) collective-permute-start(bf16[3,2,88,128]{3,2,1,0:T(8,128)(2,1)S(1)} %get-tuple-element.61), channel_id=1, source_target_pairs={{0,96},{4,100},{8,104},{12,108},{16,112},{20,116},{24,120},{28,124... | collective-permute-start | bytes 405512 | tf_op jit(solution)/shard_map/ppermute | solution.py:349
  98.4 18.6 %collective-permute-start.14 = (bf16[3,88,256]{2,1,0:T(8,128)(2,1)S(1)}, bf16[3,88,256]{2,1,0:T(8,128)(2,1)S(1)}, u32[]{:S(2)}, u32[]{:S(2)}) collective-permute-start(bf16[3,88,256]{2,1,0:T(8,128)(2,1)S(1)} %get-tuple-element.72), channel_id=1, source_target_pairs={{0,4},{4,0},{8,12},{12,8},{16,20},{20,16},{24,28},{28,24},{32,36},... | collective-permute-start | bytes 405512 | tf_op jit(solution)/shard_map/ppermute | solution.py:352
  98.4 18.6 %all-to-all-start = ((f32[128,1,128]{2,1,0:T(1,128)}), f32[128,1,128]{2,1,0:T(1,128)S(1)}, u32[]{:S(2)}, u32[]{:S(2)}) async-start(f32[128,1,128]{2,1,0:T(1,128)} %bitcast.8), calls=%async_computation | async-start | bytes 131072 | tf_op jit(solution)/shard_map/all_to_all | solution.py:353
  118.3 0.7 copy-start.3
  129.2 34.8 %all-to-all-start.1 = ((bf16[32,3,88,128]{3,2,1,0:T(8,128)(2,1)}), bf16[32,3,88,128]{3,2,1,0:T(8,128)(2,1)S(1)}, u32[]{:S(2)}, u32[]{:S(2)}) async-start(bf16[32,3,88,128]{3,2,1,0:T(8,128)(2,1)} %updates.1), calls=%async_computation.1 | async-start | bytes 4325376 | tf_op jit(solution)/shard_map/all_to_all | solution.py:359

commit v3 on v0

v3 whole, which is shorter than its diff:
```python
import functools

import jax
import jax.numpy as jnp
from jax import lax
from jax.experimental import pallas as pl
from jax.experimental.pallas import tpu as pltpu
from jax.sharding import PartitionSpec as P

STEP = 10
N_Z, N_X, N_C = 4, 4, 2
N_DP = N_Z * N_X * N_C
UNITS = 86
PAD = 88
LANES = 128
BF16 = jnp.bfloat16
F32 = jnp.float32
MB = 1 << 20


def dp_index(z, x, c):
    return ((z % N_Z) * N_X + (x % N_X)) * N_C + c % N_C


def every_chip():
    return [(z, x, c) for z in range(N_Z) for x in range(N_X) for c in range(N_C)]


CORE_PAIRS = [(dp_index(z, x, c), dp_index(z, x, c + 1)) for z, x, c in every_chip()]


FLIPS = ((1, 3), (3, 1))
FLIP_ORDER = tuple((0, b, a, a ^ b) for a, b in FLIPS)
RANK_OF = tuple(tuple(order.index(d) for d in range(4)) for order in FLIP_ORDER)


def along_x(turn):
    return [(dp_index(z, x, c), dp_index(z, x ^ FLIPS[c][turn], c)) for z, x, c in every_chip()]


def along_z(turn):
    return [(dp_index(z, x, c), dp_index(z ^ FLIPS[c][turn], x, c)) for z, x, c in every_chip()]


VMEM = pl.BlockSpec(memory_space=pltpu.VMEM)
SMEM = pl.BlockSpec(memory_space=pltpu.SMEM)
ANY = pl.BlockSpec(memory_space=pl.ANY)


def params(mib, **more):
    return pltpu.CompilerParams(vmem_limit_bytes=mib * MB, **more)


def project_kernel(steps, window, place, x_hbm, y_hbm, b_hbm, kept, sent, x, y, b, acc, sem_a, sem_b):
    wide = x.shape[1] // steps
    half = kept.shape[2]
    jobs = [(x_hbm, x, 0, (0, 1), k) for k in range(steps)] + [
        (y_hbm, y, 1, (2,), k) for k in range(steps)
    ]

    def copies(job):
        src, dst, which, matrices, k = job
        at = pl.ds(k * wide, wide)
        yield pltpu.make_async_copy(src.at[:, at], dst.at[:, at], sem_a.at[which, k])
        for m in matrices:
            yield pltpu.make_async_copy(b_hbm.at[m, at], b.at[m, at], sem_b.at[m, k])

    for job in jobs[:window]:
        for copy in copies(job):
            copy.start()
    for i, job in enumerate(jobs):
        for copy in copies(job):
            copy.wait()
        if i + window < len(jobs):
            for copy in copies(jobs[i + window]):
                copy.start()
        _, rows, _, matrices, k = job
        at = slice(k * wide, (k + 1) * wide)
        for m in matrices:
            part = jnp.dot(rows[:, at], b[m, at], preferred_element_type=F32)
            if k == 0:
                acc[m] = part
            elif k < steps - 1:
                acc[m] += part
            else:
                full = (acc[m] + part).astype(BF16)
                low, high = full[:, :half], full[:, half:]
                first = place[8] == 0
                kept[m] = jnp.where(first, low, high)
                sent[m] = jnp.where(first, high, low)


def project(place, x, y, bases):
    tokens, width = x.shape
    rank = bases.shape[2]
    steps = 8
    out = jax.ShapeDtypeStruct((3, tokens, rank // 2), BF16)
    return pl.pallas_call(
        functools.partial(project_kernel, steps, 4),
        in_specs=[SMEM, ANY, ANY, ANY],
        out_specs=[VMEM] * 2,
        out_shape=[out, out],
        scratch_shapes=[
            pltpu.VMEM((tokens, width), BF16),
            pltpu.VMEM((tokens, width), BF16),
            pltpu.VMEM((3, width, rank), BF16),
            pltpu.VMEM((3, tokens, rank), F32),
            pltpu.SemaphoreType.DMA((2, steps)),
            pltpu.SemaphoreType.DMA((3, steps)),
        ],
        compiler_params=params(58),
        cost_estimate=pl.CostEstimate(
            flops=2 * 3 * tokens * rank * width,
            bytes_accessed=2 * (2 * tokens * width + 3 * width * rank),
            transcendentals=0,
        ),
        name="project",
    )(place, x, y, bases)


def collect_kernel(place, g_two, g_one, h_two, h_one, mine, theirs, xa, xb, za, zb, terms, cut):
    step = pl.program_id(0)
    c0 = place[8]
    block = g_two.shape[1]

    @pl.when(step == 0)
    def _():
        terms[...] = jnp.zeros(terms.shape, F32)

    for m in range(3):
        here = g_two[m] if m < 2 else g_one[0]
        there = h_two[m] if m < 2 else h_one[0]
        terms[m, :block] = jnp.dot(here, mine[m], preferred_element_type=F32) + jnp.dot(
            there, theirs[m], preferred_element_type=F32
        )
        for x in range(N_X):
            at = place[4 + x]
            for c in range(N_C):
                own = lax.rem(c + c0, 2)
                d = (x * N_C + c) * UNITS
                both = terms[m, d : d + PAD].astype(BF16)
                cut[0, at, m, own] = both[:, :LANES]
                cut[1, at, m, own] = both[:, LANES:]
    xa[:, 0] = cut[0, :2]
    xb[:, 0] = cut[0, 2:]

    @pl.when(step < 2)
    def _():
        za[0] = cut[1]

    @pl.when(step >= 2)
    def _():
        zb[0] = cut[1]


def collect(place, g_two, g_one, h_two, h_one, mine, theirs):
    _, units, tokens = g_two.shape
    half = mine.shape[2]
    block = units // N_Z
    shape = (2, 4, 3, N_C, PAD, LANES)
    by_z = lambda count: pl.BlockSpec((count, block, tokens), lambda i, s: (0, s[i], 0))
    whole = pl.BlockSpec((3, tokens, half), lambda i, s: (0, 0, 0))
    x_spec = pl.BlockSpec((2, 1, 3, N_C, PAD, LANES), lambda i, s: (0, i, 0, 0, 0, 0))
    z_shape = (1, 4, 3, N_C, PAD, LANES)
    return pl.pallas_call(
        collect_kernel,
        grid_spec=pltpu.PrefetchScalarGridSpec(
            num_scalar_prefetch=1,
            grid=(N_Z,),
            in_specs=[by_z(2), by_z(1), by_z(2), by_z(1), whole, whole],
            out_specs=[
                x_spec,
                x_spec,
                pl.BlockSpec(z_shape, lambda i, s: (jnp.minimum(i, 1), 0, 0, 0, 0, 0)),
                pl.BlockSpec(z_shape, lambda i, s: (jnp.maximum(i - 2, 0), 0, 0, 0, 0, 0)),
            ],
            scratch_shapes=[
                pltpu.VMEM((3, block + 8, half), F32),
                pltpu.VMEM((2, 4, 3, N_C, PAD, LANES), BF16),
            ],
        ),
        out_shape=[jax.ShapeDtypeStruct(shape, BF16)] * 4,
        compiler_params=params(58),
        cost_estimate=pl.CostEstimate(
            flops=2 * 3 * 2 * tokens * units * half,
            bytes_accessed=2 * 3 * units * (2 * tokens + half),
            transcendentals=0,
        ),
        name="collect",
    )(place, g_two, g_one, h_two, h_one, mine, theirs)


def halve_kernel(kept, recv, stay, go):
    n = kept.shape[0] // 2
    for out, at in ((stay, slice(0, n)), (go, slice(n, 2 * n))):
        out[...] = (kept[at].astype(F32) + recv[at].astype(F32)).astype(BF16)


def halve(kept, recv):
    shape = (kept.shape[0] // 2, *kept.shape[1:])
    return pl.pallas_call(
        halve_kernel,
        in_specs=[VMEM] * 2,
        out_specs=[VMEM] * 2,
        out_shape=[jax.ShapeDtypeStruct(shape, BF16)] * 2,
        compiler_params=params(12),
        name="halve",
    )(kept, recv)


def owned_kernel(xa, xb, za, zb, mine, fix, squares):
    inside = lax.broadcasted_iota(jnp.int32, (PAD, LANES), 0) < UNITS
    total_sq = jnp.zeros((PAD, LANES), F32)
    for half, (p, q) in enumerate(((xa, xb), (za, zb))):
        lanes = slice(half * LANES, half * LANES + LANES)
        for m in range(3):
            for c in range(N_C):
                v = p[0, m, c].astype(F32) + q[0, m, c].astype(F32)
                total_sq += jnp.where(inside, v * v, 0.0)
                if c == 0:
                    mine[m, :, lanes] = v
                else:
                    fix[m, :, lanes] = v.astype(BF16)
    row = jnp.sum(total_sq, axis=0, keepdims=True)
    squares[...] = jnp.broadcast_to(row, squares.shape)


def owned_sum(xa, xb, za, zb, peers):
    return pl.pallas_call(
        owned_kernel,
        in_specs=[VMEM] * 4,
        out_specs=[VMEM] * 3,
        out_shape=[
            jax.ShapeDtypeStruct((3, PAD, 2 * LANES), F32),
            jax.ShapeDtypeStruct((3, PAD, 2 * LANES), BF16),
            jax.ShapeDtypeStruct((peers, LANES), F32),
        ],
        compiler_params=params(12),
        name="owned_sum",
    )(xa, xb, za, zb)


def update_kernel(
    limit_sq, window, place, squares, mine, recv, first, second, b_hbm, new_first, new_second, out, b, way, sem
):
    pieces = sem.shape[1]
    wide = b.shape[1] // pieces
    jobs = [(j, m) for j in range(pieces) for m in range(3)]

    def copy(job):
        j, m = job
        at = pl.ds(j * wide, wide)
        return pltpu.make_async_copy(b_hbm.at[m, at], b.at[m, at], sem.at[m, j])

    for job in jobs[:window]:
        copy(job).start()

    total = jnp.sum(squares[...])
    clip_limit = jnp.sqrt(jnp.full((1, 1), limit_sq, F32))
    factor = jnp.minimum(1.0, clip_limit / jnp.sqrt(jnp.full((1, 1), total, F32)))
    low = place[8] == 0
    for m in range(3):
        here = mine[m]
        there = recv[m].astype(F32)
        lower = jnp.where(low, here, there)
        upper = jnp.where(low, there, here)
        clipped = jnp.concatenate([lower, upper], axis=1)[:UNITS] * factor
        one = 0.9 * first[m] + 0.1 * clipped
        two = 0.95 * second[m] + 0.05 * clipped * clipped
        new_first[m] = one
        new_second[m] = two
        turn = one / (1.0 - 0.9**STEP) / (jnp.sqrt(two / (1.0 - 0.95**STEP)) + 1e-08)
        rows = way.shape[1] - UNITS
        padded = jnp.concatenate([turn, jnp.zeros((rows, turn.shape[1]), F32)], axis=0)
        way[m] = padded.astype(BF16)

    for i, (j, m) in enumerate(jobs):
        copy((j, m)).wait()
        if i + window < len(jobs):
            copy(jobs[i + window]).start()
        full = lax.dot_general(
            way[m], b[m, j * wide : (j + 1) * wide], (((1,), (1,)), ((), ())), preferred_element_type=F32
        ).astype(BF16)
        for n in range(wide // LANES):
            out[j * (wide // LANES) + n, m] = full[:, n * LANES : (n + 1) * LANES]


def update(limit_sq, place, squares, mine, recv, first, second, bases):
    _, width, rank = bases.shape
    moment = jax.ShapeDtypeStruct((3, UNITS, rank), F32)
    return pl.pallas_call(
        functools.partial(update_kernel, limit_sq, 8),
        in_specs=[SMEM] + [VMEM] * 5 + [ANY],
        out_specs=[VMEM] * 3,
        out_shape=[
            moment,
            moment,
            jax.ShapeDtypeStruct((width // LANES, 3, PAD, LANES), BF16),
        ],
        scratch_shapes=[
            pltpu.VMEM((3, width, rank), BF16),
            pltpu.VMEM((3, PAD, rank), BF16),
            pltpu.SemaphoreType.DMA((3, 8)),
        ],
        compiler_params=params(48),
        name="update",
    )(place, squares, mine, recv, first, second, bases)


def layout_kernel(pieces, gate, up, down, rows):
    units = N_DP * UNITS
    for m, out in enumerate((gate, up, down)):
        for k in range(N_DP):
            rows[m, k * UNITS : k * UNITS + PAD, :] = pieces[k, m].astype(F32)
        out[...] = rows[m, :units, :].astype(BF16)


def layout(pieces):
    units = N_DP * UNITS
    return pl.pallas_call(
        layout_kernel,
        in_specs=[VMEM],
        out_specs=[VMEM] * 3,
        out_shape=[jax.ShapeDtypeStruct((units, LANES), BF16)] * 3,
        scratch_shapes=[pltpu.VMEM((3, units + 8, LANES), F32)],
        compiler_params=params(24),
        name="layout",
    )(pieces)


def body(activations, gate_up_grads, hidden_act, down_out_grad, bases, first_moment, second_moment):
    devices = lax.axis_size("dp") * lax.axis_size("tensor")
    total_units = hidden_act.shape[1] * lax.axis_size("tensor")
    me = lax.axis_index("dp")
    z, x, c = me // (N_X * N_C), (me // N_C) % N_X, me % N_C
    order = jnp.asarray(FLIP_ORDER, jnp.int32)[c]
    ranks = jnp.asarray(RANK_OF, jnp.int32)[c]
    across = ranks[jnp.bitwise_xor(jnp.arange(N_X, dtype=jnp.int32), x)]
    place = jnp.concatenate([jnp.bitwise_xor(order, z), across, c[None]]).astype(jnp.int32)

    gate_up = jnp.swapaxes(gate_up_grads, 1, 2)
    hidden = hidden_act.T[None]
    gate_up_there = lax.ppermute(gate_up, "dp", CORE_PAIRS)
    hidden_there = lax.ppermute(hidden, "dp", CORE_PAIRS)
    kept, sent = project(place, activations, down_out_grad, bases)
    theirs = lax.ppermute(sent, "dp", CORE_PAIRS)
    xa, xb, za, zb = collect(place, gate_up, hidden, gate_up_there, hidden_there, kept, theirs)

    rounds = [(along_x, along_z, 0), (along_x, along_z, 1), (along_z, along_x, 0), (along_z, along_x, 1)]
    for i, (one_way, other_way, turn) in enumerate(rounds):
        xr = lax.ppermute(xb, "dp", one_way(turn))
        zr = lax.ppermute(zb, "dp", other_way(turn))
        if i == 1:
            xa, xr, za, zr = xa[0], xr[0], za[0], zr[0]
        if i < 3:
            xa, xb = halve(xa, xr)
            za, zb = halve(za, zr)

    mine, fix, squares = owned_sum(xa, xr, za, zr, devices)
    fix = lax.ppermute(fix, "dp", CORE_PAIRS)
    squares = lax.all_to_all(squares, ("dp", "tensor"), 0, 0, tiled=True)

    limit_sq = float(3 * bases.shape[2] * total_units)
    new_first, new_second, pieces = update(
        limit_sq, place, squares, mine, fix, first_moment[:, 0], second_moment[:, 0], bases
    )
    pieces = lax.all_to_all(pieces, "dp", 0, 0, tiled=True)
    gate_update, up_update, down_update = layout(pieces)
    return (gate_update.T, up_update.T, down_update, new_first[:, None], new_second[:, None])


def solution(mesh):
    placed = (
        P("dp", None),
        P(None, "dp", "tensor"),
        P("dp", "tensor"),
        P("dp", None),
        P(),
        P(None, "tensor", "dp", None),
        P(None, "tensor", "dp", None),
    )
    return jax.shard_map(
        body,
        mesh=mesh,
        in_specs=placed,
        out_specs=(
            P("dp", "tensor"),
            P("dp", "tensor"),
            P("tensor", "dp"),
            P(None, "tensor", "dp", None),
            P(None, "tensor", "dp", None),
        ),
        check_vma=False,
    )
```

time: 319 us -> 144 us (0.45)
  waiting for transfers between devices: 176 us -> 68.2 us
  blocking collectives: 65.6 us -> 0 us
  Pallas kernels: 0 us -> 35.3 us
  matrix products: 33.9 us -> 0 us
  starting transfers between devices: 0.08 us -> 29.1 us
  between operations: 15.4 us -> 0.78 us
  other arithmetic: 10.3 us -> 1.29 us
  local copies, waits for them, and re-layouts: 15.8 us -> 8.57 us
    unnamed x3 -> x0, waiting for transfers between devices: 122 us -> none
    psum x1 -> x0, blocking collectives: 65.6 us -> none  [global_squares(): return lax.psum(jnp.sum(values * values), ('dp', 'tensor'))]
    all_gather x1 -> x0, waiting for transfers between devices: 54 us -> none  [body(): gathered = lax.all_gather(direction, 'dp', axis=1, tiled=True)]
    all_to_all x0 -> x2, waiting for transfers between devices: none -> 37 us  [the longest x1 28.1 us: body(): pieces = lax.all_to_all(pieces, 'dp', 0, 0, tiled=True)]
    pallas_call x0 -> x11, Pallas kernels: none -> 35.3 us  [the longest x1 11.8 us: collect(): pl.pallas_call(collect_kernel, grid_spec=pltpu.PrefetchScalarGridSpec(num...]
    dot_general x5 -> x0, matrix products: 33.9 us -> none  [the longest x1 9.8 us: body(): jnp.dot(up_out_grad.T, up_reduced, preferred_element_type=jnp.float32)]
    ppermute x0 -> x12, waiting for transfers between devices: none -> 31.2 us  [the longest x4 17.9 us: body(): zr = lax.ppermute(zb, 'dp', other_way(turn))]
    ppermute x0 -> x12, starting transfers between devices: none -> 16.7 us  [the longest x4 10.7 us: body(): zr = lax.ppermute(zb, 'dp', other_way(turn))]
  transfers between devices with their start and end apart: 2 -> 14, of which waited for: 2 -> 10; matrix products, arithmetic and copies ran while one was open for 1% -> 4% of each run, Pallas kernels for 0% -> 9%
where the time goes in v3:
time: 144 us; the launch traced here: 143 us
  waiting for transfers between devices  68.2 us (47%)
  Pallas kernels  35.3 us (25%)
  starting transfers between devices  29.1 us (20%)
  local copies, waits for them, and re-layouts  8.57 us (6%)
    all_to_all x1, waiting for transfers between devices, body(): pieces = lax.all_to_all(pieces, 'dp', 0, 0, tiled=True)  28.1 us
    ppermute x4, waiting for transfers between devices, body(): zr = lax.ppermute(zb, 'dp', other_way(turn))  17.9 us
    pallas_call x1, Pallas kernels, collect(): pl.pallas_call(collect_kernel, grid_spec=pltpu.PrefetchScalarGridSpec(num...  11.8 us
    pallas_call x1, Pallas kernels, project(): pl.pallas_call(functools.partial(project_kernel, steps, 4), in_specs=[SME...  11.6 us
    ppermute x4, waiting for transfers between devices, body(): xr = lax.ppermute(xb, 'dp', one_way(turn))  10.9 us
    ppermute x4, starting transfers between devices, body(): zr = lax.ppermute(zb, 'dp', other_way(turn))  10.7 us
    all_to_all x1, waiting for transfers between devices, body(): squares = lax.all_to_all(squares, ('dp', 'tensor'), 0, 0, tiled=True)  8.94 us
    pallas_call x1, Pallas kernels, update(): pl.pallas_call(functools.partial(update_kernel, limit_sq, 8), in_specs=[S...  8.88 us
  transfers between devices with their start and end apart: 14, of which 10 were waited for; matrix products, arithmetic and copies ran while one was open for 4% of the time, Pallas kernels for 9%

profile of v3, /device:TPU:0, one launch (start us, length us, event | category | flops | bytes accessed | tf_op | source)
XLA Modules:
  0.0 143.2 jit_solution(301318753393420838)
XLA Ops:
  1.2 0.7 dynamic-slice_bitcast_fusion
  1.9 0.6 gather_fusion
  2.6 0.7 xor_bitcast_fusion
  3.8 11.6 %project.1 = (bf16[3,512,256]{2,1,0:T(8,128)(2,1)}, bf16[3,512,256]{2,1,0:T(8,128)(2,1)}) custom-call(s32[9]{0:T(128)} %pad_add_fusion.place, bf16[512,4096]{1,0:T(8,128)(2,1)} %x_hbm.1, bf16[512,4096]{1,0:T(8,128)(2,1)} %y_hbm.1, bf16[3,4096,512]{2,1,0:T(8,128)(2,1)} %b_hbm.3), custom_call_target="tpu_custom_call" | custom-call | flops 6442450944 | bytes 20971520 | tf_op jit(solution)/shard_map/project/pallas_call | solution.py:98
  15.6 2.4 %collective-permute-done.2.theirs = bf16[3,512,256]{2,1,0:T(8,128)(2,1)S(1)} collective-permute-done((bf16[3,512,256]{2,1,0:T(8,128)(2,1)}, bf16[3,512,256]{2,1,0:T(8,128)(2,1)S(1)}, u32[]{:S(2)}, u32[]{:S(2)}) %collective-permute-start.2) | collective-permute-done | bytes 786464 | tf_op jit(solution)/shard_map/ppermute | solution.py:346
  18.0 0.9 copy-done.5
  18.8 1.0 copy-done.4
  19.8 11.8 %collect.1 = (bf16[2,4,3,2,88,128]{5,4,3,2,1,0:T(8,128)(2,1)}, bf16[2,4,3,2,88,128]{5,4,3,2,1,0:T(8,128)(2,1)}, bf16[2,4,3,2,88,128]{5,4,3,2,1,0:T(8,128)(2,1)}, bf16[2,4,3,2,88,128]{5,4,3,2,1,0:T(8,128)(2,1)}) custom-call(s32[9]{0:T(128)} %pad_add_fusion.place, bf16[2,2752,512]{2,1,0:T(8,128)(2,1)} %bitcast.35, bf16[1,2752,512]{2,1,0:T(8,128)(2,1)} %bitcast.37, ...), custom_call_target="tpu_custom_call" | custom-call | flops 4328521728 | bytes 21135360 | tf_op jit(solution)/shard_map/collect/pallas_call | solution.py:165
  31.6 2.1 %collective-permute-start.7 = (bf16[2,4,3,2,88,128]{5,4,3,2,1,0:T(8,128)(2,1)}, bf16[2,4,3,2,88,128]{5,4,3,2,1,0:T(8,128)(2,1)S(1)}, u32[]{:S(2)}, u32[]{:S(2)}) collective-permute-start(bf16[2,4,3,2,88,128]{5,4,3,2,1,0:T(8,128)(2,1)} %get-tuple-element.43), channel_id=1, source_target_pairs={{0,32},{4,100},{8,40},{12,108},{16,48},{20,116},{24,56},{28,124},{... | collective-permute-start | bytes 3244040 | tf_op jit(solution)/shard_map/ppermute | solution.py:352
  33.7 1.5 %collective-permute-start.3 = (bf16[2,4,3,2,88,128]{5,4,3,2,1,0:T(8,128)(2,1)}, bf16[2,4,3,2,88,128]{5,4,3,2,1,0:T(8,128)(2,1)S(1)}, u32[]{:S(2)}, u32[]{:S(2)}) collective-permute-start(bf16[2,4,3,2,88,128]{5,4,3,2,1,0:T(8,128)(2,1)} %get-tuple-element.35), channel_id=1, source_target_pairs={{0,8},{4,28},{8,0},{12,20},{16,24},{20,12},{24,16},{28,4},{32,40},... | collective-permute-start | bytes 3244040 | tf_op jit(solution)/shard_map/ppermute | solution.py:351
  35.2 11.9 %collective-permute-done.7.recv = bf16[2,4,3,2,88,128]{5,4,3,2,1,0:T(8,128)(2,1)S(1)} collective-permute-done((bf16[2,4,3,2,88,128]{5,4,3,2,1,0:T(8,128)(2,1)}, bf16[2,4,3,2,88,128]{5,4,3,2,1,0:T(8,128)(2,1)S(1)}, u32[]{:S(2)}, u32[]{:S(2)}) %collective-permute-start.7) | collective-permute-done | bytes 1081376 | tf_op jit(solution)/shard_map/ppermute | solution.py:352
  47.1 1.2 copy-done.2
  48.5 4.2 %collective-permute-start.8 = (bf16[1,4,3,2,88,128]{5,4,3,2,1,0:T(8,128)(2,1)S(1)}, bf16[1,4,3,2,88,128]{5,4,3,2,1,0:T(8,128)(2,1)S(1)}, u32[]{:S(2)}, u32[]{:S(2)}) collective-permute-start(bf16[1,4,3,2,88,128]{5,4,3,2,1,0:T(8,128)(2,1)S(1)} %get-tuple-element.45), channel_id=1, source_target_pairs={{0,96},{4,36},{8,104},{12,44},{16,112},{20,52},{24,120},{28,60},{3... | collective-permute-start | bytes 1622024 | tf_op jit(solution)/shard_map/ppermute | solution.py:352
  53.0 2.8 %collective-permute-start.4 = (bf16[1,4,3,2,88,128]{5,4,3,2,1,0:T(8,128)(2,1)S(1)}, bf16[1,4,3,2,88,128]{5,4,3,2,1,0:T(8,128)(2,1)S(1)}, u32[]{:S(2)}, u32[]{:S(2)}) collective-permute-start(bf16[1,4,3,2,88,128]{5,4,3,2,1,0:T(8,128)(2,1)S(1)} %get-tuple-element.37), channel_id=1, source_target_pairs={{0,24},{4,12},{8,16},{12,4},{16,8},{20,28},{24,0},{28,20},{32,56},... | collective-permute-start | bytes 1622024 | tf_op jit(solution)/shard_map/ppermute | solution.py:351
  55.9 4.2 %collective-permute-done.8 = bf16[1,4,3,2,88,128]{5,4,3,2,1,0:T(8,128)(2,1)S(1)} collective-permute-done((bf16[1,4,3,2,88,128]{5,4,3,2,1,0:T(8,128)(2,1)S(1)}, bf16[1,4,3,2,88,128]{5,4,3,2,1,0:T(8,128)(2,1)S(1)}, u32[]{:S(2)}, u32[]{:S(2)}) %collective-permute-start.8) | collective-permute-done | bytes 540704 | tf_op jit(solution)/shard_map/ppermute | solution.py:352
  60.2 1.6 %collective-permute-start.9 = (bf16[2,3,2,88,128]{4,3,2,1,0:T(8,128)(2,1)S(1)}, bf16[2,3,2,88,128]{4,3,2,1,0:T(8,128)(2,1)S(1)}, u32[]{:S(2)}, u32[]{:S(2)}) collective-permute-start(bf16[2,3,2,88,128]{4,3,2,1,0:T(8,128)(2,1)S(1)} %get-tuple-element.47), channel_id=1, source_target_pairs={{0,8},{4,28},{8,0},{12,20},{16,24},{20,12},{24,16},{28,4},{32,40},... | collective-permute-start | bytes 811016 | tf_op jit(solution)/shard_map/ppermute | solution.py:352
  61.8 3.0 %collective-permute-done.4 = bf16[1,4,3,2,88,128]{5,4,3,2,1,0:T(8,128)(2,1)S(1)} collective-permute-done((bf16[1,4,3,2,88,128]{5,4,3,2,1,0:T(8,128)(2,1)S(1)}, bf16[1,4,3,2,88,128]{5,4,3,2,1,0:T(8,128)(2,1)S(1)}, u32[]{:S(2)}, u32[]{:S(2)}) %collective-permute-start.4) | collective-permute-done | bytes 540704 | tf_op jit(solution)/shard_map/ppermute | solution.py:351
  65.0 1.8 %collective-permute-done.9.recv = bf16[2,3,2,88,128]{4,3,2,1,0:T(8,128)(2,1)S(1)} collective-permute-done((bf16[2,3,2,88,128]{4,3,2,1,0:T(8,128)(2,1)S(1)}, bf16[2,3,2,88,128]{4,3,2,1,0:T(8,128)(2,1)S(1)}, u32[]{:S(2)}, u32[]{:S(2)}) %collective-permute-start.9) | collective-permute-done | bytes 270368 | tf_op jit(solution)/shard_map/ppermute | solution.py:352
  66.8 2.8 %collective-permute-start.10 = (bf16[1,3,2,88,128]{4,3,2,1,0:T(8,128)(2,1)S(1)}, bf16[1,3,2,88,128]{4,3,2,1,0:T(8,128)(2,1)S(1)}, u32[]{:S(2)}, u32[]{:S(2)}) collective-permute-start(bf16[1,3,2,88,128]{4,3,2,1,0:T(8,128)(2,1)S(1)} %get-tuple-element.49), channel_id=1, source_target_pairs={{0,24},{4,12},{8,16},{12,4},{16,8},{20,28},{24,0},{28,20},{32,56},... | collective-permute-start | bytes 405512 | tf_op jit(solution)/shard_map/ppermute | solution.py:352
  69.7 2.5 %collective-permute-done.5.recv = bf16[2,3,2,88,128]{4,3,2,1,0:T(8,128)(2,1)S(1)} collective-permute-done((bf16[2,3,2,88,128]{4,3,2,1,0:T(8,128)(2,1)S(1)}, bf16[2,3,2,88,128]{4,3,2,1,0:T(8,128)(2,1)S(1)}, u32[]{:S(2)}, u32[]{:S(2)}) %collective-permute-start.5) | collective-permute-done | bytes 270368 | tf_op jit(solution)/shard_map/ppermute | solution.py:351
  72.2 0.8 collective-permute-start.6
  73.1 5.4 %collective-permute-done.6.xb = bf16[1,3,2,88,128]{4,3,2,1,0:T(8,128)(2,1)S(1)} collective-permute-done((bf16[1,3,2,88,128]{4,3,2,1,0:T(8,128)(2,1)S(1)}, bf16[1,3,2,88,128]{4,3,2,1,0:T(8,128)(2,1)S(1)}, u32[]{:S(2)}, u32[]{:S(2)}) %collective-permute-start.6) | collective-permute-done | bytes 135200 | tf_op jit(solution)/shard_map/ppermute | solution.py:351
  78.5 0.7 owned_sum.1
  79.3 8.4 %all-to-all-start = ((f32[128,1,128]{2,1,0:T(1,128)}), f32[128,1,128]{2,1,0:T(1,128)S(1)}, u32[]{:S(2)}, u32[]{:S(2)}) async-start(f32[128,1,128]{2,1,0:T(1,128)} %bitcast.13), calls=%async_computation | async-start | bytes 131072 | tf_op jit(solution)/shard_map/all_to_all | solution.py:361
  87.8 8.9 %all-to-all-done = f32[128,1,128]{2,1,0:T(1,128)S(1)} async-done(((f32[128,1,128]{2,1,0:T(1,128)}), f32[128,1,128]{2,1,0:T(1,128)S(1)}, u32[]{:S(2)}, u32[]{:S(2)}) %all-to-all-start) | async-done | bytes 65568 | tf_op jit(solution)/shard_map/all_to_all | solution.py:361
  96.7 8.9 %update.1 = (f32[3,86,512]{2,1,0:T(8,128)S(1)}, f32[3,86,512]{2,1,0:T(8,128)S(1)}, bf16[32,3,88,128]{3,2,1,0:T(8,128)(2,1)S(1)}) custom-call(s32[9]{0:T(128)S(1)} %copy-done.3, f32[128,128]{1,0:T(8,128)S(1)} %bitcast.33, f32[3,88,256]{2,1,0:T(8,128)S(1)} %get-tuple-element.51.mine, bf16[3,88,256]{2,1,0:T(8,128)(2,1)S(1)} %collective-permute-done.11.recv, ...), custom_call_target="tpu_custom_call" | custom-call | tf_op jit(solution)/shard_map/update/pallas_call | solution.py:291
  105.6 1.4 copy-done
  107.0 4.1 %all-to-all-start.1 = ((bf16[32,3,88,128]{3,2,1,0:T(8,128)(2,1)}), bf16[32,3,88,128]{3,2,1,0:T(8,128)(2,1)S(1)}, u32[]{:S(2)}, u32[]{:S(2)}) async-start(bf16[32,3,88,128]{3,2,1,0:T(8,128)(2,1)} %copy-done), calls=%async_computation.1 | async-start | bytes 4325376 | tf_op jit(solution)/shard_map/all_to_all | solution.py:367
  111.0 1.3 copy.19
  112.4 1.3 copy.20
  113.7 28.1 %all-to-all-done.1.pieces = bf16[32,3,88,128]{3,2,1,0:T(8,128)(2,1)S(1)} async-done(((bf16[32,3,88,128]{3,2,1,0:T(8,128)(2,1)}), bf16[32,3,88,128]{3,2,1,0:T(8,128)(2,1)S(1)}, u32[]{:S(2)}, u32[]{:S(2)}) %all-to-all-start.1) | async-done | bytes 2162720 | tf_op jit(solution)/shard_map/all_to_all | solution.py:367
  141.8 1.5 %layout.1 = (bf16[2752,128]{1,0:T(8,128)(2,1)}, bf16[2752,128]{1,0:T(8,128)(2,1)}, bf16[2752,128]{1,0:T(8,128)(2,1)}) custom-call(bf16[32,3,88,128]{3,2,1,0:T(8,128)(2,1)S(1)} %all-to-all-done.1.pieces), custom_call_target="tpu_custom_call" | custom-call | tf_op jit(solution)/shard_map/layout/pallas_call | solution.py:320
  (32 shorter events, 2.5 us)
Async XLA Ops:
  0.6 17.4 %collective-permute-start = (bf16[2,2752,512]{2,1,0:T(8,128)(2,1)}, bf16[2,2752,512]{2,1,0:T(8,128)(2,1)}, u32[]{:S(2)}, u32[]{:S(2)}) collective-permute-start(bf16[2,2752,512]{2,1,0:T(8,128)(2,1)} %bitcast.34), channel_id=1, source_target_pairs={{0,4},{4,0},{8,12},{12,8},{16,20},{20,16},{24,28},{28,24},{32,36},... | collective-permute-start | bytes 16908296 | tf_op jit(solution)/shard_map/ppermute | solution.py:343
  0.7 17.3 %collective-permute-start.1 = (bf16[1,2752,512]{2,1,0:T(8,128)(2,1)}, bf16[1,2752,512]{2,1,0:T(8,128)(2,1)S(1)}, u32[]{:S(2)}, u32[]{:S(2)}) collective-permute-start(bf16[1,2752,512]{2,1,0:T(8,128)(2,1)} %bitcast.36), channel_id=1, source_target_pairs={{0,4},{4,0},{8,12},{12,8},{16,20},{20,16},{24,28},{28,24},{32,36},... | collective-permute-start | bytes 8454152 | tf_op jit(solution)/shard_map/ppermute | solution.py:344
  15.4 2.6 %collective-permute-start.2 = (bf16[3,512,256]{2,1,0:T(8,128)(2,1)}, bf16[3,512,256]{2,1,0:T(8,128)(2,1)S(1)}, u32[]{:S(2)}, u32[]{:S(2)}) collective-permute-start(bf16[3,512,256]{2,1,0:T(8,128)(2,1)} %get-tuple-element.33), channel_id=1, source_target_pairs={{0,4},{4,0},{8,12},{12,8},{16,20},{20,16},{24,28},{28,24},{32,36},... | collective-permute-start | bytes 2359304 | tf_op jit(solution)/shard_map/ppermute | solution.py:346
  18.0 0.9 copy-start.5
  18.0 1.9 %copy-start.4 = (bf16[1,2752,512]{2,1,0:T(8,128)(2,1)}, bf16[1,2752,512]{2,1,0:T(8,128)(2,1)S(1)}, u32[]{:S(2)}) copy-start(bf16[1,2752,512]{2,1,0:T(8,128)(2,1)S(1)} %collective-permute-done.1.h_one) | copy-start | bytes 8454148
  31.6 21.1 %copy-start.1 = (bf16[2,4,3,2,88,128]{5,4,3,2,1,0:T(8,128)(2,1)S(1)}, bf16[2,4,3,2,88,128]{5,4,3,2,1,0:T(8,128)(2,1)}, u32[]{:S(2)}) copy-start(bf16[2,4,3,2,88,128]{5,4,3,2,1,0:T(8,128)(2,1)} %get-tuple-element.34.kept) | copy-start | bytes 3244036
  31.6 15.4 %collective-permute-start.7 = (bf16[2,4,3,2,88,128]{5,4,3,2,1,0:T(8,128)(2,1)}, bf16[2,4,3,2,88,128]{5,4,3,2,1,0:T(8,128)(2,1)S(1)}, u32[]{:S(2)}, u32[]{:S(2)}) collective-permute-start(bf16[2,4,3,2,88,128]{5,4,3,2,1,0:T(8,128)(2,1)} %get-tuple-element.43), channel_id=1, source_target_pairs={{0,32},{4,100},{8,40},{12,108},{16,48},{20,116},{24,56},{28,124},{... | collective-permute-start | bytes 3244040 | tf_op jit(solution)/shard_map/ppermute | solution.py:352
  33.7 19.1 %collective-permute-start.3 = (bf16[2,4,3,2,88,128]{5,4,3,2,1,0:T(8,128)(2,1)}, bf16[2,4,3,2,88,128]{5,4,3,2,1,0:T(8,128)(2,1)S(1)}, u32[]{:S(2)}, u32[]{:S(2)}) collective-permute-start(bf16[2,4,3,2,88,128]{5,4,3,2,1,0:T(8,128)(2,1)} %get-tuple-element.35), channel_id=1, source_target_pairs={{0,8},{4,28},{8,0},{12,20},{16,24},{20,12},{24,16},{28,4},{32,40},... | collective-permute-start | bytes 3244040 | tf_op jit(solution)/shard_map/ppermute | solution.py:351
  47.1 1.2 copy-start.2
  48.5 11.5 %collective-permute-start.8 = (bf16[1,4,3,2,88,128]{5,4,3,2,1,0:T(8,128)(2,1)S(1)}, bf16[1,4,3,2,88,128]{5,4,3,2,1,0:T(8,128)(2,1)S(1)}, u32[]{:S(2)}, u32[]{:S(2)}) collective-permute-start(bf16[1,4,3,2,88,128]{5,4,3,2,1,0:T(8,128)(2,1)S(1)} %get-tuple-element.45), channel_id=1, source_target_pairs={{0,96},{4,36},{8,104},{12,44},{16,112},{20,52},{24,120},{28,60},{3... | collective-permute-start | bytes 1622024 | tf_op jit(solution)/shard_map/ppermute | solution.py:352
  53.0 34.6 %copy-start.6 = (f32[3,1,86,512]{3,1,2,0:T(1,128)S(1)}, f32[3,1,86,512]{3,1,2,0:T(1,128)}, u32[]{:S(2)}) copy-start(f32[3,1,86,512]{3,1,2,0:T(1,128)} %param.15) | copy-start | bytes 1585156
  53.0 34.6 %copy-start.7 = (f32[3,1,86,512]{3,1,2,0:T(1,128)S(1)}, f32[3,1,86,512]{3,1,2,0:T(1,128)}, u32[]{:S(2)}) copy-start(f32[3,1,86,512]{3,1,2,0:T(1,128)} %param.14) | copy-start | bytes 1585156
  53.0 11.7 %collective-permute-start.4 = (bf16[1,4,3,2,88,128]{5,4,3,2,1,0:T(8,128)(2,1)S(1)}, bf16[1,4,3,2,88,128]{5,4,3,2,1,0:T(8,128)(2,1)S(1)}, u32[]{:S(2)}, u32[]{:S(2)}) collective-permute-start(bf16[1,4,3,2,88,128]{5,4,3,2,1,0:T(8,128)(2,1)S(1)} %get-tuple-element.37), channel_id=1, source_target_pairs={{0,24},{4,12},{8,16},{12,4},{16,8},{20,28},{24,0},{28,20},{32,56},... | collective-permute-start | bytes 1622024 | tf_op jit(solution)/shard_map/ppermute | solution.py:351
  60.2 6.5 %collective-permute-start.9 = (bf16[2,3,2,88,128]{4,3,2,1,0:T(8,128)(2,1)S(1)}, bf16[2,3,2,88,128]{4,3,2,1,0:T(8,128)(2,1)S(1)}, u32[]{:S(2)}, u32[]{:S(2)}) collective-permute-start(bf16[2,3,2,88,128]{4,3,2,1,0:T(8,128)(2,1)S(1)} %get-tuple-element.47), channel_id=1, source_target_pairs={{0,8},{4,28},{8,0},{12,20},{16,24},{20,12},{24,16},{28,4},{32,40},... | collective-permute-start | bytes 811016 | tf_op jit(solution)/shard_map/ppermute | solution.py:352
  64.9 31.8 %copy-start.3 = (s32[9]{0:T(128)S(1)}, s32[9]{0:T(128)}, u32[]{:S(2)}) copy-start(s32[9]{0:T(128)} %pad_add_fusion.place) | copy-start | bytes 112
  64.9 7.2 %collective-permute-start.5 = (bf16[2,3,2,88,128]{4,3,2,1,0:T(8,128)(2,1)S(1)}, bf16[2,3,2,88,128]{4,3,2,1,0:T(8,128)(2,1)S(1)}, u32[]{:S(2)}, u32[]{:S(2)}) collective-permute-start(bf16[2,3,2,88,128]{4,3,2,1,0:T(8,128)(2,1)S(1)} %get-tuple-element.39), channel_id=1, source_target_pairs={{0,32},{4,100},{8,40},{12,108},{16,48},{20,116},{24,56},{28,124},{... | collective-permute-start | bytes 811016 | tf_op jit(solution)/shard_map/ppermute | solution.py:351
  66.8 6.3 %collective-permute-start.10 = (bf16[1,3,2,88,128]{4,3,2,1,0:T(8,128)(2,1)S(1)}, bf16[1,3,2,88,128]{4,3,2,1,0:T(8,128)(2,1)S(1)}, u32[]{:S(2)}, u32[]{:S(2)}) collective-permute-start(bf16[1,3,2,88,128]{4,3,2,1,0:T(8,128)(2,1)S(1)} %get-tuple-element.49), channel_id=1, source_target_pairs={{0,24},{4,12},{8,16},{12,4},{16,8},{20,28},{24,0},{28,20},{32,56},... | collective-permute-start | bytes 405512 | tf_op jit(solution)/shard_map/ppermute | solution.py:352
  72.2 6.3 %collective-permute-start.6 = (bf16[1,3,2,88,128]{4,3,2,1,0:T(8,128)(2,1)S(1)}, bf16[1,3,2,88,128]{4,3,2,1,0:T(8,128)(2,1)S(1)}, u32[]{:S(2)}, u32[]{:S(2)}) collective-permute-start(bf16[1,3,2,88,128]{4,3,2,1,0:T(8,128)(2,1)S(1)} %get-tuple-element.41), channel_id=1, source_target_pairs={{0,96},{4,36},{8,104},{12,44},{16,112},{20,52},{24,120},{28,60},{3... | collective-permute-start | bytes 405512 | tf_op jit(solution)/shard_map/ppermute | solution.py:351
  79.3 17.4 %collective-permute-start.11 = (bf16[3,88,256]{2,1,0:T(8,128)(2,1)S(1)}, bf16[3,88,256]{2,1,0:T(8,128)(2,1)S(1)}, u32[]{:S(2)}, u32[]{:S(2)}) collective-permute-start(bf16[3,88,256]{2,1,0:T(8,128)(2,1)S(1)} %get-tuple-element.52), channel_id=1, source_target_pairs={{0,4},{4,0},{8,12},{12,8},{16,20},{20,16},{24,28},{28,24},{32,36},... | collective-permute-start | bytes 405512 | tf_op jit(solution)/shard_map/ppermute | solution.py:360
  79.3 17.4 %all-to-all-start = ((f32[128,1,128]{2,1,0:T(1,128)}), f32[128,1,128]{2,1,0:T(1,128)S(1)}, u32[]{:S(2)}, u32[]{:S(2)}) async-start(f32[128,1,128]{2,1,0:T(1,128)} %bitcast.13), calls=%async_computation | async-start | bytes 131072 | tf_op jit(solution)/shard_map/all_to_all | solution.py:361
  105.6 1.4 copy-start
  107.0 34.8 %all-to-all-start.1 = ((bf16[32,3,88,128]{3,2,1,0:T(8,128)(2,1)}), bf16[32,3,88,128]{3,2,1,0:T(8,128)(2,1)S(1)}, u32[]{:S(2)}, u32[]{:S(2)}) async-start(bf16[32,3,88,128]{3,2,1,0:T(8,128)(2,1)} %copy-done), calls=%async_computation.1 | async-start | bytes 4325376 | tf_op jit(solution)/shard_map/all_to_all | solution.py:367

commit v4 on v3

--- a/solution.py
+++ b/solution.py
@@ -2,6 +2,7 @@
 
 import jax
 import jax.numpy as jnp
+import numpy as np
 from jax import lax
 from jax.experimental import pallas as pl
 from jax.experimental.pallas import tpu as pltpu
@@ -40,6 +41,23 @@
 
 def along_z(turn):
     return [(dp_index(z, x, c), dp_index(z ^ FLIPS[c][turn], x, c)) for z, x, c in every_chip()]
+
+
+def direct_x(r):
+    return [(dp_index(z, x, c), dp_index(z, x ^ FLIP_ORDER[c][r], c)) for z, x, c in every_chip()]
+
+
+def direct_z(r):
+    return [(dp_index(z, x, c), dp_index(z ^ FLIP_ORDER[c][r], x, c)) for z, x, c in every_chip()]
+
+
+PLACES = np.array(
+    [
+        [z ^ d for d in FLIP_ORDER[c]] + [RANK_OF[c][block ^ x] for block in range(N_X)] + [c]
+        for z, x, c in every_chip()
+    ],
+    np.int32,
+)
 
 
 VMEM = pl.BlockSpec(memory_space=pltpu.VMEM)
@@ -180,7 +198,7 @@
             ],
         ),
         out_shape=[jax.ShapeDtypeStruct(shape, BF16)] * 4,
-        compiler_params=params(58),
+        compiler_params=params(24),
         cost_estimate=pl.CostEstimate(
             flops=2 * 3 * 2 * tokens * units * half,
             bytes_accessed=2 * 3 * units * (2 * tokens + half),
@@ -190,32 +208,36 @@
     )(place, g_two, g_one, h_two, h_one, mine, theirs)
 
 
-def halve_kernel(kept, recv, stay, go):
-    n = kept.shape[0] // 2
-    for out, at in ((stay, slice(0, n)), (go, slice(n, 2 * n))):
+def split_kernel(kept, recv, *outs):
+    n = kept.shape[0] // len(outs)
+    for i, out in enumerate(outs):
+        at = slice(i * n, (i + 1) * n)
         out[...] = (kept[at].astype(F32) + recv[at].astype(F32)).astype(BF16)
 
 
-def halve(kept, recv):
-    shape = (kept.shape[0] // 2, *kept.shape[1:])
-    return pl.pallas_call(
-        halve_kernel,
+def split_sum(kept, recv, parts):
+    shape = (kept.shape[0] // parts, *kept.shape[1:])
+    return pl.pallas_call(
+        split_kernel,
         in_specs=[VMEM] * 2,
-        out_specs=[VMEM] * 2,
-        out_shape=[jax.ShapeDtypeStruct(shape, BF16)] * 2,
+        out_specs=[VMEM] * parts,
+        out_shape=[jax.ShapeDtypeStruct(shape, BF16)] * parts,
         compiler_params=params(12),
-        name="halve",
+        name="split_sum",
     )(kept, recv)
 
 
-def owned_kernel(xa, xb, za, zb, mine, fix, squares):
+def owned_kernel(*refs):
+    parts, (mine, fix, squares) = refs[:8], refs[8:]
     inside = lax.broadcasted_iota(jnp.int32, (PAD, LANES), 0) < UNITS
     total_sq = jnp.zeros((PAD, LANES), F32)
-    for half, (p, q) in enumerate(((xa, xb), (za, zb))):
+    for half in range(2):
+        t = parts[4 * half : 4 * half + 4]
         lanes = slice(half * LANES, half * LANES + LANES)
         for m in range(3):
             for c in range(N_C):
-                v = p[0, m, c].astype(F32) + q[0, m, c].astype(F32)
+                v = t[0][0, m, c].astype(F32) + t[1][0, m, c].astype(F32)
+                v = v + (t[2][0, m, c].astype(F32) + t[3][0, m, c].astype(F32))
                 total_sq += jnp.where(inside, v * v, 0.0)
                 if c == 0:
                     mine[m, :, lanes] = v
@@ -225,10 +247,10 @@
     squares[...] = jnp.broadcast_to(row, squares.shape)
 
 
-def owned_sum(xa, xb, za, zb, peers):
+def owned_sum(by_x, by_z, peers):
     return pl.pallas_call(
         owned_kernel,
-        in_specs=[VMEM] * 4,
+        in_specs=[VMEM] * 8,
         out_specs=[VMEM] * 3,
         out_shape=[
             jax.ShapeDtypeStruct((3, PAD, 2 * LANES), F32),
@@ -237,7 +259,7 @@
         ],
         compiler_params=params(12),
         name="owned_sum",
-    )(xa, xb, za, zb)
+    )(*by_x, *by_z)
 
 
 def update_kernel(
@@ -332,11 +354,7 @@
     devices = lax.axis_size("dp") * lax.axis_size("tensor")
     total_units = hidden_act.shape[1] * lax.axis_size("tensor")
     me = lax.axis_index("dp")
-    z, x, c = me // (N_X * N_C), (me // N_C) % N_X, me % N_C
-    order = jnp.asarray(FLIP_ORDER, jnp.int32)[c]
-    ranks = jnp.asarray(RANK_OF, jnp.int32)[c]
-    across = ranks[jnp.bitwise_xor(jnp.arange(N_X, dtype=jnp.int32), x)]
-    place = jnp.concatenate([jnp.bitwise_xor(order, z), across, c[None]]).astype(jnp.int32)
+    place = lax.dynamic_index_in_dim(jnp.asarray(PLACES), me, keepdims=False)
 
     gate_up = jnp.swapaxes(gate_up_grads, 1, 2)
     hidden = hidden_act.T[None]
@@ -346,17 +364,17 @@
     theirs = lax.ppermute(sent, "dp", CORE_PAIRS)
     xa, xb, za, zb = collect(place, gate_up, hidden, gate_up_there, hidden_there, kept, theirs)
 
-    rounds = [(along_x, along_z, 0), (along_x, along_z, 1), (along_z, along_x, 0), (along_z, along_x, 1)]
-    for i, (one_way, other_way, turn) in enumerate(rounds):
-        xr = lax.ppermute(xb, "dp", one_way(turn))
-        zr = lax.ppermute(zb, "dp", other_way(turn))
-        if i == 1:
-            xa, xr, za, zr = xa[0], xr[0], za[0], zr[0]
-        if i < 3:
-            xa, xb = halve(xa, xr)
-            za, zb = halve(za, zr)
-
-    mine, fix, squares = owned_sum(xa, xr, za, zr, devices)
+    xr = lax.ppermute(xb, "dp", along_x(0))
+    zr = lax.ppermute(zb, "dp", along_z(0))
+    xa, xb = split_sum(xa, xr, 2)
+    za, zb = split_sum(za, zr, 2)
+    xr = lax.ppermute(xb, "dp", along_x(1))
+    zr = lax.ppermute(zb, "dp", along_z(1))
+    by_x = split_sum(xa[0], xr[0], 4)
+    by_z = split_sum(za[0], zr[0], 4)
+    by_x = [by_x[0]] + [lax.ppermute(by_x[r], "dp", direct_z(r)) for r in (1, 2, 3)]
+    by_z = [by_z[0]] + [lax.ppermute(by_z[r], "dp", direct_x(r)) for r in (1, 2, 3)]
+    mine, fix, squares = owned_sum(by_x, by_z, devices)
     fix = lax.ppermute(fix, "dp", CORE_PAIRS)
     squares = lax.all_to_all(squares, ("dp", "tensor"), 0, 0, tiled=True)
 

time: 144 us -> 137 us (0.951)
  waiting for transfers between devices: 68.2 us -> 60.2 us
  starting transfers between devices: 29.1 us -> 35.3 us
  Pallas kernels: 35.3 us -> 32 us
    ppermute x8 -> x10, waiting for transfers between devices: 28.8 us -> 20.8 us  [the longest x1 11.7 us: body(): zr = lax.ppermute(zb, 'dp', along_z(0))]
    ppermute x8 -> x10, starting transfers between devices: 15.9 us -> 20.3 us  [the longest x3 4.95 us: body(): lax.ppermute(by_x[r], 'dp', direct_z(r))]
    pallas_call x1, Pallas kernels: 11.8 us -> 8.43 us  [collect(): pl.pallas_call(collect_kernel, grid_spec=pltpu.PrefetchScalarGridSpec(num...]
    all_to_all x1, starting transfers between devices: 8.36 us -> 10.1 us  [body(): squares = lax.all_to_all(squares, ('dp', 'tensor'), 0, 0, tiled=True)]
  transfers between devices with their start and end apart: 14 -> 16, of which waited for: 10 -> 9; matrix products, arithmetic and copies ran while one was open for 4% -> 3% of each run, Pallas kernels for 9% -> 9%
where the time goes in v4:
time: 137 us
  waiting for transfers between devices  60.2 us (44%)
  starting transfers between devices  35.3 us (26%)
  Pallas kernels  32 us (23%)
  local copies, waits for them, and re-layouts  8.44 us (6%)
    all_to_all x1, waiting for transfers between devices, body(): pieces = lax.all_to_all(pieces, 'dp', 0, 0, tiled=True)  28.1 us
    pallas_call x1, Pallas kernels, project(): pl.pallas_call(functools.partial(project_kernel, steps, 4), in_specs=[SME...  11.7 us
    ppermute x1, waiting for transfers between devices, body(): zr = lax.ppermute(zb, 'dp', along_z(0))  11.7 us
    all_to_all x1, starting transfers between devices, body(): squares = lax.all_to_all(squares, ('dp', 'tensor'), 0, 0, tiled=True)  10.1 us
    all_to_all x1, waiting for transfers between devices, body(): squares = lax.all_to_all(squares, ('dp', 'tensor'), 0, 0, tiled=True)  8.93 us
    pallas_call x1, Pallas kernels, update(): pl.pallas_call(functools.partial(update_kernel, limit_sq, 8), in_specs=[S...  8.87 us
    pallas_call x1, Pallas kernels, collect(): pl.pallas_call(collect_kernel, grid_spec=pltpu.PrefetchScalarGridSpec(num...  8.43 us
    unnamed x19, local copies, waits for them, and re-layouts  7.09 us
  transfers between devices with their start and end apart: 16, of which 9 were waited for; matrix products, arithmetic and copies ran while one was open for 3% of the time, Pallas kernels for 9%

profile of v4, /device:TPU:0, one launch (start us, length us, event | category | flops | bytes accessed | tf_op | source)
XLA Modules:
  0.0 136.7 jit_solution(2944625584578858637)
XLA Ops:
  0.7 0.5 collective-permute-start.1
  1.2 1.4 dynamic-slice_bitcast_fusion.place
  2.6 11.7 %project.1 = (bf16[3,512,256]{2,1,0:T(8,128)(2,1)}, bf16[3,512,256]{2,1,0:T(8,128)(2,1)}) custom-call(s32[9]{0:T(128)} %dynamic-slice_bitcast_fusion.place, bf16[512,4096]{1,0:T(8,128)(2,1)} %x_hbm.1, bf16[512,4096]{1,0:T(8,128)(2,1)} %y_hbm.1, bf16[3,4096,512]{2,1,0:T(8,128)(2,1)} %b_hbm.3), custom_call_target="tpu_custom_call" | custom-call | flops 6442450944 | bytes 20971520 | tf_op jit(solution)/shard_map/project/pallas_call | solution.py:116
  14.5 2.4 %collective-permute-done.2.theirs = bf16[3,512,256]{2,1,0:T(8,128)(2,1)S(1)} collective-permute-done((bf16[3,512,256]{2,1,0:T(8,128)(2,1)}, bf16[3,512,256]{2,1,0:T(8,128)(2,1)S(1)}, u32[]{:S(2)}, u32[]{:S(2)}) %collective-permute-start.2) | collective-permute-done | bytes 786464 | tf_op jit(solution)/shard_map/ppermute | solution.py:364
  16.9 1.8 %copy-done = bf16[512,2752]{0,1:T(8,128)(2,1)S(1)} copy-done((bf16[512,2752]{0,1:T(8,128)(2,1)S(1)}, bf16[512,2752]{0,1:T(8,128)(2,1)}, u32[]{:S(2)}) %copy-start) | copy-done | bytes 2818072
  18.7 1.1 copy-done.2
  19.8 8.4 %collect.1 = (bf16[2,4,3,2,88,128]{5,4,3,2,1,0:T(8,128)(2,1)S(1)}, bf16[2,4,3,2,88,128]{5,4,3,2,1,0:T(8,128)(2,1)S(1)}, bf16[2,4,3,2,88,128]{5,4,3,2,1,0:T(8,128)(2,1)S(1)}, bf16[2,4,3,2,88,128]{5,4,3,2,1,0:T(8,128)(2,1)S(1)}) custom-call(s32[9]{0:T(128)S(1)} %copy-done.3, bf16[2,2752,512]{2,1,0:T(8,128)(2,1)S(1)} %bitcast.25, ...), custom_call_target="tpu_custom_call" | custom-call | flops 4328521728 | bytes 21135360 | tf_op jit(solution)/shard_map/collect/pallas_call | solution.py:183
  28.3 2.1 %collective-permute-start.8 = (bf16[2,4,3,2,88,128]{5,4,3,2,1,0:T(8,128)(2,1)S(1)}, bf16[2,4,3,2,88,128]{5,4,3,2,1,0:T(8,128)(2,1)S(1)}, u32[]{:S(2)}, u32[]{:S(2)}) collective-permute-start(bf16[2,4,3,2,88,128]{5,4,3,2,1,0:T(8,128)(2,1)S(1)} %get-tuple-element.43), channel_id=1, source_target_pairs={{0,32},{4,100},{8,40},{12,108},{16,48},{20,116},{24,56},{28,124},{... | collective-permute-start | bytes 3244040 | tf_op jit(solution)/shard_map/ppermute | solution.py:368
  30.3 1.5 %collective-permute-start.3 = (bf16[2,4,3,2,88,128]{5,4,3,2,1,0:T(8,128)(2,1)S(1)}, bf16[2,4,3,2,88,128]{5,4,3,2,1,0:T(8,128)(2,1)S(1)}, u32[]{:S(2)}, u32[]{:S(2)}) collective-permute-start(bf16[2,4,3,2,88,128]{5,4,3,2,1,0:T(8,128)(2,1)S(1)} %get-tuple-element.35), channel_id=1, source_target_pairs={{0,8},{4,28},{8,0},{12,20},{16,24},{20,12},{24,16},{28,4},{32,40},... | collective-permute-start | bytes 3244040 | tf_op jit(solution)/shard_map/ppermute | solution.py:367
  31.8 11.7 %collective-permute-done.8.recv = bf16[2,4,3,2,88,128]{5,4,3,2,1,0:T(8,128)(2,1)S(1)} collective-permute-done((bf16[2,4,3,2,88,128]{5,4,3,2,1,0:T(8,128)(2,1)S(1)}, bf16[2,4,3,2,88,128]{5,4,3,2,1,0:T(8,128)(2,1)S(1)}, u32[]{:S(2)}, u32[]{:S(2)}) %collective-permute-start.8) | collective-permute-done | bytes 1081376 | tf_op jit(solution)/shard_map/ppermute | solution.py:368
  43.5 0.2 split_sum.6
  43.7 4.2 %collective-permute-start.9 = (bf16[1,4,3,2,88,128]{5,4,3,2,1,0:T(8,128)(2,1)S(1)}, bf16[1,4,3,2,88,128]{5,4,3,2,1,0:T(8,128)(2,1)S(1)}, u32[]{:S(2)}, u32[]{:S(2)}) collective-permute-start(bf16[1,4,3,2,88,128]{5,4,3,2,1,0:T(8,128)(2,1)S(1)} %get-tuple-element.45), channel_id=1, source_target_pairs={{0,96},{4,36},{8,104},{12,44},{16,112},{20,52},{24,120},{28,60},{3... | collective-permute-start | bytes 1622024 | tf_op jit(solution)/shard_map/ppermute | solution.py:372
  47.9 0.2 split_sum.4
  48.2 2.8 %collective-permute-start.4 = (bf16[1,4,3,2,88,128]{5,4,3,2,1,0:T(8,128)(2,1)S(1)}, bf16[1,4,3,2,88,128]{5,4,3,2,1,0:T(8,128)(2,1)S(1)}, u32[]{:S(2)}, u32[]{:S(2)}) collective-permute-start(bf16[1,4,3,2,88,128]{5,4,3,2,1,0:T(8,128)(2,1)S(1)} %get-tuple-element.37), channel_id=1, source_target_pairs={{0,24},{4,12},{8,16},{12,4},{16,8},{20,28},{24,0},{28,20},{32,56},... | collective-permute-start | bytes 1622024 | tf_op jit(solution)/shard_map/ppermute | solution.py:371
  51.1 4.2 %collective-permute-done.9 = bf16[1,4,3,2,88,128]{5,4,3,2,1,0:T(8,128)(2,1)S(1)} collective-permute-done((bf16[1,4,3,2,88,128]{5,4,3,2,1,0:T(8,128)(2,1)S(1)}, bf16[1,4,3,2,88,128]{5,4,3,2,1,0:T(8,128)(2,1)S(1)}, u32[]{:S(2)}, u32[]{:S(2)}) %collective-permute-start.9) | collective-permute-done | bytes 540704 | tf_op jit(solution)/shard_map/ppermute | solution.py:372
  55.4 2.8 %collective-permute-start.10 = (bf16[1,3,2,88,128]{4,3,2,1,0:T(8,128)(2,1)S(1)}, bf16[1,3,2,88,128]{4,3,2,1,0:T(8,128)(2,1)S(1)}, u32[]{:S(2)}, u32[]{:S(2)}) collective-permute-start(bf16[1,3,2,88,128]{4,3,2,1,0:T(8,128)(2,1)S(1)} %get-tuple-element.47), channel_id=1, source_target_pairs={{0,24},{4,12},{8,16},{12,4},{16,8},{20,28},{24,0},{28,20},{32,56},... | collective-permute-start | bytes 405512 | tf_op jit(solution)/shard_map/ppermute | solution.py:376
  58.5 1.7 %collective-permute-start.12 = (bf16[1,3,2,88,128]{4,3,2,1,0:T(8,128)(2,1)S(1)}, bf16[1,3,2,88,128]{4,3,2,1,0:T(8,128)(2,1)S(1)}, u32[]{:S(2)}, u32[]{:S(2)}) collective-permute-start(bf16[1,3,2,88,128]{4,3,2,1,0:T(8,128)(2,1)S(1)} %get-tuple-element.49), channel_id=1, source_target_pairs={{0,16},{4,20},{8,24},{12,28},{16,0},{20,4},{24,8},{28,12},{32,48},... | collective-permute-start | bytes 405512 | tf_op jit(solution)/shard_map/ppermute | solution.py:376
  60.3 3.3 %collective-permute-start.5 = (bf16[1,3,2,88,128]{4,3,2,1,0:T(8,128)(2,1)S(1)}, bf16[1,3,2,88,128]{4,3,2,1,0:T(8,128)(2,1)S(1)}, u32[]{:S(2)}, u32[]{:S(2)}) collective-permute-start(bf16[1,3,2,88,128]{4,3,2,1,0:T(8,128)(2,1)S(1)} %get-tuple-element.39), channel_id=1, source_target_pairs={{0,96},{4,36},{8,104},{12,44},{16,112},{20,52},{24,120},{28,60},{3... | collective-permute-start | bytes 405512 | tf_op jit(solution)/shard_map/ppermute | solution.py:375
  63.6 1.6 %collective-permute-start.7 = (bf16[1,3,2,88,128]{4,3,2,1,0:T(8,128)(2,1)S(1)}, bf16[1,3,2,88,128]{4,3,2,1,0:T(8,128)(2,1)S(1)}, u32[]{:S(2)}, u32[]{:S(2)}) collective-permute-start(bf16[1,3,2,88,128]{4,3,2,1,0:T(8,128)(2,1)S(1)} %get-tuple-element.41), channel_id=1, source_target_pairs={{0,64},{4,68},{8,72},{12,76},{16,80},{20,84},{24,88},{28,92},{32,9... | collective-permute-start | bytes 405512 | tf_op jit(solution)/shard_map/ppermute | solution.py:375
  65.4 2.2 %collective-permute-done.5.refs_1_ = bf16[1,3,2,88,128]{4,3,2,1,0:T(8,128)(2,1)S(1)} collective-permute-done((bf16[1,3,2,88,128]{4,3,2,1,0:T(8,128)(2,1)S(1)}, bf16[1,3,2,88,128]{4,3,2,1,0:T(8,128)(2,1)S(1)}, u32[]{:S(2)}, u32[]{:S(2)}) %collective-permute-start.5) | collective-permute-done | bytes 135200 | tf_op jit(solution)/shard_map/ppermute | solution.py:375
  67.5 1.1 collective-permute-done.6.refs_2_
  68.6 1.5 %collective-permute-done.7.refs_3_ = bf16[1,3,2,88,128]{4,3,2,1,0:T(8,128)(2,1)S(1)} collective-permute-done((bf16[1,3,2,88,128]{4,3,2,1,0:T(8,128)(2,1)S(1)}, bf16[1,3,2,88,128]{4,3,2,1,0:T(8,128)(2,1)S(1)}, u32[]{:S(2)}, u32[]{:S(2)}) %collective-permute-start.7) | collective-permute-done | bytes 135200 | tf_op jit(solution)/shard_map/ppermute | solution.py:375
  70.2 0.8 owned_sum.1
  71.0 10.1 %all-to-all-start = ((f32[128,1,128]{2,1,0:T(1,128)}), f32[128,1,128]{2,1,0:T(1,128)S(1)}, u32[]{:S(2)}, u32[]{:S(2)}) async-start(f32[128,1,128]{2,1,0:T(1,128)} %bitcast.10), calls=%async_computation | async-start | bytes 131072 | tf_op jit(solution)/shard_map/all_to_all | solution.py:379
  81.2 8.9 %all-to-all-done = f32[128,1,128]{2,1,0:T(1,128)S(1)} async-done(((f32[128,1,128]{2,1,0:T(1,128)}), f32[128,1,128]{2,1,0:T(1,128)S(1)}, u32[]{:S(2)}, u32[]{:S(2)}) %all-to-all-start) | async-done | bytes 65568 | tf_op jit(solution)/shard_map/all_to_all | solution.py:379
  90.2 8.9 %update.1 = (f32[3,86,512]{2,1,0:T(8,128)S(1)}, f32[3,86,512]{2,1,0:T(8,128)S(1)}, bf16[32,3,88,128]{3,2,1,0:T(8,128)(2,1)S(1)}) custom-call(s32[9]{0:T(128)S(1)} %copy-done.3, f32[128,128]{1,0:T(8,128)S(1)} %bitcast.34, f32[3,88,256]{2,1,0:T(8,128)S(1)} %get-tuple-element.51.mine, bf16[3,88,256]{2,1,0:T(8,128)(2,1)S(1)} %collective-permute-done.13.recv, ...), custom_call_target="tpu_custom_call" | custom-call | tf_op jit(solution)/shard_map/update/pallas_call | solution.py:313
  99.1 1.4 copy-done.1
  100.4 4.1 %all-to-all-start.1 = ((bf16[32,3,88,128]{3,2,1,0:T(8,128)(2,1)}), bf16[32,3,88,128]{3,2,1,0:T(8,128)(2,1)S(1)}, u32[]{:S(2)}, u32[]{:S(2)}) async-start(bf16[32,3,88,128]{3,2,1,0:T(8,128)(2,1)} %copy-done.1), calls=%async_computation.1 | async-start | bytes 4325376 | tf_op jit(solution)/shard_map/all_to_all | solution.py:385
  104.5 1.3 copy.16
  105.8 1.3 copy.17
  107.2 28.1 %all-to-all-done.1.pieces = bf16[32,3,88,128]{3,2,1,0:T(8,128)(2,1)S(1)} async-done(((bf16[32,3,88,128]{3,2,1,0:T(8,128)(2,1)}), bf16[32,3,88,128]{3,2,1,0:T(8,128)(2,1)S(1)}, u32[]{:S(2)}, u32[]{:S(2)}) %all-to-all-start.1) | async-done | bytes 2162720 | tf_op jit(solution)/shard_map/all_to_all | solution.py:385
  135.2 1.5 %layout.1 = (bf16[2752,128]{1,0:T(8,128)(2,1)}, bf16[2752,128]{1,0:T(8,128)(2,1)}, bf16[2752,128]{1,0:T(8,128)(2,1)}) custom-call(bf16[32,3,88,128]{3,2,1,0:T(8,128)(2,1)S(1)} %all-to-all-done.1.pieces), custom_call_target="tpu_custom_call" | custom-call | tf_op jit(solution)/shard_map/layout/pallas_call | solution.py:342
  (30 shorter events, 1.0 us)
Async XLA Ops:
  0.6 16.2 %collective-permute-start = (bf16[2,2752,512]{2,1,0:T(8,128)(2,1)}, bf16[2,2752,512]{2,1,0:T(8,128)(2,1)}, u32[]{:S(2)}, u32[]{:S(2)}) collective-permute-start(bf16[2,2752,512]{2,1,0:T(8,128)(2,1)} %bitcast.22), channel_id=1, source_target_pairs={{0,4},{4,0},{8,12},{12,8},{16,20},{20,16},{24,28},{28,24},{32,36},... | collective-permute-start | bytes 16908296 | tf_op jit(solution)/shard_map/ppermute | solution.py:361
  0.7 16.1 %collective-permute-start.1 = (bf16[1,2752,512]{2,1,0:T(8,128)(2,1)}, bf16[1,2752,512]{2,1,0:T(8,128)(2,1)}, u32[]{:S(2)}, u32[]{:S(2)}) collective-permute-start(bf16[1,2752,512]{2,1,0:T(8,128)(2,1)} %bitcast.26), channel_id=1, source_target_pairs={{0,4},{4,0},{8,12},{12,8},{16,20},{20,16},{24,28},{28,24},{32,36},... | collective-permute-start | bytes 8454152 | tf_op jit(solution)/shard_map/ppermute | solution.py:362
  1.2 15.6 %slice-start = ((s8[5636096]{0:T(1024)(128)(4,1)}), s8[4194304]{0:T(1024)(128)(4,1)S(1)}, s32[]{:S(2)}) async-start(s8[5636096]{0:T(1024)(128)(4,1)} %bitcast.23), calls=%async_computation.2 | async-start | bytes 8388608
  2.6 14.3 %slice-start.1 = ((s8[5636096]{0:T(1024)(128)(4,1)}), s8[1441792]{0:T(1024)(128)(4,1)S(1)}, s32[]{:S(2)}) async-start(s8[5636096]{0:T(1024)(128)(4,1)} %bitcast.23), calls=%async_computation.3 | async-start | bytes 2883584
  2.6 14.3 %copy-start.3 = (s32[9]{0:T(128)S(1)}, s32[9]{0:T(128)}, u32[]{:S(2)}) copy-start(s32[9]{0:T(128)} %dynamic-slice_bitcast_fusion.place) | copy-start | bytes 112
  14.3 2.6 %collective-permute-start.2 = (bf16[3,512,256]{2,1,0:T(8,128)(2,1)}, bf16[3,512,256]{2,1,0:T(8,128)(2,1)S(1)}, u32[]{:S(2)}, u32[]{:S(2)}) collective-permute-start(bf16[3,512,256]{2,1,0:T(8,128)(2,1)} %get-tuple-element.33), channel_id=1, source_target_pairs={{0,4},{4,0},{8,12},{12,8},{16,20},{20,16},{24,28},{28,24},{32,36},... | collective-permute-start | bytes 2359304 | tf_op jit(solution)/shard_map/ppermute | solution.py:364
  16.9 1.8 %copy-start = (bf16[512,2752]{0,1:T(8,128)(2,1)S(1)}, bf16[512,2752]{0,1:T(8,128)(2,1)}, u32[]{:S(2)}) copy-start(bf16[512,2752]{0,1:T(8,128)(2,1)} %param.10) | copy-start | bytes 8454148
  18.7 1.1 copy-start.2
  28.3 15.2 %collective-permute-start.8 = (bf16[2,4,3,2,88,128]{5,4,3,2,1,0:T(8,128)(2,1)S(1)}, bf16[2,4,3,2,88,128]{5,4,3,2,1,0:T(8,128)(2,1)S(1)}, u32[]{:S(2)}, u32[]{:S(2)}) collective-permute-start(bf16[2,4,3,2,88,128]{5,4,3,2,1,0:T(8,128)(2,1)S(1)} %get-tuple-element.43), channel_id=1, source_target_pairs={{0,32},{4,100},{8,40},{12,108},{16,48},{20,116},{24,56},{28,124},{... | collective-permute-start | bytes 3244040 | tf_op jit(solution)/shard_map/ppermute | solution.py:368
  30.3 17.6 %collective-permute-start.3 = (bf16[2,4,3,2,88,128]{5,4,3,2,1,0:T(8,128)(2,1)S(1)}, bf16[2,4,3,2,88,128]{5,4,3,2,1,0:T(8,128)(2,1)S(1)}, u32[]{:S(2)}, u32[]{:S(2)}) collective-permute-start(bf16[2,4,3,2,88,128]{5,4,3,2,1,0:T(8,128)(2,1)S(1)} %get-tuple-element.35), channel_id=1, source_target_pairs={{0,8},{4,28},{8,0},{12,20},{16,24},{20,12},{24,16},{28,4},{32,40},... | collective-permute-start | bytes 3244040 | tf_op jit(solution)/shard_map/ppermute | solution.py:367
  43.7 11.5 %collective-permute-start.9 = (bf16[1,4,3,2,88,128]{5,4,3,2,1,0:T(8,128)(2,1)S(1)}, bf16[1,4,3,2,88,128]{5,4,3,2,1,0:T(8,128)(2,1)S(1)}, u32[]{:S(2)}, u32[]{:S(2)}) collective-permute-start(bf16[1,4,3,2,88,128]{5,4,3,2,1,0:T(8,128)(2,1)S(1)} %get-tuple-element.45), channel_id=1, source_target_pairs={{0,96},{4,36},{8,104},{12,44},{16,112},{20,52},{24,120},{28,60},{3... | collective-permute-start | bytes 1622024 | tf_op jit(solution)/shard_map/ppermute | solution.py:372
  48.2 32.9 %copy-start.4 = (f32[3,1,86,512]{3,1,2,0:T(1,128)S(1)}, f32[3,1,86,512]{3,1,2,0:T(1,128)}, u32[]{:S(2)}) copy-start(f32[3,1,86,512]{3,1,2,0:T(1,128)} %param.14) | copy-start | bytes 1585156
  48.2 32.9 %copy-start.5 = (f32[3,1,86,512]{3,1,2,0:T(1,128)S(1)}, f32[3,1,86,512]{3,1,2,0:T(1,128)}, u32[]{:S(2)}) copy-start(f32[3,1,86,512]{3,1,2,0:T(1,128)} %param.13) | copy-start | bytes 1585156
  48.2 12.0 %collective-permute-start.4 = (bf16[1,4,3,2,88,128]{5,4,3,2,1,0:T(8,128)(2,1)S(1)}, bf16[1,4,3,2,88,128]{5,4,3,2,1,0:T(8,128)(2,1)S(1)}, u32[]{:S(2)}, u32[]{:S(2)}) collective-permute-start(bf16[1,4,3,2,88,128]{5,4,3,2,1,0:T(8,128)(2,1)S(1)} %get-tuple-element.37), channel_id=1, source_target_pairs={{0,24},{4,12},{8,16},{12,4},{16,8},{20,28},{24,0},{28,20},{32,56},... | collective-permute-start | bytes 1622024 | tf_op jit(solution)/shard_map/ppermute | solution.py:371
  55.4 8.2 %collective-permute-start.10 = (bf16[1,3,2,88,128]{4,3,2,1,0:T(8,128)(2,1)S(1)}, bf16[1,3,2,88,128]{4,3,2,1,0:T(8,128)(2,1)S(1)}, u32[]{:S(2)}, u32[]{:S(2)}) collective-permute-start(bf16[1,3,2,88,128]{4,3,2,1,0:T(8,128)(2,1)S(1)} %get-tuple-element.47), channel_id=1, source_target_pairs={{0,24},{4,12},{8,16},{12,4},{16,8},{20,28},{24,0},{28,20},{32,56},... | collective-permute-start | bytes 405512 | tf_op jit(solution)/shard_map/ppermute | solution.py:376
  58.2 7.0 %collective-permute-start.11 = (bf16[1,3,2,88,128]{4,3,2,1,0:T(8,128)(2,1)S(1)}, bf16[1,3,2,88,128]{4,3,2,1,0:T(8,128)(2,1)S(1)}, u32[]{:S(2)}, u32[]{:S(2)}) collective-permute-start(bf16[1,3,2,88,128]{4,3,2,1,0:T(8,128)(2,1)S(1)} %get-tuple-element.48), channel_id=1, source_target_pairs={{0,8},{4,28},{8,0},{12,20},{16,24},{20,12},{24,16},{28,4},{32,40},... | collective-permute-start | bytes 405512 | tf_op jit(solution)/shard_map/ppermute | solution.py:376
  58.5 6.9 %collective-permute-start.12 = (bf16[1,3,2,88,128]{4,3,2,1,0:T(8,128)(2,1)S(1)}, bf16[1,3,2,88,128]{4,3,2,1,0:T(8,128)(2,1)S(1)}, u32[]{:S(2)}, u32[]{:S(2)}) collective-permute-start(bf16[1,3,2,88,128]{4,3,2,1,0:T(8,128)(2,1)S(1)} %get-tuple-element.49), channel_id=1, source_target_pairs={{0,16},{4,20},{8,24},{12,28},{16,0},{20,4},{24,8},{28,12},{32,48},... | collective-permute-start | bytes 405512 | tf_op jit(solution)/shard_map/ppermute | solution.py:376
  60.3 7.2 %collective-permute-start.5 = (bf16[1,3,2,88,128]{4,3,2,1,0:T(8,128)(2,1)S(1)}, bf16[1,3,2,88,128]{4,3,2,1,0:T(8,128)(2,1)S(1)}, u32[]{:S(2)}, u32[]{:S(2)}) collective-permute-start(bf16[1,3,2,88,128]{4,3,2,1,0:T(8,128)(2,1)S(1)} %get-tuple-element.39), channel_id=1, source_target_pairs={{0,96},{4,36},{8,104},{12,44},{16,112},{20,52},{24,120},{28,60},{3... | collective-permute-start | bytes 405512 | tf_op jit(solution)/shard_map/ppermute | solution.py:375
  63.6 5.0 %collective-permute-start.6 = (bf16[1,3,2,88,128]{4,3,2,1,0:T(8,128)(2,1)S(1)}, bf16[1,3,2,88,128]{4,3,2,1,0:T(8,128)(2,1)S(1)}, u32[]{:S(2)}, u32[]{:S(2)}) collective-permute-start(bf16[1,3,2,88,128]{4,3,2,1,0:T(8,128)(2,1)S(1)} %get-tuple-element.40), channel_id=1, source_target_pairs={{0,32},{4,100},{8,40},{12,108},{16,48},{20,116},{24,56},{28,124},{... | collective-permute-start | bytes 405512 | tf_op jit(solution)/shard_map/ppermute | solution.py:375
  63.6 6.5 %collective-permute-start.7 = (bf16[1,3,2,88,128]{4,3,2,1,0:T(8,128)(2,1)S(1)}, bf16[1,3,2,88,128]{4,3,2,1,0:T(8,128)(2,1)S(1)}, u32[]{:S(2)}, u32[]{:S(2)}) collective-permute-start(bf16[1,3,2,88,128]{4,3,2,1,0:T(8,128)(2,1)S(1)} %get-tuple-element.41), channel_id=1, source_target_pairs={{0,64},{4,68},{8,72},{12,76},{16,80},{20,84},{24,88},{28,92},{32,9... | collective-permute-start | bytes 405512 | tf_op jit(solution)/shard_map/ppermute | solution.py:375
  71.0 19.2 %collective-permute-start.13 = (bf16[3,88,256]{2,1,0:T(8,128)(2,1)S(1)}, bf16[3,88,256]{2,1,0:T(8,128)(2,1)S(1)}, u32[]{:S(2)}, u32[]{:S(2)}) collective-permute-start(bf16[3,88,256]{2,1,0:T(8,128)(2,1)S(1)} %get-tuple-element.52), channel_id=1, source_target_pairs={{0,4},{4,0},{8,12},{12,8},{16,20},{20,16},{24,28},{28,24},{32,36},... | collective-permute-start | bytes 405512 | tf_op jit(solution)/shard_map/ppermute | solution.py:378
  71.0 19.2 %all-to-all-start = ((f32[128,1,128]{2,1,0:T(1,128)}), f32[128,1,128]{2,1,0:T(1,128)S(1)}, u32[]{:S(2)}, u32[]{:S(2)}) async-start(f32[128,1,128]{2,1,0:T(1,128)} %bitcast.10), calls=%async_computation | async-start | bytes 131072 | tf_op jit(solution)/shard_map/all_to_all | solution.py:379
  99.1 1.4 %copy-start.1 = (bf16[32,3,88,128]{3,2,1,0:T(8,128)(2,1)}, bf16[32,3,88,128]{3,2,1,0:T(8,128)(2,1)S(1)}, u32[]{:S(2)}) copy-start(bf16[32,3,88,128]{3,2,1,0:T(8,128)(2,1)S(1)} %get-tuple-element.53) | copy-start | bytes 6488068
  100.4 34.8 %all-to-all-start.1 = ((bf16[32,3,88,128]{3,2,1,0:T(8,128)(2,1)}), bf16[32,3,88,128]{3,2,1,0:T(8,128)(2,1)S(1)}, u32[]{:S(2)}, u32[]{:S(2)}) async-start(bf16[32,3,88,128]{3,2,1,0:T(8,128)(2,1)} %copy-done.1), calls=%async_computation.1 | async-start | bytes 4325376 | tf_op jit(solution)/shard_map/all_to_all | solution.py:385

commit v5 on v4

v5 whole, which is shorter than its diff:
```python
import functools

import jax
import jax.numpy as jnp
from jax import lax
from jax.experimental import pallas as pl
from jax.experimental.pallas import tpu as pltpu
from jax.sharding import PartitionSpec as P

STEP = 10
N_Z, N_X, N_C = 4, 4, 2
N_DP = N_Z * N_X * N_C
UNITS = 86
PAD = 88
LANES = 128
BF16 = jnp.bfloat16
F32 = jnp.float32
MB = 1 << 20


def dp_index(z, x, c):
    return ((z % N_Z) * N_X + (x % N_X)) * N_C + c % N_C


def every_chip():
    return [(z, x, c) for z in range(N_Z) for x in range(N_X) for c in range(N_C)]


CORE_PAIRS = [(dp_index(z, x, c), dp_index(z, x, c + 1)) for z, x, c in every_chip()]


FLIPS = ((1, 3), (3, 1))
FLIP_ORDER = tuple((0, b, a, a ^ b) for a, b in FLIPS)


def along_x(turn):
    return [(dp_index(z, x, c), dp_index(z, x ^ FLIPS[c][turn], c)) for z, x, c in every_chip()]


def along_z(turn):
    return [(dp_index(z, x, c), dp_index(z ^ FLIPS[c][turn], x, c)) for z, x, c in every_chip()]


def direct_x(r):
    return [(dp_index(z, x, c), dp_index(z, x ^ FLIP_ORDER[c][r], c)) for z, x, c in every_chip()]


def direct_z(r):
    return [(dp_index(z, x, c), dp_index(z ^ FLIP_ORDER[c][r], x, c)) for z, x, c in every_chip()]


def my_place():
    me = lax.axis_index("dp")
    z = lax.shift_right_logical(me, 3)
    x = lax.bitwise_and(lax.shift_right_logical(me, 1), 3)
    return z, x, lax.bitwise_and(me, 1)


def my_core():
    return my_place()[2]


def turned(offset):
    return jnp.where(my_core() == 0, lax.bitwise_and(4 - offset, 3), offset)


def flip_order(r):
    return turned(lax.bitwise_xor(r, lax.shift_right_logical(r, 1)))


def rank_of(offset):
    at = turned(offset)
    return lax.bitwise_xor(at, lax.shift_right_logical(at, 1))


VMEM = pl.BlockSpec(memory_space=pltpu.VMEM)
ANY = pl.BlockSpec(memory_space=pl.ANY)


def params(mib, **more):
    return pltpu.CompilerParams(vmem_limit_bytes=mib * MB, **more)


def project_kernel(first, steps, window, x_hbm, b_hbm, kept, sent, x, b, acc, sem_a, sem_b):
    count = acc.shape[0]
    wide = x.shape[1] // steps
    half = kept.shape[2]

    def copies(k):
        at = pl.ds(k * wide, wide)
        yield pltpu.make_async_copy(x_hbm.at[:, at], x.at[:, at], sem_a.at[k])
        for m in range(count):
            yield pltpu.make_async_copy(b_hbm.at[first + m, at], b.at[m, at], sem_b.at[m, k])

    for k in range(window):
        for copy in copies(k):
            copy.start()
    for k in range(steps):
        for copy in copies(k):
            copy.wait()
        if k + window < steps:
            for copy in copies(k + window):
                copy.start()
        at = slice(k * wide, (k + 1) * wide)
        for m in range(count):
            part = jnp.dot(x[:, at], b[m, at], preferred_element_type=F32)
            if k == 0:
                acc[m] = part
            elif k < steps - 1:
                acc[m] += part
            else:
                full = (acc[m] + part).astype(BF16)
                low, high = full[:, :half], full[:, half:]
                lower = my_core() == 0
                kept[m] = jnp.where(lower, low, high)
                sent[m] = jnp.where(lower, high, low)


def project(x, bases, first, count):
    tokens, width = x.shape
    rank = bases.shape[2]
    steps = 8
    out = jax.ShapeDtypeStruct((count, tokens, rank // 2), BF16)
    return pl.pallas_call(
        functools.partial(project_kernel, first, steps, 4),
        in_specs=[ANY, ANY],
        out_specs=[VMEM] * 2,
        out_shape=[out, out],
        scratch_shapes=[
            pltpu.VMEM((tokens, width), BF16),
            pltpu.VMEM((count, width, rank), BF16),
            pltpu.VMEM((count, tokens, rank), F32),
            pltpu.SemaphoreType.DMA((steps,)),
            pltpu.SemaphoreType.DMA((count, steps)),
        ],
        compiler_params=params(58),
        cost_estimate=pl.CostEstimate(
            flops=2 * count * tokens * rank * width,
            bytes_accessed=2 * (tokens * width + count * width * rank),
            transcendentals=0,
        ),
        name="project",
    )(x, bases)


PIECES_TWO = ((("x", 0), ("x", 1)), (("x", 2), ("z", 2)))
PIECES_ONE = ((("z", 0), ("z", 1)),)


def collect_kernel(pieces, g, h, mine, theirs, *refs):
    *outs, terms, cut_x, cut_z = refs
    step = pl.program_id(0)
    _, x0, c0 = my_place()
    block = g.shape[1]

    @pl.when(step == 0)
    def _():
        terms[...] = jnp.zeros(terms.shape, F32)

    z_pieces = cut_z.shape[1]
    for m, halves in enumerate(pieces):
        terms[m, :block] = jnp.dot(g[m], mine[m], preferred_element_type=F32) + jnp.dot(
            h[m], theirs[m], preferred_element_type=F32
        )
        for x in range(N_X):
            at = rank_of(lax.bitwise_xor(x0, x))
            for c in range(N_C):
                own = lax.bitwise_xor(c0, c)
                d = (x * N_C + c) * UNITS
                both = terms[m, d : d + PAD].astype(BF16)
                for half, (flow, piece) in enumerate(halves):
                    part = both[:, half * LANES : (half + 1) * LANES]
                    if flow == "x":
                        cut_x[at, piece, own] = part
                    else:
                        cut_z[at, piece % z_pieces, own] = part
    if len(outs) == 4:
        outs[0][:, 0] = cut_x[:2]
        outs[1][:, 0] = cut_x[2:]
    za, zb = outs[-2:]

    @pl.when(step < 2)
    def _():
        za[0] = cut_z[...]

    @pl.when(step >= 2)
    def _():
        zb[0] = cut_z[...]


def collect(pieces, g, h, mine, theirs):
    count, units, tokens = g.shape
    half = mine.shape[2]
    block = units // N_Z
    array = lambda count: jax.ShapeDtypeStruct((2, 4, count, N_C, PAD, LANES), BF16)
    z_of = lambda i: lax.bitwise_xor(my_place()[0], flip_order(i))
    by_z = pl.BlockSpec((count, block, tokens), lambda i: (0, z_of(i), 0))
    whole = pl.BlockSpec((count, tokens, half), lambda i: (0, 0, 0))
    x_spec = pl.BlockSpec((2, 1, 3, N_C, PAD, LANES), lambda i: (0, i, 0, 0, 0, 0))
    z_pieces = sum(flow == "z" for halves in pieces for flow, _ in halves)
    both = len(pieces) > 1
    z_shape = (1, 4, z_pieces, N_C, PAD, LANES)
    z_specs = [
        pl.BlockSpec(z_shape, lambda i: (jnp.minimum(i, 1), 0, 0, 0, 0, 0)),
        pl.BlockSpec(z_shape, lambda i: (jnp.maximum(i - 2, 0), 0, 0, 0, 0, 0)),
    ]
    out_specs = [x_spec, x_spec, *z_specs] if both else z_specs
    out_shape = [array(3)] * 2 * both + [array(z_pieces)] * 2
    return pl.pallas_call(
        functools.partial(collect_kernel, pieces),
        grid=(N_Z,),
        in_specs=[by_z, by_z, whole, whole],
        out_specs=out_specs,
        scratch_shapes=[
            pltpu.VMEM((count, block + 8, half), F32),
            pltpu.VMEM((4, 3, N_C, PAD, LANES), BF16),
            pltpu.VMEM((4, z_pieces, N_C, PAD, LANES), BF16),
        ],
        out_shape=out_shape,
        compiler_params=params(24),
        cost_estimate=pl.CostEstimate(
            flops=2 * count * 2 * tokens * units * half,
            bytes_accessed=2 * count * units * (2 * tokens + half),
            transcendentals=0,
        ),
        name="collect",
    )(g, h, mine, theirs)


def split_kernel(count, *refs):
    outs = refs[2 * count :]
    n = refs[0].shape[0] // len(outs)
    for i, out in enumerate(outs):
        at = slice(i * n, (i + 1) * n)
        piece = 0
        for kept, recv in zip(refs[:count], refs[count : 2 * count]):
            more = kept.shape[-4]
            total = (kept[at].astype(F32) + recv[at].astype(F32)).astype(BF16)
            if count == 1:
                out[...] = total
            else:
                out[:, :, piece : piece + more] = total
            piece += more


def split_sum(kept, recv, parts):
    first = kept[0].shape
    pieces = sum(t.shape[-4] for t in kept)
    shape = (first[0] // parts, *first[1:-4], pieces, *first[-3:])
    return pl.pallas_call(
        functools.partial(split_kernel, len(kept)),
        in_specs=[VMEM] * 2 * len(kept),
        out_specs=[VMEM] * parts,
        out_shape=[jax.ShapeDtypeStruct(shape, BF16)] * parts,
        compiler_params=params(12),
        name="split_sum",
    )(*kept, *recv)


def owned_kernel(*refs):
    parts, (mine, fix, squares) = refs[:8], refs[8:]
    inside = lax.broadcasted_iota(jnp.int32, (PAD, LANES), 0) < UNITS
    total_sq = jnp.zeros((PAD, LANES), F32)
    for m, halves in enumerate(PIECES_TWO + PIECES_ONE):
        for half, (flow, piece) in enumerate(halves):
            t = parts[:4] if flow == "x" else parts[4:]
            lanes = slice(half * LANES, half * LANES + LANES)
            for c in range(N_C):
                v = t[0][0, piece, c].astype(F32) + t[1][0, piece, c].astype(F32)
                v = v + (t[2][0, piece, c].astype(F32) + t[3][0, piece, c].astype(F32))
                total_sq += jnp.where(inside, v * v, 0.0)
                if c == 0:
                    mine[m, :, lanes] = v
                else:
                    fix[m, :, lanes] = v.astype(BF16)
    row = jnp.sum(total_sq, axis=0, keepdims=True)
    squares[...] = jnp.broadcast_to(row, squares.shape)


def owned_sum(by_x, by_z, peers):
    return pl.pallas_call(
        owned_kernel,
        in_specs=[VMEM] * 8,
        out_specs=[VMEM] * 3,
        out_shape=[
            jax.ShapeDtypeStruct((3, PAD, 2 * LANES), F32),
            jax.ShapeDtypeStruct((3, PAD, 2 * LANES), BF16),
            jax.ShapeDtypeStruct((peers, LANES), F32),
        ],
        compiler_params=params(12),
        name="owned_sum",
    )(*by_x, *by_z)


def update_kernel(limit_sq, squares, mine, recv, first, second, b, new_first, new_second, out, way):
    @pl.when(pl.program_id(0) == 0)
    def _():
        total = jnp.sum(squares[...])
        clip_limit = jnp.sqrt(jnp.full((1, 1), limit_sq, F32))
        factor = jnp.minimum(1.0, clip_limit / jnp.sqrt(jnp.full((1, 1), total, F32)))
        low = my_core() == 0
        for m in range(3):
            near = mine[m]
            far = recv[m].astype(F32)
            lower = jnp.where(low, near, far)
            upper = jnp.where(low, far, near)
            clipped = jnp.concatenate([lower, upper], axis=1)[:UNITS] * factor
            one = 0.9 * first[m] + 0.1 * clipped
            two = 0.95 * second[m] + 0.05 * clipped * clipped
            new_first[m] = one
            new_second[m] = two
            turn = one / (1.0 - 0.9**STEP) / (jnp.sqrt(two / (1.0 - 0.95**STEP)) + 1e-08)
            padded = jnp.concatenate([turn, jnp.zeros((PAD - UNITS, turn.shape[1]), F32)], axis=0)
            way[m] = padded.astype(BF16)

    for m in range(3):
        full = lax.dot_general(
            way[m], b[m], (((1,), (1,)), ((), ())), preferred_element_type=F32
        ).astype(BF16)
        for n in range(out.shape[0]):
            out[n, m] = full[:, n * LANES : (n + 1) * LANES]


def update(limit_sq, squares, mine, recv, first, second, bases):
    _, width, rank = bases.shape
    steps = 4
    moment = jax.ShapeDtypeStruct((3, UNITS, rank), F32)
    whole = lambda array: pl.BlockSpec(array.shape, lambda i: (0,) * array.ndim)
    inputs = (squares, mine, recv, first, second)
    owners = width // LANES
    return pl.pallas_call(
        functools.partial(update_kernel, limit_sq),
        grid=(steps,),
        in_specs=[whole(t) for t in inputs]
        + [pl.BlockSpec((3, width // steps, rank), lambda i: (0, i, 0))],
        out_specs=[
            whole(moment),
            whole(moment),
            pl.BlockSpec((owners // steps, 3, PAD, LANES), lambda i: (i, 0, 0, 0)),
        ],
        out_shape=[moment, moment, jax.ShapeDtypeStruct((owners, 3, PAD, LANES), BF16)],
        scratch_shapes=[pltpu.VMEM((3, PAD, rank), BF16)],
        compiler_params=params(52),
        name="update",
    )(*inputs, bases)


def layout_kernel(pieces, gate, up, down, rows):
    units = N_DP * UNITS
    for m, out in enumerate((gate, up, down)):
        for k in range(N_DP):
            rows[m, k * UNITS : k * UNITS + PAD, :] = pieces[k, m].astype(F32)
        out[...] = rows[m, :units, :].astype(BF16)


def layout(pieces):
    units = N_DP * UNITS
    return pl.pallas_call(
        layout_kernel,
        in_specs=[VMEM],
        out_specs=[VMEM] * 3,
        out_shape=[jax.ShapeDtypeStruct((units, LANES), BF16)] * 3,
        scratch_shapes=[pltpu.VMEM((3, units + 8, LANES), F32)],
        compiler_params=params(24),
        name="layout",
    )(pieces)


def body(activations, gate_up_grads, hidden_act, down_out_grad, bases, first_moment, second_moment):
    devices = lax.axis_size("dp") * lax.axis_size("tensor")
    total_units = hidden_act.shape[1] * lax.axis_size("tensor")
    gate_up = jnp.swapaxes(gate_up_grads, 1, 2)
    hidden = hidden_act.T[None]
    gate_up_there = lax.ppermute(gate_up, "dp", CORE_PAIRS)
    hidden_there = lax.ppermute(hidden, "dp", CORE_PAIRS)
    kept_two, sent_two = project(activations, bases, 0, 2)
    theirs_two = lax.ppermute(sent_two, "dp", CORE_PAIRS)
    kept_one, sent_one = project(down_out_grad, bases, 2, 1)
    theirs_one = lax.ppermute(sent_one, "dp", CORE_PAIRS)
    xa, xb, za_one, zb_one = collect(PIECES_TWO, gate_up, gate_up_there, kept_two, theirs_two)
    xr = lax.ppermute(xb, "dp", along_x(0))
    zr_one = lax.ppermute(zb_one, "dp", along_z(0))
    za_two, zb_two = collect(PIECES_ONE, hidden, hidden_there, kept_one, theirs_one)
    zr_two = lax.ppermute(zb_two, "dp", along_z(0))

    xa, xb = split_sum([xa], [xr], 2)
    za_one, za_two, xb = lax.optimization_barrier((za_one, za_two, xb))
    xr = lax.ppermute(xb, "dp", along_x(1))
    za, zb = split_sum([za_two, za_one], [zr_two, zr_one], 2)
    zr = lax.ppermute(zb, "dp", along_z(1))
    by_x = split_sum([xa[0]], [xr[0]], 4)
    za, *by_x = lax.optimization_barrier((za, *by_x))
    by_z = split_sum([za[0]], [zr[0]], 4)
    by_x = [by_x[0]] + [lax.ppermute(by_x[r], "dp", direct_z(r)) for r in (1, 2, 3)]
    by_z = [by_z[0]] + [lax.ppermute(by_z[r], "dp", direct_x(r)) for r in (1, 2, 3)]
    mine, fix, squares = owned_sum(by_x, by_z, devices)
    fix = lax.ppermute(fix, "dp", CORE_PAIRS)
    squares = lax.all_to_all(squares, ("dp", "tensor"), 0, 0, tiled=True)

    limit_sq = float(3 * bases.shape[2] * total_units)
    new_first, new_second, pieces = update(
        limit_sq, squares, mine, fix, first_moment[:, 0], second_moment[:, 0], bases
    )
    pieces = lax.all_to_all(pieces, "dp", 0, 0, tiled=True)
    gate_update, up_update, down_update = layout(pieces)
    return (gate_update.T, up_update.T, down_update, new_first[:, None], new_second[:, None])


def solution(mesh):
    placed = (
        P("dp", None),
        P(None, "dp", "tensor"),
        P("dp", "tensor"),
        P("dp", None),
        P(),
        P(None, "tensor", "dp", None),
        P(None, "tensor", "dp", None),
    )
    return jax.shard_map(
        body,
        mesh=mesh,
        in_specs=placed,
        out_specs=(
            P("dp", "tensor"),
            P("dp", "tensor"),
            P("tensor", "dp"),
            P(None, "tensor", "dp", None),
            P(None, "tensor", "dp", None),
        ),
        check_vma=False,
    )
```

time: 137 us -> 134 us (0.978)
  Pallas kernels: 32 us -> 36.8 us
  local copies, waits for them, and re-layouts: 8.44 us -> 3.8 us
  waiting for transfers between devices: 60.2 us -> 57.8 us
    ppermute x2 -> x4, waiting for transfers between devices: 14.1 us -> 2.63 us  [the longest x1 2.62 us: body(): zr_one = lax.ppermute(zb_one, 'dp', along_z(0))]
    ppermute x1, waiting for transfers between devices: 0.01 us -> 7.31 us  [body(): xr = lax.ppermute(xb, 'dp', along_x(0))]
    pallas_call x7 -> x9, Pallas kernels: 29.7 us -> 34.5 us  [the longest x2 13.6 us: project(): pl.pallas_call(functools.partial(project_kernel, first, steps, 4), in_spe...]
    unnamed x19 -> x17, local copies, waits for them, and re-layouts: 7.09 us -> 3.8 us
    ppermute x1, waiting for transfers between devices: 4.22 us -> 6.5 us  [body(): zr = lax.ppermute(zb, 'dp', along_z(1))]
    all_to_all x1, starting transfers between devices: 10.1 us -> 8.06 us  [body(): squares = lax.all_to_all(squares, ('dp', 'tensor'), 0, 0, tiled=True)]
    ppermute x2 -> x4, starting transfers between devices: 2.25 us -> 2.92 us  [the longest x1 1.99 us: body(): zr_two = lax.ppermute(zb_two, 'dp', along_z(0))]
  transfers between devices with their start and end apart: 16 -> 18, of which waited for: 9 -> 8; matrix products, arithmetic and copies ran while one was open for 3% -> 3% of each run, Pallas kernels for 9% -> 19%
where the time goes in v5:
time: 134 us; the launch traced here: 133 us
  waiting for transfers between devices  57.8 us (43%)
  Pallas kernels  36.8 us (27%)
  starting transfers between devices  34 us (25%)
  local copies, waits for them, and re-layouts  3.8 us (3%)
    all_to_all x1, waiting for transfers between devices, body(): pieces = lax.all_to_all(pieces, 'dp', 0, 0, tiled=True)  28.1 us
    pallas_call x2, Pallas kernels, project(): pl.pallas_call(functools.partial(project_kernel, first, steps, 4), in_spe...  13.6 us
    pallas_call x2, Pallas kernels, collect(): pl.pallas_call(functools.partial(collect_kernel, pieces), grid=(N_Z,), in...  10.8 us
    pallas_call x1, Pallas kernels, update(): pl.pallas_call(functools.partial(update_kernel, limit_sq), grid=(steps,),...  9.36 us
    all_to_all x1, starting transfers between devices, body(): squares = lax.all_to_all(squares, ('dp', 'tensor'), 0, 0, tiled=True)  8.06 us
    all_to_all x1, waiting for transfers between devices, body(): squares = lax.all_to_all(squares, ('dp', 'tensor'), 0, 0, tiled=True)  7.96 us
    ppermute x1, waiting for transfers between devices, body(): xr = lax.ppermute(xb, 'dp', along_x(0))  7.31 us
    ppermute x1, waiting for transfers between devices, body(): zr = lax.ppermute(zb, 'dp', along_z(1))  6.5 us
  transfers between devices with their start and end apart: 18, of which 8 were waited for; matrix products, arithmetic and copies ran while one was open for 3% of the time, Pallas kernels for 19%

profile of v5, /device:TPU:0, one launch (start us, length us, event | category | flops | bytes accessed | tf_op | source)
XLA Modules:
  0.0 133.2 jit_solution(11057754879649008131)
XLA Ops:
  0.7 0.5 collective-permute-start.2
  1.2 7.7 %project.2 = (bf16[2,512,256]{2,1,0:T(8,128)(2,1)}, bf16[2,512,256]{2,1,0:T(8,128)(2,1)}) custom-call(bf16[512,4096]{1,0:T(8,128)(2,1)} %x_hbm.2, bf16[3,4096,512]{2,1,0:T(8,128)(2,1)} %b.1), custom_call_target="tpu_custom_call" | custom-call | flops 4294967296 | bytes 12582912 | tf_op jit(solution)/shard_map/project/pallas_call | solution.py:124
  9.2 5.9 %project.3 = (bf16[1,512,256]{2,1,0:T(8,128)(2,1)}, bf16[1,512,256]{2,1,0:T(8,128)(2,1)}) custom-call(bf16[512,4096]{1,0:T(8,128)(2,1)} %x_hbm.3, bf16[3,4096,512]{2,1,0:T(8,128)(2,1)} %b.1), custom_call_target="tpu_custom_call" | custom-call | flops 2147483648 | bytes 8388608 | tf_op jit(solution)/shard_map/project/pallas_call | solution.py:124
  15.1 0.6 collective-permute-start.3
  15.8 6.6 %collect.2 = (bf16[2,4,3,2,88,128]{5,4,3,2,1,0:T(8,128)(2,1)S(1)}, bf16[2,4,3,2,88,128]{5,4,3,2,1,0:T(8,128)(2,1)S(1)}, bf16[2,4,1,2,88,128]{5,4,3,2,1,0:T(8,128)(2,1)S(1)}, bf16[2,4,1,2,88,128]{5,4,3,2,1,0:T(8,128)(2,1)S(1)}) custom-call(bf16[2,2752,512]{2,1,0:T(8,128)(2,1)S(1)} %bitcast.23, bf16[2,2752,512]{2,1,0:T(8,128)(2,1)} %collective-permute-done.h, ...), custom_call_target="tpu_custom_call" | custom-call | flops 2885681152 | bytes 14090240 | tf_op jit(solution)/shard_map/collect/pallas_call | solution.py:209
  22.4 1.7 %collective-permute-start.4 = (bf16[2,4,3,2,88,128]{5,4,3,2,1,0:T(8,128)(2,1)S(1)}, bf16[2,4,3,2,88,128]{5,4,3,2,1,0:T(8,128)(2,1)S(1)}, u32[]{:S(2)}, u32[]{:S(2)}) collective-permute-start(bf16[2,4,3,2,88,128]{5,4,3,2,1,0:T(8,128)(2,1)S(1)} %get-tuple-element.51), channel_id=1, source_target_pairs={{0,8},{4,28},{8,0},{12,20},{16,24},{20,12},{24,16},{28,4},{32,40},... | collective-permute-start | bytes 3244040 | tf_op jit(solution)/shard_map/ppermute | solution.py:381
  24.1 4.1 %collect.3 = (bf16[2,4,2,2,88,128]{5,4,3,2,1,0:T(8,128)(2,1)S(1)}, bf16[2,4,2,2,88,128]{5,4,3,2,1,0:T(8,128)(2,1)S(1)}) custom-call(bf16[1,2752,512]{2,1,0:T(8,128)(2,1)S(1)} %bitcast.25, bf16[1,2752,512]{2,1,0:T(8,128)(2,1)} %collective-permute-done.2.h, bf16[1,512,256]{2,1,0:T(8,128)(2,1)S(1)} %copy-done.2, ...), custom_call_target="tpu_custom_call" | custom-call | flops 1442840576 | bytes 7045120 | tf_op jit(solution)/shard_map/collect/pallas_call | solution.py:209
  28.2 2.0 %collective-permute-start.5 = (bf16[2,4,2,2,88,128]{5,4,3,2,1,0:T(8,128)(2,1)S(1)}, bf16[2,4,2,2,88,128]{5,4,3,2,1,0:T(8,128)(2,1)S(1)}, u32[]{:S(2)}, u32[]{:S(2)}) collective-permute-start(bf16[2,4,2,2,88,128]{5,4,3,2,1,0:T(8,128)(2,1)S(1)} %get-tuple-element.55), channel_id=1, source_target_pairs={{0,32},{4,100},{8,40},{12,108},{16,48},{20,116},{24,56},{28,124},{... | collective-permute-start | bytes 2162696 | tf_op jit(solution)/shard_map/ppermute | solution.py:384
  30.3 7.3 %collective-permute-done.4.refs_1_ = bf16[2,4,3,2,88,128]{5,4,3,2,1,0:T(8,128)(2,1)S(1)} collective-permute-done((bf16[2,4,3,2,88,128]{5,4,3,2,1,0:T(8,128)(2,1)S(1)}, bf16[2,4,3,2,88,128]{5,4,3,2,1,0:T(8,128)(2,1)S(1)}, u32[]{:S(2)}, u32[]{:S(2)}) %collective-permute-start.4) | collective-permute-done | bytes 1081376 | tf_op jit(solution)/shard_map/ppermute | solution.py:381
  37.9 2.9 %collective-permute-start.7 = (bf16[1,4,3,2,88,128]{5,4,3,2,1,0:T(8,128)(2,1)S(1)}, bf16[1,4,3,2,88,128]{5,4,3,2,1,0:T(8,128)(2,1)S(1)}, u32[]{:S(2)}, u32[]{:S(2)}) collective-permute-start(bf16[1,4,3,2,88,128]{5,4,3,2,1,0:T(8,128)(2,1)S(1)} %get-tuple-element.59), channel_id=1, source_target_pairs={{0,24},{4,12},{8,16},{12,4},{16,8},{20,28},{24,0},{28,20},{32,56},... | collective-permute-start | bytes 1622024 | tf_op jit(solution)/shard_map/ppermute | solution.py:388
  40.8 2.6 %collective-permute-done.6.refs_3_ = bf16[2,4,1,2,88,128]{5,4,3,2,1,0:T(8,128)(2,1)S(1)} collective-permute-done((bf16[2,4,1,2,88,128]{5,4,3,2,1,0:T(8,128)(2,1)S(1)}, bf16[2,4,1,2,88,128]{5,4,3,2,1,0:T(8,128)(2,1)S(1)}, u32[]{:S(2)}, u32[]{:S(2)}) %collective-permute-start.6) | collective-permute-done | bytes 360480 | tf_op jit(solution)/shard_map/ppermute | solution.py:382
  43.7 4.1 %collective-permute-start.11 = (bf16[1,4,3,2,88,128]{5,4,3,2,1,0:T(8,128)(2,1)S(1)}, bf16[1,4,3,2,88,128]{5,4,3,2,1,0:T(8,128)(2,1)S(1)}, u32[]{:S(2)}, u32[]{:S(2)}) collective-permute-start(bf16[1,4,3,2,88,128]{5,4,3,2,1,0:T(8,128)(2,1)S(1)} %get-tuple-element.69), channel_id=1, source_target_pairs={{0,96},{4,36},{8,104},{12,44},{16,112},{20,52},{24,120},{28,60},{3... | collective-permute-start | bytes 1622024 | tf_op jit(solution)/shard_map/ppermute | solution.py:390
  47.9 0.7 collective-permute-done.7
  48.7 6.5 %collective-permute-done.11 = bf16[1,4,3,2,88,128]{5,4,3,2,1,0:T(8,128)(2,1)S(1)} collective-permute-done((bf16[1,4,3,2,88,128]{5,4,3,2,1,0:T(8,128)(2,1)S(1)}, bf16[1,4,3,2,88,128]{5,4,3,2,1,0:T(8,128)(2,1)S(1)}, u32[]{:S(2)}, u32[]{:S(2)}) %collective-permute-start.11) | collective-permute-done | bytes 540704 | tf_op jit(solution)/shard_map/ppermute | solution.py:390
  55.3 2.2 %collective-permute-start.12 = (bf16[1,3,2,88,128]{4,3,2,1,0:T(8,128)(2,1)S(1)}, bf16[1,3,2,88,128]{4,3,2,1,0:T(8,128)(2,1)S(1)}, u32[]{:S(2)}, u32[]{:S(2)}) collective-permute-start(bf16[1,3,2,88,128]{4,3,2,1,0:T(8,128)(2,1)S(1)} %get-tuple-element.71), channel_id=1, source_target_pairs={{0,24},{4,12},{8,16},{12,4},{16,8},{20,28},{24,0},{28,20},{32,56},... | collective-permute-start | bytes 405512 | tf_op jit(solution)/shard_map/ppermute | solution.py:395
  57.5 0.6 collective-permute-start.13
  58.1 2.0 %collective-permute-start.14 = (bf16[1,3,2,88,128]{4,3,2,1,0:T(8,128)(2,1)S(1)}, bf16[1,3,2,88,128]{4,3,2,1,0:T(8,128)(2,1)S(1)}, u32[]{:S(2)}, u32[]{:S(2)}) collective-permute-start(bf16[1,3,2,88,128]{4,3,2,1,0:T(8,128)(2,1)S(1)} %get-tuple-element.73), channel_id=1, source_target_pairs={{0,16},{4,20},{8,24},{12,28},{16,0},{20,4},{24,8},{28,12},{32,48},... | collective-permute-start | bytes 405512 | tf_op jit(solution)/shard_map/ppermute | solution.py:395
  60.1 1.9 %collective-permute-start.10 = (bf16[1,3,2,88,128]{4,3,2,1,0:T(8,128)(2,1)S(1)}, bf16[1,3,2,88,128]{4,3,2,1,0:T(8,128)(2,1)S(1)}, u32[]{:S(2)}, u32[]{:S(2)}) collective-permute-start(bf16[1,3,2,88,128]{4,3,2,1,0:T(8,128)(2,1)S(1)} %get-tuple-element.67), channel_id=1, source_target_pairs={{0,64},{4,68},{8,72},{12,76},{16,80},{20,84},{24,88},{28,92},{32,9... | collective-permute-start | bytes 405512 | tf_op jit(solution)/shard_map/ppermute | solution.py:394
  62.0 1.4 %collective-permute-start.8 = (bf16[1,3,2,88,128]{4,3,2,1,0:T(8,128)(2,1)S(1)}, bf16[1,3,2,88,128]{4,3,2,1,0:T(8,128)(2,1)S(1)}, u32[]{:S(2)}, u32[]{:S(2)}) collective-permute-start(bf16[1,3,2,88,128]{4,3,2,1,0:T(8,128)(2,1)S(1)} %get-tuple-element.65), channel_id=1, source_target_pairs={{0,96},{4,36},{8,104},{12,44},{16,112},{20,52},{24,120},{28,60},{3... | collective-permute-start | bytes 405512 | tf_op jit(solution)/shard_map/ppermute | solution.py:394
  63.3 1.6 %collective-permute-start.9 = (bf16[1,3,2,88,128]{4,3,2,1,0:T(8,128)(2,1)S(1)}, bf16[1,3,2,88,128]{4,3,2,1,0:T(8,128)(2,1)S(1)}, u32[]{:S(2)}, u32[]{:S(2)}) collective-permute-start(bf16[1,3,2,88,128]{4,3,2,1,0:T(8,128)(2,1)S(1)} %get-tuple-element.66), channel_id=1, source_target_pairs={{0,32},{4,100},{8,40},{12,108},{16,48},{20,116},{24,56},{28,124},{... | collective-permute-start | bytes 405512 | tf_op jit(solution)/shard_map/ppermute | solution.py:394
  65.0 1.8 %collective-permute-done.10.refs_3_ = bf16[1,3,2,88,128]{4,3,2,1,0:T(8,128)(2,1)S(1)} collective-permute-done((bf16[1,3,2,88,128]{4,3,2,1,0:T(8,128)(2,1)S(1)}, bf16[1,3,2,88,128]{4,3,2,1,0:T(8,128)(2,1)S(1)}, u32[]{:S(2)}, u32[]{:S(2)}) %collective-permute-start.10) | collective-permute-done | bytes 135200 | tf_op jit(solution)/shard_map/ppermute | solution.py:394
  66.8 2.8 %collective-permute-done.8.refs_1_ = bf16[1,3,2,88,128]{4,3,2,1,0:T(8,128)(2,1)S(1)} collective-permute-done((bf16[1,3,2,88,128]{4,3,2,1,0:T(8,128)(2,1)S(1)}, bf16[1,3,2,88,128]{4,3,2,1,0:T(8,128)(2,1)S(1)}, u32[]{:S(2)}, u32[]{:S(2)}) %collective-permute-start.8) | collective-permute-done | bytes 135200 | tf_op jit(solution)/shard_map/ppermute | solution.py:394
  69.6 0.8 owned_sum.1
  70.4 8.1 %all-to-all-start = ((f32[128,1,128]{2,1,0:T(1,128)}), f32[128,1,128]{2,1,0:T(1,128)S(1)}, u32[]{:S(2)}, u32[]{:S(2)}) async-start(f32[128,1,128]{2,1,0:T(1,128)} %bitcast.9), calls=%async_computation | async-start | bytes 131072 | tf_op jit(solution)/shard_map/all_to_all | solution.py:398
  78.5 1.1 copy_bitcast_fusion
  79.6 8.0 %all-to-all-done = f32[128,1,128]{2,1,0:T(1,128)S(1)} async-done(((f32[128,1,128]{2,1,0:T(1,128)}), f32[128,1,128]{2,1,0:T(1,128)S(1)}, u32[]{:S(2)}, u32[]{:S(2)}) %all-to-all-start) | async-done | bytes 65568 | tf_op jit(solution)/shard_map/all_to_all | solution.py:398
  87.6 9.4 %update.1 = (f32[3,86,512]{2,1,0:T(8,128)S(1)}, f32[3,86,512]{2,1,0:T(8,128)S(1)}, bf16[32,3,88,128]{3,2,1,0:T(8,128)(2,1)}) custom-call(f32[128,128]{1,0:T(8,128)S(1)} %bitcast.32, f32[3,88,256]{2,1,0:T(8,128)S(1)} %get-tuple-element.75.mine, bf16[3,88,256]{2,1,0:T(8,128)(2,1)S(1)} %collective-permute-done.15.recv, f32[3,86,512]{2,1,0:T(8,128)} %get-tuple-element.94.first, ...), custom_call_target="tpu_custom_call" | custom-call | tf_op jit(solution)/shard_map/update/pallas_call | solution.py:331
  96.9 4.1 %all-to-all-start.1 = ((bf16[32,3,88,128]{3,2,1,0:T(8,128)(2,1)}), bf16[32,3,88,128]{3,2,1,0:T(8,128)(2,1)S(1)}, u32[]{:S(2)}, u32[]{:S(2)}) async-start(bf16[32,3,88,128]{3,2,1,0:T(8,128)(2,1)} %get-tuple-element.77), calls=%async_computation.1 | async-start | bytes 4325376 | tf_op jit(solution)/shard_map/all_to_all | solution.py:404
  101.0 1.3 %copy.15 = f32[3,1,86,512]{3,1,2,0:T(1,128)} copy(f32[3,1,86,512]{3,2,0,1:T(8,128)S(1)} %bitcast.31) | data formatting | bytes 1056768
  102.3 1.3 %copy.16 = f32[3,1,86,512]{3,1,2,0:T(1,128)} copy(f32[3,1,86,512]{3,2,0,1:T(8,128)S(1)} %bitcast.30) | data formatting | bytes 1056768
  103.7 28.1 %all-to-all-done.1.pieces = bf16[32,3,88,128]{3,2,1,0:T(8,128)(2,1)S(1)} async-done(((bf16[32,3,88,128]{3,2,1,0:T(8,128)(2,1)}), bf16[32,3,88,128]{3,2,1,0:T(8,128)(2,1)S(1)}, u32[]{:S(2)}, u32[]{:S(2)}) %all-to-all-start.1) | async-done | bytes 2162720 | tf_op jit(solution)/shard_map/all_to_all | solution.py:404
  131.7 1.5 %layout.1 = (bf16[2752,128]{1,0:T(8,128)(2,1)}, bf16[2752,128]{1,0:T(8,128)(2,1)}, bf16[2752,128]{1,0:T(8,128)(2,1)}) custom-call(bf16[32,3,88,128]{3,2,1,0:T(8,128)(2,1)S(1)} %all-to-all-done.1.pieces), custom_call_target="tpu_custom_call" | custom-call | tf_op jit(solution)/shard_map/layout/pallas_call | solution.py:358
  (33 shorter events, 1.2 us)
Async XLA Ops:
  0.6 15.1 %collective-permute-start = (bf16[2,2752,512]{2,1,0:T(8,128)(2,1)}, bf16[2,2752,512]{2,1,0:T(8,128)(2,1)}, u32[]{:S(2)}, u32[]{:S(2)}) collective-permute-start(bf16[2,2752,512]{2,1,0:T(8,128)(2,1)} %bitcast.20), channel_id=1, source_target_pairs={{0,4},{4,0},{8,12},{12,8},{16,20},{20,16},{24,28},{28,24},{32,36},... | collective-permute-start | bytes 16908296 | tf_op jit(solution)/shard_map/ppermute | solution.py:374
  0.7 23.4 %collective-permute-start.2 = (bf16[1,2752,512]{2,1,0:T(8,128)(2,1)}, bf16[1,2752,512]{2,1,0:T(8,128)(2,1)}, u32[]{:S(2)}, u32[]{:S(2)}) collective-permute-start(bf16[1,2752,512]{2,1,0:T(8,128)(2,1)} %bitcast.24), channel_id=1, source_target_pairs={{0,4},{4,0},{8,12},{12,8},{16,20},{20,16},{24,28},{28,24},{32,36},... | collective-permute-start | bytes 8454152 | tf_op jit(solution)/shard_map/ppermute | solution.py:375
  9.0 6.7 %slice-start = ((s8[5636096]{0:T(1024)(128)(4,1)}), s8[4194304]{0:T(1024)(128)(4,1)S(1)}, s32[]{:S(2)}) async-start(s8[5636096]{0:T(1024)(128)(4,1)} %bitcast.21), calls=%async_computation.2 | async-start | bytes 8388608
  9.0 6.7 %slice-start.1 = ((s8[5636096]{0:T(1024)(128)(4,1)}), s8[1441792]{0:T(1024)(128)(4,1)S(1)}, s32[]{:S(2)}) async-start(s8[5636096]{0:T(1024)(128)(4,1)} %bitcast.21), calls=%async_computation.3 | async-start | bytes 2883584
  9.0 6.7 %copy-start.1 = (bf16[2,512,256]{2,1,0:T(8,128)(2,1)S(1)}, bf16[2,512,256]{2,1,0:T(8,128)(2,1)}, u32[]{:S(2)}) copy-start(bf16[2,512,256]{2,1,0:T(8,128)(2,1)} %get-tuple-element.44.mine) | copy-start | bytes 1572868
  9.0 6.7 %collective-permute-start.1 = (bf16[2,512,256]{2,1,0:T(8,128)(2,1)}, bf16[2,512,256]{2,1,0:T(8,128)(2,1)}, u32[]{:S(2)}, u32[]{:S(2)}) collective-permute-start(bf16[2,512,256]{2,1,0:T(8,128)(2,1)} %get-tuple-element.45), channel_id=1, source_target_pairs={{0,4},{4,0},{8,12},{12,8},{16,20},{20,16},{24,28},{28,24},{32,36},... | collective-permute-start | bytes 1572872 | tf_op jit(solution)/shard_map/ppermute | solution.py:377
  15.1 9.0 %collective-permute-start.3 = (bf16[1,512,256]{2,1,0:T(8,128)(2,1)}, bf16[1,512,256]{2,1,0:T(8,128)(2,1)S(1)}, u32[]{:S(2)}, u32[]{:S(2)}) collective-permute-start(bf16[1,512,256]{2,1,0:T(8,128)(2,1)} %get-tuple-element.48), channel_id=1, source_target_pairs={{0,4},{4,0},{8,12},{12,8},{16,20},{20,16},{24,28},{28,24},{32,36},... | collective-permute-start | bytes 786440 | tf_op jit(solution)/shard_map/ppermute | solution.py:379
  15.7 8.3 %copy-start = (bf16[512,2752]{0,1:T(8,128)(2,1)S(1)}, bf16[512,2752]{0,1:T(8,128)(2,1)}, u32[]{:S(2)}) copy-start(bf16[512,2752]{0,1:T(8,128)(2,1)} %param.9) | copy-start | bytes 8454148
  15.8 8.3 %copy-start.2 = (bf16[1,512,256]{2,1,0:T(8,128)(2,1)S(1)}, bf16[1,512,256]{2,1,0:T(8,128)(2,1)}, u32[]{:S(2)}) copy-start(bf16[1,512,256]{2,1,0:T(8,128)(2,1)} %get-tuple-element.47.mine) | copy-start | bytes 786436
  22.4 15.2 %collective-permute-start.4 = (bf16[2,4,3,2,88,128]{5,4,3,2,1,0:T(8,128)(2,1)S(1)}, bf16[2,4,3,2,88,128]{5,4,3,2,1,0:T(8,128)(2,1)S(1)}, u32[]{:S(2)}, u32[]{:S(2)}) collective-permute-start(bf16[2,4,3,2,88,128]{5,4,3,2,1,0:T(8,128)(2,1)S(1)} %get-tuple-element.51), channel_id=1, source_target_pairs={{0,8},{4,28},{8,0},{12,20},{16,24},{20,12},{24,16},{28,4},{32,40},... | collective-permute-start | bytes 3244040 | tf_op jit(solution)/shard_map/ppermute | solution.py:381
  28.2 12.6 %collective-permute-start.5 = (bf16[2,4,2,2,88,128]{5,4,3,2,1,0:T(8,128)(2,1)S(1)}, bf16[2,4,2,2,88,128]{5,4,3,2,1,0:T(8,128)(2,1)S(1)}, u32[]{:S(2)}, u32[]{:S(2)}) collective-permute-start(bf16[2,4,2,2,88,128]{5,4,3,2,1,0:T(8,128)(2,1)S(1)} %get-tuple-element.55), channel_id=1, source_target_pairs={{0,32},{4,100},{8,40},{12,108},{16,48},{20,116},{24,56},{28,124},{... | collective-permute-start | bytes 2162696 | tf_op jit(solution)/shard_map/ppermute | solution.py:384
  30.2 13.2 %collective-permute-start.6 = (bf16[2,4,1,2,88,128]{5,4,3,2,1,0:T(8,128)(2,1)S(1)}, bf16[2,4,1,2,88,128]{5,4,3,2,1,0:T(8,128)(2,1)S(1)}, u32[]{:S(2)}, u32[]{:S(2)}) collective-permute-start(bf16[2,4,1,2,88,128]{5,4,3,2,1,0:T(8,128)(2,1)S(1)} %get-tuple-element.56), channel_id=1, source_target_pairs={{0,32},{4,100},{8,40},{12,108},{16,48},{20,116},{24,56},{28,124},{... | collective-permute-start | bytes 1081352 | tf_op jit(solution)/shard_map/ppermute | solution.py:382
  37.9 40.6 %copy-start.3 = (f32[3,1,86,512]{3,1,2,0:T(1,128)S(1)}, f32[3,1,86,512]{3,1,2,0:T(1,128)}, u32[]{:S(2)}) copy-start(f32[3,1,86,512]{3,1,2,0:T(1,128)} %param.13) | copy-start | bytes 1585156
  37.9 40.6 %copy-start.4 = (f32[3,1,86,512]{3,1,2,0:T(1,128)S(1)}, f32[3,1,86,512]{3,1,2,0:T(1,128)}, u32[]{:S(2)}) copy-start(f32[3,1,86,512]{3,1,2,0:T(1,128)} %param.12) | copy-start | bytes 1585156
  37.9 10.6 %collective-permute-start.7 = (bf16[1,4,3,2,88,128]{5,4,3,2,1,0:T(8,128)(2,1)S(1)}, bf16[1,4,3,2,88,128]{5,4,3,2,1,0:T(8,128)(2,1)S(1)}, u32[]{:S(2)}, u32[]{:S(2)}) collective-permute-start(bf16[1,4,3,2,88,128]{5,4,3,2,1,0:T(8,128)(2,1)S(1)} %get-tuple-element.59), channel_id=1, source_target_pairs={{0,24},{4,12},{8,16},{12,4},{16,8},{20,28},{24,0},{28,20},{32,56},... | collective-permute-start | bytes 1622024 | tf_op jit(solution)/shard_map/ppermute | solution.py:388
  43.7 11.5 %collective-permute-start.11 = (bf16[1,4,3,2,88,128]{5,4,3,2,1,0:T(8,128)(2,1)S(1)}, bf16[1,4,3,2,88,128]{5,4,3,2,1,0:T(8,128)(2,1)S(1)}, u32[]{:S(2)}, u32[]{:S(2)}) collective-permute-start(bf16[1,4,3,2,88,128]{5,4,3,2,1,0:T(8,128)(2,1)S(1)} %get-tuple-element.69), channel_id=1, source_target_pairs={{0,96},{4,36},{8,104},{12,44},{16,112},{20,52},{24,120},{28,60},{3... | collective-permute-start | bytes 1622024 | tf_op jit(solution)/shard_map/ppermute | solution.py:390
  55.3 8.0 %collective-permute-start.12 = (bf16[1,3,2,88,128]{4,3,2,1,0:T(8,128)(2,1)S(1)}, bf16[1,3,2,88,128]{4,3,2,1,0:T(8,128)(2,1)S(1)}, u32[]{:S(2)}, u32[]{:S(2)}) collective-permute-start(bf16[1,3,2,88,128]{4,3,2,1,0:T(8,128)(2,1)S(1)} %get-tuple-element.71), channel_id=1, source_target_pairs={{0,24},{4,12},{8,16},{12,4},{16,8},{20,28},{24,0},{28,20},{32,56},... | collective-permute-start | bytes 405512 | tf_op jit(solution)/shard_map/ppermute | solution.py:395
  57.5 7.5 %collective-permute-start.13 = (bf16[1,3,2,88,128]{4,3,2,1,0:T(8,128)(2,1)S(1)}, bf16[1,3,2,88,128]{4,3,2,1,0:T(8,128)(2,1)S(1)}, u32[]{:S(2)}, u32[]{:S(2)}) collective-permute-start(bf16[1,3,2,88,128]{4,3,2,1,0:T(8,128)(2,1)S(1)} %get-tuple-element.72), channel_id=1, source_target_pairs={{0,8},{4,28},{8,0},{12,20},{16,24},{20,12},{24,16},{28,4},{32,40},... | collective-permute-start | bytes 405512 | tf_op jit(solution)/shard_map/ppermute | solution.py:395
  58.1 6.9 %collective-permute-start.14 = (bf16[1,3,2,88,128]{4,3,2,1,0:T(8,128)(2,1)S(1)}, bf16[1,3,2,88,128]{4,3,2,1,0:T(8,128)(2,1)S(1)}, u32[]{:S(2)}, u32[]{:S(2)}) collective-permute-start(bf16[1,3,2,88,128]{4,3,2,1,0:T(8,128)(2,1)S(1)} %get-tuple-element.73), channel_id=1, source_target_pairs={{0,16},{4,20},{8,24},{12,28},{16,0},{20,4},{24,8},{28,12},{32,48},... | collective-permute-start | bytes 405512 | tf_op jit(solution)/shard_map/ppermute | solution.py:395
  60.1 6.7 %collective-permute-start.10 = (bf16[1,3,2,88,128]{4,3,2,1,0:T(8,128)(2,1)S(1)}, bf16[1,3,2,88,128]{4,3,2,1,0:T(8,128)(2,1)S(1)}, u32[]{:S(2)}, u32[]{:S(2)}) collective-permute-start(bf16[1,3,2,88,128]{4,3,2,1,0:T(8,128)(2,1)S(1)} %get-tuple-element.67), channel_id=1, source_target_pairs={{0,64},{4,68},{8,72},{12,76},{16,80},{20,84},{24,88},{28,92},{32,9... | collective-permute-start | bytes 405512 | tf_op jit(solution)/shard_map/ppermute | solution.py:394
  62.0 7.6 %collective-permute-start.8 = (bf16[1,3,2,88,128]{4,3,2,1,0:T(8,128)(2,1)S(1)}, bf16[1,3,2,88,128]{4,3,2,1,0:T(8,128)(2,1)S(1)}, u32[]{:S(2)}, u32[]{:S(2)}) collective-permute-start(bf16[1,3,2,88,128]{4,3,2,1,0:T(8,128)(2,1)S(1)} %get-tuple-element.65), channel_id=1, source_target_pairs={{0,96},{4,36},{8,104},{12,44},{16,112},{20,52},{24,120},{28,60},{3... | collective-permute-start | bytes 405512 | tf_op jit(solution)/shard_map/ppermute | solution.py:394
  63.3 6.2 %collective-permute-start.9 = (bf16[1,3,2,88,128]{4,3,2,1,0:T(8,128)(2,1)S(1)}, bf16[1,3,2,88,128]{4,3,2,1,0:T(8,128)(2,1)S(1)}, u32[]{:S(2)}, u32[]{:S(2)}) collective-permute-start(bf16[1,3,2,88,128]{4,3,2,1,0:T(8,128)(2,1)S(1)} %get-tuple-element.66), channel_id=1, source_target_pairs={{0,32},{4,100},{8,40},{12,108},{16,48},{20,116},{24,56},{28,124},{... | collective-permute-start | bytes 405512 | tf_op jit(solution)/shard_map/ppermute | solution.py:394
  70.4 17.1 %collective-permute-start.15 = (bf16[3,88,256]{2,1,0:T(8,128)(2,1)S(1)}, bf16[3,88,256]{2,1,0:T(8,128)(2,1)S(1)}, u32[]{:S(2)}, u32[]{:S(2)}) collective-permute-start(bf16[3,88,256]{2,1,0:T(8,128)(2,1)S(1)} %get-tuple-element.76), channel_id=1, source_target_pairs={{0,4},{4,0},{8,12},{12,8},{16,20},{20,16},{24,28},{28,24},{32,36},... | collective-permute-start | bytes 405512 | tf_op jit(solution)/shard_map/ppermute | solution.py:397
  70.4 17.1 %all-to-all-start = ((f32[128,1,128]{2,1,0:T(1,128)}), f32[128,1,128]{2,1,0:T(1,128)S(1)}, u32[]{:S(2)}, u32[]{:S(2)}) async-start(f32[128,1,128]{2,1,0:T(1,128)} %bitcast.9), calls=%async_computation | async-start | bytes 131072 | tf_op jit(solution)/shard_map/all_to_all | solution.py:398
  96.9 34.8 %all-to-all-start.1 = ((bf16[32,3,88,128]{3,2,1,0:T(8,128)(2,1)}), bf16[32,3,88,128]{3,2,1,0:T(8,128)(2,1)S(1)}, u32[]{:S(2)}, u32[]{:S(2)}) async-start(bf16[32,3,88,128]{3,2,1,0:T(8,128)(2,1)} %get-tuple-element.77), calls=%async_computation.1 | async-start | bytes 4325376 | tf_op jit(solution)/shard_map/all_to_all | solution.py:404

commit v6 on v5

--- a/solution.py
+++ b/solution.py
@@ -122,7 +122,7 @@
     steps = 8
     out = jax.ShapeDtypeStruct((count, tokens, rank // 2), BF16)
     return pl.pallas_call(
-        functools.partial(project_kernel, first, steps, 4),
+        functools.partial(project_kernel, first, steps, 8),
         in_specs=[ANY, ANY],
         out_specs=[VMEM] * 2,
         out_shape=[out, out],
@@ -143,12 +143,7 @@
     )(x, bases)
 
 
-PIECES_TWO = ((("x", 0), ("x", 1)), (("x", 2), ("z", 2)))
-PIECES_ONE = ((("z", 0), ("z", 1)),)
-
-
-def collect_kernel(pieces, g, h, mine, theirs, *refs):
-    *outs, terms, cut_x, cut_z = refs
+def collect_kernel(x_first, g, h, mine, theirs, stay, go, terms, cut):
     step = pl.program_id(0)
     _, x0, c0 = my_place()
     block = g.shape[1]
@@ -157,8 +152,7 @@
     def _():
         terms[...] = jnp.zeros(terms.shape, F32)
 
-    z_pieces = cut_z.shape[1]
-    for m, halves in enumerate(pieces):
+    for m in range(g.shape[0]):
         terms[m, :block] = jnp.dot(g[m], mine[m], preferred_element_type=F32) + jnp.dot(
             h[m], theirs[m], preferred_element_type=F32
         )
@@ -168,55 +162,49 @@
                 own = lax.bitwise_xor(c0, c)
                 d = (x * N_C + c) * UNITS
                 both = terms[m, d : d + PAD].astype(BF16)
-                for half, (flow, piece) in enumerate(halves):
-                    part = both[:, half * LANES : (half + 1) * LANES]
-                    if flow == "x":
-                        cut_x[at, piece, own] = part
-                    else:
-                        cut_z[at, piece % z_pieces, own] = part
-    if len(outs) == 4:
-        outs[0][:, 0] = cut_x[:2]
-        outs[1][:, 0] = cut_x[2:]
-    za, zb = outs[-2:]
+                cut[at, 2 * m, own] = both[:, :LANES]
+                cut[at, 2 * m + 1, own] = both[:, LANES:]
+    if x_first:
+        stay[:, 0] = cut[:2]
+        go[:, 0] = cut[2:]
+        return
 
     @pl.when(step < 2)
     def _():
-        za[0] = cut_z[...]
+        stay[0] = cut[...]
 
     @pl.when(step >= 2)
     def _():
-        zb[0] = cut_z[...]
-
-
-def collect(pieces, g, h, mine, theirs):
+        go[0] = cut[...]
+
+
+def collect(x_first, g, h, mine, theirs):
     count, units, tokens = g.shape
     half = mine.shape[2]
     block = units // N_Z
-    array = lambda count: jax.ShapeDtypeStruct((2, 4, count, N_C, PAD, LANES), BF16)
+    pieces = 2 * count
+    array = jax.ShapeDtypeStruct((2, 4, pieces, N_C, PAD, LANES), BF16)
     z_of = lambda i: lax.bitwise_xor(my_place()[0], flip_order(i))
     by_z = pl.BlockSpec((count, block, tokens), lambda i: (0, z_of(i), 0))
     whole = pl.BlockSpec((count, tokens, half), lambda i: (0, 0, 0))
-    x_spec = pl.BlockSpec((2, 1, 3, N_C, PAD, LANES), lambda i: (0, i, 0, 0, 0, 0))
-    z_pieces = sum(flow == "z" for halves in pieces for flow, _ in halves)
-    both = len(pieces) > 1
-    z_shape = (1, 4, z_pieces, N_C, PAD, LANES)
-    z_specs = [
-        pl.BlockSpec(z_shape, lambda i: (jnp.minimum(i, 1), 0, 0, 0, 0, 0)),
-        pl.BlockSpec(z_shape, lambda i: (jnp.maximum(i - 2, 0), 0, 0, 0, 0, 0)),
-    ]
-    out_specs = [x_spec, x_spec, *z_specs] if both else z_specs
-    out_shape = [array(3)] * 2 * both + [array(z_pieces)] * 2
-    return pl.pallas_call(
-        functools.partial(collect_kernel, pieces),
+    if x_first:
+        out_specs = [pl.BlockSpec((2, 1, pieces, N_C, PAD, LANES), lambda i: (0, i, 0, 0, 0, 0))] * 2
+    else:
+        shape = (1, 4, pieces, N_C, PAD, LANES)
+        out_specs = [
+            pl.BlockSpec(shape, lambda i: (jnp.minimum(i, 1), 0, 0, 0, 0, 0)),
+            pl.BlockSpec(shape, lambda i: (jnp.maximum(i - 2, 0), 0, 0, 0, 0, 0)),
+        ]
+    return pl.pallas_call(
+        functools.partial(collect_kernel, x_first),
         grid=(N_Z,),
         in_specs=[by_z, by_z, whole, whole],
         out_specs=out_specs,
         scratch_shapes=[
             pltpu.VMEM((count, block + 8, half), F32),
-            pltpu.VMEM((4, 3, N_C, PAD, LANES), BF16),
-            pltpu.VMEM((4, z_pieces, N_C, PAD, LANES), BF16),
+            pltpu.VMEM((4, pieces, N_C, PAD, LANES), BF16),
         ],
-        out_shape=out_shape,
+        out_shape=[array] * 2,
         compiler_params=params(24),
         cost_estimate=pl.CostEstimate(
             flops=2 * count * 2 * tokens * units * half,
@@ -227,43 +215,32 @@
     )(g, h, mine, theirs)
 
 
-def split_kernel(count, *refs):
-    outs = refs[2 * count :]
-    n = refs[0].shape[0] // len(outs)
+def split_kernel(kept, recv, *outs):
+    n = kept.shape[0] // len(outs)
     for i, out in enumerate(outs):
         at = slice(i * n, (i + 1) * n)
-        piece = 0
-        for kept, recv in zip(refs[:count], refs[count : 2 * count]):
-            more = kept.shape[-4]
-            total = (kept[at].astype(F32) + recv[at].astype(F32)).astype(BF16)
-            if count == 1:
-                out[...] = total
-            else:
-                out[:, :, piece : piece + more] = total
-            piece += more
+        out[...] = (kept[at].astype(F32) + recv[at].astype(F32)).astype(BF16)
 
 
 def split_sum(kept, recv, parts):
-    first = kept[0].shape
-    pieces = sum(t.shape[-4] for t in kept)
-    shape = (first[0] // parts, *first[1:-4], pieces, *first[-3:])
-    return pl.pallas_call(
-        functools.partial(split_kernel, len(kept)),
-        in_specs=[VMEM] * 2 * len(kept),
+    shape = (kept.shape[0] // parts, *kept.shape[1:])
+    return pl.pallas_call(
+        split_kernel,
+        in_specs=[VMEM] * 2,
         out_specs=[VMEM] * parts,
         out_shape=[jax.ShapeDtypeStruct(shape, BF16)] * parts,
         compiler_params=params(12),
         name="split_sum",
-    )(*kept, *recv)
+    )(kept, recv)
 
 
 def owned_kernel(*refs):
     parts, (mine, fix, squares) = refs[:8], refs[8:]
     inside = lax.broadcasted_iota(jnp.int32, (PAD, LANES), 0) < UNITS
     total_sq = jnp.zeros((PAD, LANES), F32)
-    for m, halves in enumerate(PIECES_TWO + PIECES_ONE):
-        for half, (flow, piece) in enumerate(halves):
-            t = parts[:4] if flow == "x" else parts[4:]
+    for m in range(3):
+        for half in range(2):
+            t, piece = (parts[:4], 2 * m + half) if m < 2 else (parts[4:], half)
             lanes = slice(half * LANES, half * LANES + LANES)
             for c in range(N_C):
                 v = t[0][0, piece, c].astype(F32) + t[1][0, piece, c].astype(F32)
@@ -292,9 +269,19 @@
     )(*by_x, *by_z)
 
 
-def update_kernel(limit_sq, squares, mine, recv, first, second, b, new_first, new_second, out, way):
-    @pl.when(pl.program_id(0) == 0)
+def update_kernel(
+    limit_sq, squares, mine, recv, first, second, b_hbm, new_first, new_second, out, way, b, sem
+):
+    step = pl.program_id(0)
+    wide = b.shape[2]
+
+    def copy(j):
+        return pltpu.make_async_copy(b_hbm.at[:, pl.ds(j * wide, wide)], b.at[j], sem.at[j])
+
+    @pl.when(step == 0)
     def _():
+        for j in range(b.shape[0]):
+            copy(j).start()
         total = jnp.sum(squares[...])
         clip_limit = jnp.sqrt(jnp.full((1, 1), limit_sq, F32))
         factor = jnp.minimum(1.0, clip_limit / jnp.sqrt(jnp.full((1, 1), total, F32)))
@@ -313,9 +300,10 @@
             padded = jnp.concatenate([turn, jnp.zeros((PAD - UNITS, turn.shape[1]), F32)], axis=0)
             way[m] = padded.astype(BF16)
 
+    copy(step).wait()
     for m in range(3):
         full = lax.dot_general(
-            way[m], b[m], (((1,), (1,)), ((), ())), preferred_element_type=F32
+            way[m], b[step, m], (((1,), (1,)), ((), ())), preferred_element_type=F32
         ).astype(BF16)
         for n in range(out.shape[0]):
             out[n, m] = full[:, n * LANES : (n + 1) * LANES]
@@ -331,15 +319,18 @@
     return pl.pallas_call(
         functools.partial(update_kernel, limit_sq),
         grid=(steps,),
-        in_specs=[whole(t) for t in inputs]
-        + [pl.BlockSpec((3, width // steps, rank), lambda i: (0, i, 0))],
+        in_specs=[whole(t) for t in inputs] + [ANY],
         out_specs=[
             whole(moment),
             whole(moment),
             pl.BlockSpec((owners // steps, 3, PAD, LANES), lambda i: (i, 0, 0, 0)),
         ],
         out_shape=[moment, moment, jax.ShapeDtypeStruct((owners, 3, PAD, LANES), BF16)],
-        scratch_shapes=[pltpu.VMEM((3, PAD, rank), BF16)],
+        scratch_shapes=[
+            pltpu.VMEM((3, PAD, rank), BF16),
+            pltpu.VMEM((steps, 3, width // steps, rank), BF16),
+            pltpu.SemaphoreType.DMA((steps,)),
+        ],
         compiler_params=params(52),
         name="update",
     )(*inputs, bases)
@@ -377,22 +368,20 @@
     theirs_two = lax.ppermute(sent_two, "dp", CORE_PAIRS)
     kept_one, sent_one = project(down_out_grad, bases, 2, 1)
     theirs_one = lax.ppermute(sent_one, "dp", CORE_PAIRS)
-    xa, xb, za_one, zb_one = collect(PIECES_TWO, gate_up, gate_up_there, kept_two, theirs_two)
+    kept_two, kept_one = lax.optimization_barrier((kept_two, kept_one))
+    xa, xb = collect(True, gate_up, gate_up_there, kept_two, theirs_two)
     xr = lax.ppermute(xb, "dp", along_x(0))
-    zr_one = lax.ppermute(zb_one, "dp", along_z(0))
-    za_two, zb_two = collect(PIECES_ONE, hidden, hidden_there, kept_one, theirs_one)
-    zr_two = lax.ppermute(zb_two, "dp", along_z(0))
-
-    xa, xb = split_sum([xa], [xr], 2)
-    za_one, za_two, xb = lax.optimization_barrier((za_one, za_two, xb))
+    za, zb = collect(False, hidden, hidden_there, kept_one, theirs_one)
+    zr = lax.ppermute(zb, "dp", along_z(0))
+    za, zb = split_sum(za, zr, 2)
+    xa, zb = lax.optimization_barrier((xa, zb))
+    xa, xb = split_sum(xa, xr, 2)
+    zr = lax.ppermute(zb, "dp", along_z(1))
     xr = lax.ppermute(xb, "dp", along_x(1))
-    za, zb = split_sum([za_two, za_one], [zr_two, zr_one], 2)
-    zr = lax.ppermute(zb, "dp", along_z(1))
-    by_x = split_sum([xa[0]], [xr[0]], 4)
-    za, *by_x = lax.optimization_barrier((za, *by_x))
-    by_z = split_sum([za[0]], [zr[0]], 4)
+    by_z = split_sum(za[0], zr[0], 4)
+    by_x = split_sum(xa[0], xr[0], 4)
+    by_z = [by_z[0]] + [lax.ppermute(by_z[r], "dp", direct_x(r)) for r in (1, 2, 3)]
     by_x = [by_x[0]] + [lax.ppermute(by_x[r], "dp", direct_z(r)) for r in (1, 2, 3)]
-    by_z = [by_z[0]] + [lax.ppermute(by_z[r], "dp", direct_x(r)) for r in (1, 2, 3)]
     mine, fix, squares = owned_sum(by_x, by_z, devices)
     fix = lax.ppermute(fix, "dp", CORE_PAIRS)
     squares = lax.all_to_all(squares, ("dp", "tensor"), 0, 0, tiled=True)

time: 134 us -> 132 us (0.985)
  waiting for transfers between devices: 57.8 us -> 55.6 us
  starting transfers between devices: 34 us -> 36.1 us
    ppermute x1, waiting for transfers between devices: 7.31 us -> 0.01 us  [body(): xr = lax.ppermute(xb, 'dp', along_x(0))]
    ppermute x2 -> x1, waiting for transfers between devices: 2.62 us -> 9.37 us  [body(): zr = lax.ppermute(zb, 'dp', along_z(0))]
    ppermute x3, waiting for transfers between devices: 4.61 us -> 0.01 us  [body(): lax.ppermute(by_x[r], 'dp', direct_z(r))]
    ppermute x3, waiting for transfers between devices: 0.01 us -> 3.47 us  [body(): lax.ppermute(by_z[r], 'dp', direct_x(r))]
    all_to_all x1, starting transfers between devices: 8.06 us -> 9.71 us  [body(): squares = lax.all_to_all(squares, ('dp', 'tensor'), 0, 0, tiled=True)]
    unnamed x17 -> x19, local copies, waits for them, and re-layouts: 3.8 us -> 3.8 us
  transfers between devices with their start and end apart: 18 -> 17, of which waited for: 8 -> 8; matrix products, arithmetic and copies ran while one was open for 3% -> 3% of each run, Pallas kernels for 19% -> 19%
where the time goes in v6:
time: 132 us
  waiting for transfers between devices  55.6 us (42%)
  starting transfers between devices  36.1 us (27%)
  Pallas kernels  35.6 us (27%)
  local copies, waits for them, and re-layouts  3.8 us (3%)
    all_to_all x1, waiting for transfers between devices, body(): pieces = lax.all_to_all(pieces, 'dp', 0, 0, tiled=True)  28.1 us
    pallas_call x2, Pallas kernels, project(): pl.pallas_call(functools.partial(project_kernel, first, steps, 8), in_spe...  13.4 us
    pallas_call x2, Pallas kernels, collect(): pl.pallas_call(functools.partial(collect_kernel, x_first), grid=(N_Z,), i...  10.9 us
    all_to_all x1, starting transfers between devices, body(): squares = lax.all_to_all(squares, ('dp', 'tensor'), 0, 0, tiled=True)  9.71 us
    ppermute x1, waiting for transfers between devices, body(): zr = lax.ppermute(zb, 'dp', along_z(0))  9.37 us
    pallas_call x1, Pallas kernels, update(): pl.pallas_call(functools.partial(update_kernel, limit_sq), grid=(steps,),...  8.32 us
    all_to_all x1, waiting for transfers between devices, body(): squares = lax.all_to_all(squares, ('dp', 'tensor'), 0, 0, tiled=True)  7.86 us
    ppermute x1, waiting for transfers between devices, body(): zr = lax.ppermute(zb, 'dp', along_z(1))  5.4 us
  transfers between devices with their start and end apart: 17, of which 8 were waited for; matrix products, arithmetic and copies ran while one was open for 3% of the time, Pallas kernels for 19%

profile of v6, /device:TPU:0, one launch (start us, length us, event | category | flops | bytes accessed | tf_op | source)
XLA Modules:
  0.0 131.9 jit_solution(8174814696645682167)
XLA Ops:
  0.7 0.5 collective-permute-start.2
  1.2 8.4 %project.2 = (bf16[2,512,256]{2,1,0:T(8,128)(2,1)}, bf16[2,512,256]{2,1,0:T(8,128)(2,1)}) custom-call(bf16[512,4096]{1,0:T(8,128)(2,1)} %x_hbm.2, bf16[3,4096,512]{2,1,0:T(8,128)(2,1)} %b_hbm.5), custom_call_target="tpu_custom_call" | custom-call | flops 4294967296 | bytes 12582912 | tf_op jit(solution)/shard_map/project/pallas_call | solution.py:124
  9.8 5.0 %project.3 = (bf16[1,512,256]{2,1,0:T(8,128)(2,1)}, bf16[1,512,256]{2,1,0:T(8,128)(2,1)}) custom-call(bf16[512,4096]{1,0:T(8,128)(2,1)} %x_hbm.3, bf16[3,4096,512]{2,1,0:T(8,128)(2,1)} %b_hbm.5), custom_call_target="tpu_custom_call" | custom-call | flops 2147483648 | bytes 8388608 | tf_op jit(solution)/shard_map/project/pallas_call | solution.py:124
  14.8 0.2 collective-permute-done.1.theirs
  15.1 6.8 %collect.2 = (bf16[2,4,4,2,88,128]{5,4,3,2,1,0:T(8,128)(2,1)S(1)}, bf16[2,4,4,2,88,128]{5,4,3,2,1,0:T(8,128)(2,1)S(1)}) custom-call(bf16[2,2752,512]{2,1,0:T(8,128)(2,1)S(1)} %bitcast.23, bf16[2,2752,512]{2,1,0:T(8,128)(2,1)} %collective-permute-done.h, bf16[2,512,256]{2,1,0:T(8,128)(2,1)S(1)} %copy-done.1, bf16[2,512,256]{2,1,0:T(8,128)(2,1)} %collective-permute-done.1.theirs), custom_call_target="tpu_custom_call" | custom-call | flops 2885681152 | bytes 14090240 | tf_op jit(solution)/shard_map/collect/pallas_call | solution.py:198
  21.9 1.7 %collective-permute-start.5 = (bf16[2,4,4,2,88,128]{5,4,3,2,1,0:T(8,128)(2,1)S(1)}, bf16[2,4,4,2,88,128]{5,4,3,2,1,0:T(8,128)(2,1)S(1)}, u32[]{:S(2)}, u32[]{:S(2)}) collective-permute-start(bf16[2,4,4,2,88,128]{5,4,3,2,1,0:T(8,128)(2,1)S(1)} %get-tuple-element.49), channel_id=1, source_target_pairs={{0,8},{4,28},{8,0},{12,20},{16,24},{20,12},{24,16},{28,4},{32,40},... | collective-permute-start | bytes 4325384 | tf_op jit(solution)/shard_map/ppermute | solution.py:373
  23.5 1.3 collective-permute-start.3
  24.8 1.2 collective-permute-done.3.theirs
  25.9 4.1 %collect.3 = (bf16[2,4,2,2,88,128]{5,4,3,2,1,0:T(8,128)(2,1)S(1)}, bf16[2,4,2,2,88,128]{5,4,3,2,1,0:T(8,128)(2,1)S(1)}) custom-call(bf16[1,2752,512]{2,1,0:T(8,128)(2,1)S(1)} %bitcast.25, bf16[1,2752,512]{2,1,0:T(8,128)(2,1)} %collective-permute-done.2.h, bf16[1,512,256]{2,1,0:T(8,128)(2,1)S(1)} %copy-done.2, ...), custom_call_target="tpu_custom_call" | custom-call | flops 1442840576 | bytes 7045120 | tf_op jit(solution)/shard_map/collect/pallas_call | solution.py:198
  30.1 2.0 %collective-permute-start.4 = (bf16[2,4,2,2,88,128]{5,4,3,2,1,0:T(8,128)(2,1)S(1)}, bf16[2,4,2,2,88,128]{5,4,3,2,1,0:T(8,128)(2,1)S(1)}, u32[]{:S(2)}, u32[]{:S(2)}) collective-permute-start(bf16[2,4,2,2,88,128]{5,4,3,2,1,0:T(8,128)(2,1)S(1)} %get-tuple-element.46), channel_id=1, source_target_pairs={{0,32},{4,100},{8,40},{12,108},{16,48},{20,116},{24,56},{28,124},{... | collective-permute-start | bytes 2162696 | tf_op jit(solution)/shard_map/ppermute | solution.py:375
  32.1 9.4 %collective-permute-done.4.recv = bf16[2,4,2,2,88,128]{5,4,3,2,1,0:T(8,128)(2,1)S(1)} collective-permute-done((bf16[2,4,2,2,88,128]{5,4,3,2,1,0:T(8,128)(2,1)S(1)}, bf16[2,4,2,2,88,128]{5,4,3,2,1,0:T(8,128)(2,1)S(1)}, u32[]{:S(2)}, u32[]{:S(2)}) %collective-permute-start.4) | collective-permute-done | bytes 720928 | tf_op jit(solution)/shard_map/ppermute | solution.py:375
  41.7 0.3 split_sum.5
  42.0 2.2 %collective-permute-start.6 = (bf16[1,4,4,2,88,128]{5,4,3,2,1,0:T(8,128)(2,1)S(1)}, bf16[1,4,4,2,88,128]{5,4,3,2,1,0:T(8,128)(2,1)S(1)}, u32[]{:S(2)}, u32[]{:S(2)}) collective-permute-start(bf16[1,4,4,2,88,128]{5,4,3,2,1,0:T(8,128)(2,1)S(1)} %get-tuple-element.51), channel_id=1, source_target_pairs={{0,24},{4,12},{8,16},{12,4},{16,8},{20,28},{24,0},{28,20},{32,56},... | collective-permute-start | bytes 2162696 | tf_op jit(solution)/shard_map/ppermute | solution.py:380
  44.2 4.0 %collective-permute-start.10 = (bf16[1,4,2,2,88,128]{5,4,3,2,1,0:T(8,128)(2,1)S(1)}, bf16[1,4,2,2,88,128]{5,4,3,2,1,0:T(8,128)(2,1)S(1)}, u32[]{:S(2)}, u32[]{:S(2)}) collective-permute-start(bf16[1,4,2,2,88,128]{5,4,3,2,1,0:T(8,128)(2,1)S(1)} %get-tuple-element.57), channel_id=1, source_target_pairs={{0,96},{4,36},{8,104},{12,44},{16,112},{20,52},{24,120},{28,60},{3... | collective-permute-start | bytes 1081352 | tf_op jit(solution)/shard_map/ppermute | solution.py:379
  48.2 5.4 %collective-permute-done.10 = bf16[1,4,2,2,88,128]{5,4,3,2,1,0:T(8,128)(2,1)S(1)} collective-permute-done((bf16[1,4,2,2,88,128]{5,4,3,2,1,0:T(8,128)(2,1)S(1)}, bf16[1,4,2,2,88,128]{5,4,3,2,1,0:T(8,128)(2,1)S(1)}, u32[]{:S(2)}, u32[]{:S(2)}) %collective-permute-start.10) | collective-permute-done | bytes 360480 | tf_op jit(solution)/shard_map/ppermute | solution.py:379
  53.7 1.2 collective-permute-start.11
  55.1 3.8 %collective-permute-start.7 = (bf16[1,4,2,88,128]{4,3,2,1,0:T(8,128)(2,1)S(1)}, bf16[1,4,2,88,128]{4,3,2,1,0:T(8,128)(2,1)S(1)}, u32[]{:S(2)}, u32[]{:S(2)}) collective-permute-start(bf16[1,4,2,88,128]{4,3,2,1,0:T(8,128)(2,1)S(1)} %get-tuple-element.53), channel_id=1, source_target_pairs={{0,96},{4,36},{8,104},{12,44},{16,112},{20,52},{24,120},{28,60},{3... | collective-permute-start | bytes 540680 | tf_op jit(solution)/shard_map/ppermute | solution.py:384
  58.9 1.6 %collective-permute-start.9 = (bf16[1,4,2,88,128]{4,3,2,1,0:T(8,128)(2,1)S(1)}, bf16[1,4,2,88,128]{4,3,2,1,0:T(8,128)(2,1)S(1)}, u32[]{:S(2)}, u32[]{:S(2)}) collective-permute-start(bf16[1,4,2,88,128]{4,3,2,1,0:T(8,128)(2,1)S(1)} %get-tuple-element.55), channel_id=1, source_target_pairs={{0,64},{4,68},{8,72},{12,76},{16,80},{20,84},{24,88},{28,92},{32,9... | collective-permute-start | bytes 540680 | tf_op jit(solution)/shard_map/ppermute | solution.py:384
  60.4 3.6 %collective-permute-start.13 = (bf16[1,2,2,88,128]{4,3,2,1,0:T(8,128)(2,1)S(1)}, bf16[1,2,2,88,128]{4,3,2,1,0:T(8,128)(2,1)S(1)}, u32[]{:S(2)}, u32[]{:S(2)}) collective-permute-start(bf16[1,2,2,88,128]{4,3,2,1,0:T(8,128)(2,1)S(1)} %get-tuple-element.61), channel_id=1, source_target_pairs={{0,16},{4,20},{8,24},{12,28},{16,0},{20,4},{24,8},{28,12},{32,48},... | collective-permute-start | bytes 270344 | tf_op jit(solution)/shard_map/ppermute | solution.py:383
  64.0 0.9 collective-permute-done.12.refs_6_
  64.9 2.5 %collective-permute-done.13.refs_7_ = bf16[1,2,2,88,128]{4,3,2,1,0:T(8,128)(2,1)S(1)} collective-permute-done((bf16[1,2,2,88,128]{4,3,2,1,0:T(8,128)(2,1)S(1)}, bf16[1,2,2,88,128]{4,3,2,1,0:T(8,128)(2,1)S(1)}, u32[]{:S(2)}, u32[]{:S(2)}) %collective-permute-start.13) | collective-permute-done | bytes 90144 | tf_op jit(solution)/shard_map/ppermute | solution.py:383
  67.5 0.8 owned_sum.1
  68.3 9.7 %all-to-all-start = ((f32[128,1,128]{2,1,0:T(1,128)}), f32[128,1,128]{2,1,0:T(1,128)S(1)}, u32[]{:S(2)}, u32[]{:S(2)}) async-start(f32[128,1,128]{2,1,0:T(1,128)} %bitcast.9), calls=%async_computation | async-start | bytes 131072 | tf_op jit(solution)/shard_map/all_to_all | solution.py:387
  78.0 0.3 collective-permute-start.14
  78.3 1.1 copy_bitcast_fusion
  79.4 7.9 %all-to-all-done = f32[128,1,128]{2,1,0:T(1,128)S(1)} async-done(((f32[128,1,128]{2,1,0:T(1,128)}), f32[128,1,128]{2,1,0:T(1,128)S(1)}, u32[]{:S(2)}, u32[]{:S(2)}) %all-to-all-start) | async-done | bytes 65568 | tf_op jit(solution)/shard_map/all_to_all | solution.py:387
  87.3 8.3 %update.1 = (f32[3,86,512]{2,1,0:T(8,128)S(1)}, f32[3,86,512]{2,1,0:T(8,128)S(1)}, bf16[32,3,88,128]{3,2,1,0:T(8,128)(2,1)}) custom-call(f32[128,128]{1,0:T(8,128)S(1)} %bitcast.32, f32[3,88,256]{2,1,0:T(8,128)S(1)} %get-tuple-element.63.mine, bf16[3,88,256]{2,1,0:T(8,128)(2,1)S(1)} %collective-permute-done.14.recv, f32[3,86,512]{2,1,0:T(8,128)} %get-tuple-element.82.first, ...), custom_call_target="tpu_custom_call" | custom-call | tf_op jit(solution)/shard_map/update/pallas_call | solution.py:319
  95.6 4.1 %all-to-all-start.1 = ((bf16[32,3,88,128]{3,2,1,0:T(8,128)(2,1)}), bf16[32,3,88,128]{3,2,1,0:T(8,128)(2,1)S(1)}, u32[]{:S(2)}, u32[]{:S(2)}) async-start(bf16[32,3,88,128]{3,2,1,0:T(8,128)(2,1)} %get-tuple-element.65), calls=%async_computation.1 | async-start | bytes 4325376 | tf_op jit(solution)/shard_map/all_to_all | solution.py:393
  99.7 1.3 %copy.15 = f32[3,1,86,512]{3,1,2,0:T(1,128)} copy(f32[3,1,86,512]{3,2,0,1:T(8,128)S(1)} %bitcast.29) | data formatting | bytes 1056768
  101.0 1.3 %copy.16 = f32[3,1,86,512]{3,1,2,0:T(1,128)} copy(f32[3,1,86,512]{3,2,0,1:T(8,128)S(1)} %bitcast.28) | data formatting | bytes 1056768
  102.3 28.1 %all-to-all-done.1.pieces = bf16[32,3,88,128]{3,2,1,0:T(8,128)(2,1)S(1)} async-done(((bf16[32,3,88,128]{3,2,1,0:T(8,128)(2,1)}), bf16[32,3,88,128]{3,2,1,0:T(8,128)(2,1)S(1)}, u32[]{:S(2)}, u32[]{:S(2)}) %all-to-all-start.1) | async-done | bytes 2162720 | tf_op jit(solution)/shard_map/all_to_all | solution.py:393
  130.4 1.5 %layout.1 = (bf16[2752,128]{1,0:T(8,128)(2,1)}, bf16[2752,128]{1,0:T(8,128)(2,1)}, bf16[2752,128]{1,0:T(8,128)(2,1)}) custom-call(bf16[32,3,88,128]{3,2,1,0:T(8,128)(2,1)S(1)} %all-to-all-done.1.pieces), custom_call_target="tpu_custom_call" | custom-call | tf_op jit(solution)/shard_map/layout/pallas_call | solution.py:349
  (33 shorter events, 0.8 us)
Async XLA Ops:
  0.6 14.4 %collective-permute-start = (bf16[2,2752,512]{2,1,0:T(8,128)(2,1)}, bf16[2,2752,512]{2,1,0:T(8,128)(2,1)}, u32[]{:S(2)}, u32[]{:S(2)}) collective-permute-start(bf16[2,2752,512]{2,1,0:T(8,128)(2,1)} %bitcast.20), channel_id=1, source_target_pairs={{0,4},{4,0},{8,12},{12,8},{16,20},{20,16},{24,28},{28,24},{32,36},... | collective-permute-start | bytes 16908296 | tf_op jit(solution)/shard_map/ppermute | solution.py:365
  0.7 25.2 %collective-permute-start.2 = (bf16[1,2752,512]{2,1,0:T(8,128)(2,1)}, bf16[1,2752,512]{2,1,0:T(8,128)(2,1)}, u32[]{:S(2)}, u32[]{:S(2)}) collective-permute-start(bf16[1,2752,512]{2,1,0:T(8,128)(2,1)} %bitcast.24), channel_id=1, source_target_pairs={{0,4},{4,0},{8,12},{12,8},{16,20},{20,16},{24,28},{28,24},{32,36},... | collective-permute-start | bytes 8454152 | tf_op jit(solution)/shard_map/ppermute | solution.py:366
  9.6 5.5 %slice-start = ((s8[5636096]{0:T(1024)(128)(4,1)}), s8[4194304]{0:T(1024)(128)(4,1)S(1)}, s32[]{:S(2)}) async-start(s8[5636096]{0:T(1024)(128)(4,1)} %bitcast.21), calls=%async_computation.2 | async-start | bytes 8388608
  9.6 5.5 %slice-start.1 = ((s8[5636096]{0:T(1024)(128)(4,1)}), s8[1441792]{0:T(1024)(128)(4,1)S(1)}, s32[]{:S(2)}) async-start(s8[5636096]{0:T(1024)(128)(4,1)} %bitcast.21), calls=%async_computation.3 | async-start | bytes 2883584
  9.6 5.5 %copy-start.1 = (bf16[2,512,256]{2,1,0:T(8,128)(2,1)S(1)}, bf16[2,512,256]{2,1,0:T(8,128)(2,1)}, u32[]{:S(2)}) copy-start(bf16[2,512,256]{2,1,0:T(8,128)(2,1)} %get-tuple-element.40.mine) | copy-start | bytes 1572868
  9.6 5.4 %collective-permute-start.1 = (bf16[2,512,256]{2,1,0:T(8,128)(2,1)}, bf16[2,512,256]{2,1,0:T(8,128)(2,1)}, u32[]{:S(2)}, u32[]{:S(2)}) collective-permute-start(bf16[2,512,256]{2,1,0:T(8,128)(2,1)} %get-tuple-element.41), channel_id=1, source_target_pairs={{0,4},{4,0},{8,12},{12,8},{16,20},{20,16},{24,28},{28,24},{32,36},... | collective-permute-start | bytes 1572872 | tf_op jit(solution)/shard_map/ppermute | solution.py:368
  14.8 8.7 %copy-start.5 = (bf16[1,512,256]{2,1,0:T(8,128)(2,1)S(1)}, bf16[1,512,256]{2,1,0:T(8,128)(2,1)}, u32[]{:S(2)}) copy-start(bf16[1,512,256]{2,1,0:T(8,128)(2,1)} %get-tuple-element.44) | copy-start | bytes 786436
  14.8 11.1 %copy-start = (bf16[512,2752]{0,1:T(8,128)(2,1)S(1)}, bf16[512,2752]{0,1:T(8,128)(2,1)}, u32[]{:S(2)}) copy-start(bf16[512,2752]{0,1:T(8,128)(2,1)} %param.9) | copy-start | bytes 8454148
  14.8 11.1 %copy-start.2 = (bf16[1,512,256]{2,1,0:T(8,128)(2,1)S(1)}, bf16[1,512,256]{2,1,0:T(8,128)(2,1)}, u32[]{:S(2)}) copy-start(bf16[1,512,256]{2,1,0:T(8,128)(2,1)} %get-tuple-element.43.mine) | copy-start | bytes 786436
  21.9 19.8 %collective-permute-start.5 = (bf16[2,4,4,2,88,128]{5,4,3,2,1,0:T(8,128)(2,1)S(1)}, bf16[2,4,4,2,88,128]{5,4,3,2,1,0:T(8,128)(2,1)S(1)}, u32[]{:S(2)}, u32[]{:S(2)}) collective-permute-start(bf16[2,4,4,2,88,128]{5,4,3,2,1,0:T(8,128)(2,1)S(1)} %get-tuple-element.49), channel_id=1, source_target_pairs={{0,8},{4,28},{8,0},{12,20},{16,24},{20,12},{24,16},{28,4},{32,40},... | collective-permute-start | bytes 4325384 | tf_op jit(solution)/shard_map/ppermute | solution.py:373
  23.5 2.4 %collective-permute-start.3 = (bf16[1,512,256]{2,1,0:T(8,128)(2,1)S(1)}, bf16[1,512,256]{2,1,0:T(8,128)(2,1)S(1)}, u32[]{:S(2)}, u32[]{:S(2)}) collective-permute-start(bf16[1,512,256]{2,1,0:T(8,128)(2,1)S(1)} %copy-done.5), channel_id=1, source_target_pairs={{0,4},{4,0},{8,12},{12,8},{16,20},{20,16},{24,28},{28,24},{32,36},... | collective-permute-start | bytes 786440 | tf_op jit(solution)/shard_map/ppermute | solution.py:370
  30.1 11.4 %collective-permute-start.4 = (bf16[2,4,2,2,88,128]{5,4,3,2,1,0:T(8,128)(2,1)S(1)}, bf16[2,4,2,2,88,128]{5,4,3,2,1,0:T(8,128)(2,1)S(1)}, u32[]{:S(2)}, u32[]{:S(2)}) collective-permute-start(bf16[2,4,2,2,88,128]{5,4,3,2,1,0:T(8,128)(2,1)S(1)} %get-tuple-element.46), channel_id=1, source_target_pairs={{0,32},{4,100},{8,40},{12,108},{16,48},{20,116},{24,56},{28,124},{... | collective-permute-start | bytes 2162696 | tf_op jit(solution)/shard_map/ppermute | solution.py:375
  41.6 36.7 %copy-start.3 = (f32[3,1,86,512]{3,1,2,0:T(1,128)S(1)}, f32[3,1,86,512]{3,1,2,0:T(1,128)}, u32[]{:S(2)}) copy-start(f32[3,1,86,512]{3,1,2,0:T(1,128)} %param.13) | copy-start | bytes 1585156
  41.6 36.7 %copy-start.4 = (f32[3,1,86,512]{3,1,2,0:T(1,128)S(1)}, f32[3,1,86,512]{3,1,2,0:T(1,128)}, u32[]{:S(2)}) copy-start(f32[3,1,86,512]{3,1,2,0:T(1,128)} %param.12) | copy-start | bytes 1585156
  42.0 12.9 %collective-permute-start.6 = (bf16[1,4,4,2,88,128]{5,4,3,2,1,0:T(8,128)(2,1)S(1)}, bf16[1,4,4,2,88,128]{5,4,3,2,1,0:T(8,128)(2,1)S(1)}, u32[]{:S(2)}, u32[]{:S(2)}) collective-permute-start(bf16[1,4,4,2,88,128]{5,4,3,2,1,0:T(8,128)(2,1)S(1)} %get-tuple-element.51), channel_id=1, source_target_pairs={{0,24},{4,12},{8,16},{12,4},{16,8},{20,28},{24,0},{28,20},{32,56},... | collective-permute-start | bytes 2162696 | tf_op jit(solution)/shard_map/ppermute | solution.py:380
  44.2 9.4 %collective-permute-start.10 = (bf16[1,4,2,2,88,128]{5,4,3,2,1,0:T(8,128)(2,1)S(1)}, bf16[1,4,2,2,88,128]{5,4,3,2,1,0:T(8,128)(2,1)S(1)}, u32[]{:S(2)}, u32[]{:S(2)}) collective-permute-start(bf16[1,4,2,2,88,128]{5,4,3,2,1,0:T(8,128)(2,1)S(1)} %get-tuple-element.57), channel_id=1, source_target_pairs={{0,96},{4,36},{8,104},{12,44},{16,112},{20,52},{24,120},{28,60},{3... | collective-permute-start | bytes 1081352 | tf_op jit(solution)/shard_map/ppermute | solution.py:379
  53.7 6.7 %collective-permute-start.11 = (bf16[1,2,2,88,128]{4,3,2,1,0:T(8,128)(2,1)S(1)}, bf16[1,2,2,88,128]{4,3,2,1,0:T(8,128)(2,1)S(1)}, u32[]{:S(2)}, u32[]{:S(2)}) collective-permute-start(bf16[1,2,2,88,128]{4,3,2,1,0:T(8,128)(2,1)S(1)} %get-tuple-element.59), channel_id=1, source_target_pairs={{0,24},{4,12},{8,16},{12,4},{16,8},{20,28},{24,0},{28,20},{32,56},... | collective-permute-start | bytes 270344 | tf_op jit(solution)/shard_map/ppermute | solution.py:383
  55.1 12.4 %collective-permute-start.7 = (bf16[1,4,2,88,128]{4,3,2,1,0:T(8,128)(2,1)S(1)}, bf16[1,4,2,88,128]{4,3,2,1,0:T(8,128)(2,1)S(1)}, u32[]{:S(2)}, u32[]{:S(2)}) collective-permute-start(bf16[1,4,2,88,128]{4,3,2,1,0:T(8,128)(2,1)S(1)} %get-tuple-element.53), channel_id=1, source_target_pairs={{0,96},{4,36},{8,104},{12,44},{16,112},{20,52},{24,120},{28,60},{3... | collective-permute-start | bytes 540680 | tf_op jit(solution)/shard_map/ppermute | solution.py:384
  58.9 8.6 %collective-permute-start.8 = (bf16[1,4,2,88,128]{4,3,2,1,0:T(8,128)(2,1)S(1)}, bf16[1,4,2,88,128]{4,3,2,1,0:T(8,128)(2,1)S(1)}, u32[]{:S(2)}, u32[]{:S(2)}) collective-permute-start(bf16[1,4,2,88,128]{4,3,2,1,0:T(8,128)(2,1)S(1)} %get-tuple-element.54), channel_id=1, source_target_pairs={{0,32},{4,100},{8,40},{12,108},{16,48},{20,116},{24,56},{28,124},{... | collective-permute-start | bytes 540680 | tf_op jit(solution)/shard_map/ppermute | solution.py:384
  58.9 8.6 %collective-permute-start.9 = (bf16[1,4,2,88,128]{4,3,2,1,0:T(8,128)(2,1)S(1)}, bf16[1,4,2,88,128]{4,3,2,1,0:T(8,128)(2,1)S(1)}, u32[]{:S(2)}, u32[]{:S(2)}) collective-permute-start(bf16[1,4,2,88,128]{4,3,2,1,0:T(8,128)(2,1)S(1)} %get-tuple-element.55), channel_id=1, source_target_pairs={{0,64},{4,68},{8,72},{12,76},{16,80},{20,84},{24,88},{28,92},{32,9... | collective-permute-start | bytes 540680 | tf_op jit(solution)/shard_map/ppermute | solution.py:384
  60.4 4.5 %collective-permute-start.12 = (bf16[1,2,2,88,128]{4,3,2,1,0:T(8,128)(2,1)S(1)}, bf16[1,2,2,88,128]{4,3,2,1,0:T(8,128)(2,1)S(1)}, u32[]{:S(2)}, u32[]{:S(2)}) collective-permute-start(bf16[1,2,2,88,128]{4,3,2,1,0:T(8,128)(2,1)S(1)} %get-tuple-element.60), channel_id=1, source_target_pairs={{0,8},{4,28},{8,0},{12,20},{16,24},{20,12},{24,16},{28,4},{32,40},... | collective-permute-start | bytes 270344 | tf_op jit(solution)/shard_map/ppermute | solution.py:383
  60.4 7.0 %collective-permute-start.13 = (bf16[1,2,2,88,128]{4,3,2,1,0:T(8,128)(2,1)S(1)}, bf16[1,2,2,88,128]{4,3,2,1,0:T(8,128)(2,1)S(1)}, u32[]{:S(2)}, u32[]{:S(2)}) collective-permute-start(bf16[1,2,2,88,128]{4,3,2,1,0:T(8,128)(2,1)S(1)} %get-tuple-element.61), channel_id=1, source_target_pairs={{0,16},{4,20},{8,24},{12,28},{16,0},{20,4},{24,8},{28,12},{32,48},... | collective-permute-start | bytes 270344 | tf_op jit(solution)/shard_map/ppermute | solution.py:383
  68.3 19.0 %all-to-all-start = ((f32[128,1,128]{2,1,0:T(1,128)}), f32[128,1,128]{2,1,0:T(1,128)S(1)}, u32[]{:S(2)}, u32[]{:S(2)}) async-start(f32[128,1,128]{2,1,0:T(1,128)} %bitcast.9), calls=%async_computation | async-start | bytes 131072 | tf_op jit(solution)/shard_map/all_to_all | solution.py:387
  78.0 9.2 %collective-permute-start.14 = (bf16[3,88,256]{2,1,0:T(8,128)(2,1)S(1)}, bf16[3,88,256]{2,1,0:T(8,128)(2,1)S(1)}, u32[]{:S(2)}, u32[]{:S(2)}) collective-permute-start(bf16[3,88,256]{2,1,0:T(8,128)(2,1)S(1)} %get-tuple-element.64), channel_id=1, source_target_pairs={{0,4},{4,0},{8,12},{12,8},{16,20},{20,16},{24,28},{28,24},{32,36},... | collective-permute-start | bytes 405512 | tf_op jit(solution)/shard_map/ppermute | solution.py:386
  95.6 34.8 %all-to-all-start.1 = ((bf16[32,3,88,128]{3,2,1,0:T(8,128)(2,1)}), bf16[32,3,88,128]{3,2,1,0:T(8,128)(2,1)S(1)}, u32[]{:S(2)}, u32[]{:S(2)}) async-start(bf16[32,3,88,128]{3,2,1,0:T(8,128)(2,1)} %get-tuple-element.65), calls=%async_computation.1 | async-start | bytes 4325376 | tf_op jit(solution)/shard_map/all_to_all | solution.py:393

commit v7 on v6

--- a/solution.py
+++ b/solution.py
@@ -116,13 +116,13 @@
                 sent[m] = jnp.where(lower, high, low)
 
 
-def project(x, bases, first, count):
+def project(x, bases, first, count, window):
     tokens, width = x.shape
     rank = bases.shape[2]
     steps = 8
     out = jax.ShapeDtypeStruct((count, tokens, rank // 2), BF16)
     return pl.pallas_call(
-        functools.partial(project_kernel, first, steps, 8),
+        functools.partial(project_kernel, first, steps, window),
         in_specs=[ANY, ANY],
         out_specs=[VMEM] * 2,
         out_shape=[out, out],
@@ -235,7 +235,7 @@
 
 
 def owned_kernel(*refs):
-    parts, (mine, fix, squares) = refs[:8], refs[8:]
+    parts, (mine, fix, squares) = refs[:-3], refs[-3:]
     inside = lax.broadcasted_iota(jnp.int32, (PAD, LANES), 0) < UNITS
     total_sq = jnp.zeros((PAD, LANES), F32)
     for m in range(3):
@@ -243,8 +243,7 @@
             t, piece = (parts[:4], 2 * m + half) if m < 2 else (parts[4:], half)
             lanes = slice(half * LANES, half * LANES + LANES)
             for c in range(N_C):
-                v = t[0][0, piece, c].astype(F32) + t[1][0, piece, c].astype(F32)
-                v = v + (t[2][0, piece, c].astype(F32) + t[3][0, piece, c].astype(F32))
+                v = sum(u[0, piece, c].astype(F32) for u in t)
                 total_sq += jnp.where(inside, v * v, 0.0)
                 if c == 0:
                     mine[m, :, lanes] = v
@@ -257,7 +256,7 @@
 def owned_sum(by_x, by_z, peers):
     return pl.pallas_call(
         owned_kernel,
-        in_specs=[VMEM] * 8,
+        in_specs=[VMEM] * len((*by_x, *by_z)),
         out_specs=[VMEM] * 3,
         out_shape=[
             jax.ShapeDtypeStruct((3, PAD, 2 * LANES), F32),
@@ -336,12 +335,17 @@
     )(*inputs, bases)
 
 
-def layout_kernel(pieces, gate, up, down, rows):
+def layout_kernel(pieces, gate, up, down, rows, done, sem):
     units = N_DP * UNITS
+    copies = []
     for m, out in enumerate((gate, up, down)):
         for k in range(N_DP):
             rows[m, k * UNITS : k * UNITS + PAD, :] = pieces[k, m].astype(F32)
-        out[...] = rows[m, :units, :].astype(BF16)
+        done[m] = rows[m, :units, :].astype(BF16)
+        copies.append(pltpu.make_async_copy(done.at[m], out, sem.at[m]))
+        copies[-1].start()
+    for copy in copies:
+        copy.wait()
 
 
 def layout(pieces):
@@ -349,9 +353,13 @@
     return pl.pallas_call(
         layout_kernel,
         in_specs=[VMEM],
-        out_specs=[VMEM] * 3,
+        out_specs=[ANY] * 3,
         out_shape=[jax.ShapeDtypeStruct((units, LANES), BF16)] * 3,
-        scratch_shapes=[pltpu.VMEM((3, units + 8, LANES), F32)],
+        scratch_shapes=[
+            pltpu.VMEM((3, units + 8, LANES), F32),
+            pltpu.VMEM((3, units, LANES), BF16),
+            pltpu.SemaphoreType.DMA((3,)),
+        ],
         compiler_params=params(24),
         name="layout",
     )(pieces)
@@ -363,12 +371,14 @@
     gate_up = jnp.swapaxes(gate_up_grads, 1, 2)
     hidden = hidden_act.T[None]
     gate_up_there = lax.ppermute(gate_up, "dp", CORE_PAIRS)
-    hidden_there = lax.ppermute(hidden, "dp", CORE_PAIRS)
-    kept_two, sent_two = project(activations, bases, 0, 2)
+    kept_two, sent_two = project(activations, bases, 0, 2, 4)
     theirs_two = lax.ppermute(sent_two, "dp", CORE_PAIRS)
-    kept_one, sent_one = project(down_out_grad, bases, 2, 1)
+    kept_one, sent_one = project(down_out_grad, bases, 2, 1, 8)
     theirs_one = lax.ppermute(sent_one, "dp", CORE_PAIRS)
-    kept_two, kept_one = lax.optimization_barrier((kept_two, kept_one))
+    kept_two, kept_one, theirs_two, later = lax.optimization_barrier(
+        (kept_two, kept_one, theirs_two, hidden)
+    )
+    hidden_there = lax.ppermute(later, "dp", CORE_PAIRS)
     xa, xb = collect(True, gate_up, gate_up_there, kept_two, theirs_two)
     xr = lax.ppermute(xb, "dp", along_x(0))
     za, zb = collect(False, hidden, hidden_there, kept_one, theirs_one)
@@ -378,9 +388,11 @@
     xa, xb = split_sum(xa, xr, 2)
     zr = lax.ppermute(zb, "dp", along_z(1))
     xr = lax.ppermute(xb, "dp", along_x(1))
-    by_z = split_sum(za[0], zr[0], 4)
+    za, zb = split_sum(za[0], zr[0], 2)
+    zr = lax.ppermute(zb, "dp", along_x(0))
+    za, zb = split_sum(za, zr, 2)
     by_x = split_sum(xa[0], xr[0], 4)
-    by_z = [by_z[0]] + [lax.ppermute(by_z[r], "dp", direct_x(r)) for r in (1, 2, 3)]
+    by_z = [za, lax.ppermute(zb, "dp", along_x(1))]
     by_x = [by_x[0]] + [lax.ppermute(by_x[r], "dp", direct_z(r)) for r in (1, 2, 3)]
     mine, fix, squares = owned_sum(by_x, by_z, devices)
     fix = lax.ppermute(fix, "dp", CORE_PAIRS)

time: 132 us -> 131 us (level)
  Pallas kernels: 35.6 us -> 33.4 us
    ppermute x4 -> x3, starting transfers between devices: 5.27 us -> 3.45 us  [the longest x1 3.05 us: body(): by_z = [za, lax.ppermute(zb, 'dp', along_x(1))]]
    pallas_call x2, Pallas kernels: 10.9 us -> 9.11 us  [collect(): pl.pallas_call(functools.partial(collect_kernel, x_first), grid=(N_Z,), i...]
    ppermute x4 -> x3, waiting for transfers between devices: 3.47 us -> 2.77 us  [the longest x1 2.76 us: body(): by_z = [za, lax.ppermute(zb, 'dp', along_x(1))]]
  transfers between devices with their start and end apart: 17 -> 16, of which waited for: 8 -> 8; matrix products, arithmetic and copies ran while one was open for 3% -> 3% of each run, Pallas kernels for 19% -> 17%
where the time goes in v7:
time: 131 us
  waiting for transfers between devices  56.3 us (43%)
  starting transfers between devices  36.5 us (28%)
  Pallas kernels  33.4 us (25%)
  local copies, waits for them, and re-layouts  3.8 us (3%)
    all_to_all x1, waiting for transfers between devices, body(): pieces = lax.all_to_all(pieces, 'dp', 0, 0, tiled=True)  28.1 us
    pallas_call x2, Pallas kernels, project(): pl.pallas_call(functools.partial(project_kernel, first, steps, window), i...  12.9 us
    all_to_all x1, starting transfers between devices, body(): squares = lax.all_to_all(squares, ('dp', 'tensor'), 0, 0, tiled=True)  10.1 us
    ppermute x1, waiting for transfers between devices, body(): zr = lax.ppermute(zb, 'dp', along_z(0))  9.37 us
    pallas_call x2, Pallas kernels, collect(): pl.pallas_call(functools.partial(collect_kernel, x_first), grid=(N_Z,), i...  9.11 us
    pallas_call x1, Pallas kernels, update(): pl.pallas_call(functools.partial(update_kernel, limit_sq), grid=(steps,),...  8.32 us
    all_to_all x1, waiting for transfers between devices, body(): squares = lax.all_to_all(squares, ('dp', 'tensor'), 0, 0, tiled=True)  7.86 us
    ppermute x3, starting transfers between devices, body(): lax.ppermute(by_x[r], 'dp', direct_z(r))  6.01 us
  transfers between devices with their start and end apart: 16, of which 8 were waited for; matrix products, arithmetic and copies ran while one was open for 3% of the time, Pallas kernels for 17%

profile of v7, /device:TPU:0, one launch (start us, length us, event | category | flops | bytes accessed | tf_op | source)
XLA Modules:
  0.0 131.0 jit_solution(2548273944898349595)
XLA Ops:
  0.7 7.7 %project.2 = (bf16[2,512,256]{2,1,0:T(8,128)(2,1)}, bf16[2,512,256]{2,1,0:T(8,128)(2,1)}) custom-call(bf16[512,4096]{1,0:T(8,128)(2,1)} %x_hbm.2, bf16[3,4096,512]{2,1,0:T(8,128)(2,1)} %b_hbm.5), custom_call_target="tpu_custom_call" | custom-call | flops 4294967296 | bytes 12582912 | tf_op jit(solution)/shard_map/project/pallas_call | solution.py:124
  8.5 0.6 collective-permute-start.1
  9.1 5.1 %project.3 = (bf16[1,512,256]{2,1,0:T(8,128)(2,1)}, bf16[1,512,256]{2,1,0:T(8,128)(2,1)}) custom-call(bf16[512,4096]{1,0:T(8,128)(2,1)} %x_hbm.3, bf16[3,4096,512]{2,1,0:T(8,128)(2,1)} %b_hbm.5), custom_call_target="tpu_custom_call" | custom-call | flops 2147483648 | bytes 8388608 | tf_op jit(solution)/shard_map/project/pallas_call | solution.py:124
  14.4 6.7 %collect.2 = (bf16[2,4,4,2,88,128]{5,4,3,2,1,0:T(8,128)(2,1)S(1)}, bf16[2,4,4,2,88,128]{5,4,3,2,1,0:T(8,128)(2,1)S(1)}) custom-call(bf16[2,2752,512]{2,1,0:T(8,128)(2,1)S(1)} %bitcast.23, bf16[2,2752,512]{2,1,0:T(8,128)(2,1)} %collective-permute-done.h, bf16[2,512,256]{2,1,0:T(8,128)(2,1)S(1)} %copy-done.1, bf16[2,512,256]{2,1,0:T(8,128)(2,1)} %collective-permute-done.1.theirs), custom_call_target="tpu_custom_call" | custom-call | flops 2885681152 | bytes 14090240 | tf_op jit(solution)/shard_map/collect/pallas_call | solution.py:198
  21.1 1.7 %collective-permute-start.5 = (bf16[2,4,4,2,88,128]{5,4,3,2,1,0:T(8,128)(2,1)S(1)}, bf16[2,4,4,2,88,128]{5,4,3,2,1,0:T(8,128)(2,1)S(1)}, u32[]{:S(2)}, u32[]{:S(2)}) collective-permute-start(bf16[2,4,4,2,88,128]{5,4,3,2,1,0:T(8,128)(2,1)S(1)} %get-tuple-element.53), channel_id=1, source_target_pairs={{0,8},{4,28},{8,0},{12,20},{16,24},{20,12},{24,16},{28,4},{32,40},... | collective-permute-start | bytes 4325384 | tf_op jit(solution)/shard_map/ppermute | solution.py:383
  22.8 1.4 %collective-permute-start.3 = (bf16[1,512,256]{2,1,0:T(8,128)(2,1)S(1)}, bf16[1,512,256]{2,1,0:T(8,128)(2,1)S(1)}, u32[]{:S(2)}, u32[]{:S(2)}) collective-permute-start(bf16[1,512,256]{2,1,0:T(8,128)(2,1)S(1)} %copy-done.5), channel_id=1, source_target_pairs={{0,4},{4,0},{8,12},{12,8},{16,20},{20,16},{24,28},{28,24},{32,36},... | collective-permute-start | bytes 786440 | tf_op jit(solution)/shard_map/ppermute | solution.py:377
  24.2 1.2 collective-permute-done.3.theirs
  25.4 2.4 %collect.3 = (bf16[2,4,2,2,88,128]{5,4,3,2,1,0:T(8,128)(2,1)S(1)}, bf16[2,4,2,2,88,128]{5,4,3,2,1,0:T(8,128)(2,1)S(1)}) custom-call(bf16[1,2752,512]{2,1,0:T(8,128)(2,1)S(1)} %bitcast.25, bf16[1,2752,512]{2,1,0:T(8,128)(2,1)S(1)} %collective-permute-done.2.h, bf16[1,512,256]{2,1,0:T(8,128)(2,1)S(1)} %copy-done.2, ...), custom_call_target="tpu_custom_call" | custom-call | flops 1442840576 | bytes 7045120 | tf_op jit(solution)/shard_map/collect/pallas_call | solution.py:198
  27.8 2.0 %collective-permute-start.4 = (bf16[2,4,2,2,88,128]{5,4,3,2,1,0:T(8,128)(2,1)S(1)}, bf16[2,4,2,2,88,128]{5,4,3,2,1,0:T(8,128)(2,1)S(1)}, u32[]{:S(2)}, u32[]{:S(2)}) collective-permute-start(bf16[2,4,2,2,88,128]{5,4,3,2,1,0:T(8,128)(2,1)S(1)} %get-tuple-element.50), channel_id=1, source_target_pairs={{0,32},{4,100},{8,40},{12,108},{16,48},{20,116},{24,56},{28,124},{... | collective-permute-start | bytes 2162696 | tf_op jit(solution)/shard_map/ppermute | solution.py:385
  29.7 9.4 %collective-permute-done.4.recv = bf16[2,4,2,2,88,128]{5,4,3,2,1,0:T(8,128)(2,1)S(1)} collective-permute-done((bf16[2,4,2,2,88,128]{5,4,3,2,1,0:T(8,128)(2,1)S(1)}, bf16[2,4,2,2,88,128]{5,4,3,2,1,0:T(8,128)(2,1)S(1)}, u32[]{:S(2)}, u32[]{:S(2)}) %collective-permute-start.4) | collective-permute-done | bytes 720928 | tf_op jit(solution)/shard_map/ppermute | solution.py:385
  39.3 0.9 collective-permute-done.5.recv
  40.2 0.3 split_sum.6
  40.6 2.9 %collective-permute-start.6 = (bf16[1,4,4,2,88,128]{5,4,3,2,1,0:T(8,128)(2,1)S(1)}, bf16[1,4,4,2,88,128]{5,4,3,2,1,0:T(8,128)(2,1)S(1)}, u32[]{:S(2)}, u32[]{:S(2)}) collective-permute-start(bf16[1,4,4,2,88,128]{5,4,3,2,1,0:T(8,128)(2,1)S(1)} %get-tuple-element.55), channel_id=1, source_target_pairs={{0,24},{4,12},{8,16},{12,4},{16,8},{20,28},{24,0},{28,20},{32,56},... | collective-permute-start | bytes 2162696 | tf_op jit(solution)/shard_map/ppermute | solution.py:390
  43.5 4.0 %collective-permute-start.10 = (bf16[1,4,2,2,88,128]{5,4,3,2,1,0:T(8,128)(2,1)S(1)}, bf16[1,4,2,2,88,128]{5,4,3,2,1,0:T(8,128)(2,1)S(1)}, u32[]{:S(2)}, u32[]{:S(2)}) collective-permute-start(bf16[1,4,2,2,88,128]{5,4,3,2,1,0:T(8,128)(2,1)S(1)} %get-tuple-element.61), channel_id=1, source_target_pairs={{0,96},{4,36},{8,104},{12,44},{16,112},{20,52},{24,120},{28,60},{3... | collective-permute-start | bytes 1081352 | tf_op jit(solution)/shard_map/ppermute | solution.py:389
  47.5 5.4 %collective-permute-done.10 = bf16[1,4,2,2,88,128]{5,4,3,2,1,0:T(8,128)(2,1)S(1)} collective-permute-done((bf16[1,4,2,2,88,128]{5,4,3,2,1,0:T(8,128)(2,1)S(1)}, bf16[1,4,2,2,88,128]{5,4,3,2,1,0:T(8,128)(2,1)S(1)}, u32[]{:S(2)}, u32[]{:S(2)}) %collective-permute-start.10) | collective-permute-done | bytes 360480 | tf_op jit(solution)/shard_map/ppermute | solution.py:389
  53.0 0.3 collective-permute-start.11
  53.3 0.7 collective-permute-done.6
  54.2 4.5 %collective-permute-start.7 = (bf16[1,4,2,88,128]{4,3,2,1,0:T(8,128)(2,1)S(1)}, bf16[1,4,2,88,128]{4,3,2,1,0:T(8,128)(2,1)S(1)}, u32[]{:S(2)}, u32[]{:S(2)}) collective-permute-start(bf16[1,4,2,88,128]{4,3,2,1,0:T(8,128)(2,1)S(1)} %get-tuple-element.57), channel_id=1, source_target_pairs={{0,96},{4,36},{8,104},{12,44},{16,112},{20,52},{24,120},{28,60},{3... | collective-permute-start | bytes 540680 | tf_op jit(solution)/shard_map/ppermute | solution.py:396
  58.6 1.6 %collective-permute-start.9 = (bf16[1,4,2,88,128]{4,3,2,1,0:T(8,128)(2,1)S(1)}, bf16[1,4,2,88,128]{4,3,2,1,0:T(8,128)(2,1)S(1)}, u32[]{:S(2)}, u32[]{:S(2)}) collective-permute-start(bf16[1,4,2,88,128]{4,3,2,1,0:T(8,128)(2,1)S(1)} %get-tuple-element.59), channel_id=1, source_target_pairs={{0,64},{4,68},{8,72},{12,76},{16,80},{20,84},{24,88},{28,92},{32,9... | collective-permute-start | bytes 540680 | tf_op jit(solution)/shard_map/ppermute | solution.py:396
  60.2 3.1 %collective-permute-start.12 = (bf16[1,2,2,88,128]{4,3,2,1,0:T(8,128)(2,1)S(1)}, bf16[1,2,2,88,128]{4,3,2,1,0:T(8,128)(2,1)S(1)}, u32[]{:S(2)}, u32[]{:S(2)}) collective-permute-start(bf16[1,2,2,88,128]{4,3,2,1,0:T(8,128)(2,1)S(1)} %get-tuple-element.65), channel_id=1, source_target_pairs={{0,24},{4,12},{8,16},{12,4},{16,8},{20,28},{24,0},{28,20},{32,56},... | collective-permute-start | bytes 270344 | tf_op jit(solution)/shard_map/ppermute | solution.py:395
  63.3 2.8 %collective-permute-done.12.refs_5_ = bf16[1,2,2,88,128]{4,3,2,1,0:T(8,128)(2,1)S(1)} collective-permute-done((bf16[1,2,2,88,128]{4,3,2,1,0:T(8,128)(2,1)S(1)}, bf16[1,2,2,88,128]{4,3,2,1,0:T(8,128)(2,1)S(1)}, u32[]{:S(2)}, u32[]{:S(2)}) %collective-permute-start.12) | collective-permute-done | bytes 90144 | tf_op jit(solution)/shard_map/ppermute | solution.py:395
  66.1 0.8 owned_sum.1
  66.9 10.1 %all-to-all-start = ((f32[128,1,128]{2,1,0:T(1,128)}), f32[128,1,128]{2,1,0:T(1,128)S(1)}, u32[]{:S(2)}, u32[]{:S(2)}) async-start(f32[128,1,128]{2,1,0:T(1,128)} %bitcast.9), calls=%async_computation | async-start | bytes 131072 | tf_op jit(solution)/shard_map/all_to_all | solution.py:399
  77.0 0.3 collective-permute-start.13
  77.3 1.1 copy_bitcast_fusion
  78.4 7.9 %all-to-all-done = f32[128,1,128]{2,1,0:T(1,128)S(1)} async-done(((f32[128,1,128]{2,1,0:T(1,128)}), f32[128,1,128]{2,1,0:T(1,128)S(1)}, u32[]{:S(2)}, u32[]{:S(2)}) %all-to-all-start) | async-done | bytes 65568 | tf_op jit(solution)/shard_map/all_to_all | solution.py:399
  86.2 8.3 %update.1 = (f32[3,86,512]{2,1,0:T(8,128)S(1)}, f32[3,86,512]{2,1,0:T(8,128)S(1)}, bf16[32,3,88,128]{3,2,1,0:T(8,128)(2,1)}) custom-call(f32[128,128]{1,0:T(8,128)S(1)} %bitcast.32, f32[3,88,256]{2,1,0:T(8,128)S(1)} %get-tuple-element.67.mine, bf16[3,88,256]{2,1,0:T(8,128)(2,1)S(1)} %collective-permute-done.13.recv, f32[3,86,512]{2,1,0:T(8,128)} %get-tuple-element.86.first, ...), custom_call_target="tpu_custom_call" | custom-call | tf_op jit(solution)/shard_map/update/pallas_call | solution.py:318
  94.6 4.1 %all-to-all-start.1 = ((bf16[32,3,88,128]{3,2,1,0:T(8,128)(2,1)}), bf16[32,3,88,128]{3,2,1,0:T(8,128)(2,1)S(1)}, u32[]{:S(2)}, u32[]{:S(2)}) async-start(bf16[32,3,88,128]{3,2,1,0:T(8,128)(2,1)} %get-tuple-element.69), calls=%async_computation.1 | async-start | bytes 4325376 | tf_op jit(solution)/shard_map/all_to_all | solution.py:405
  98.6 1.3 %copy.15 = f32[3,1,86,512]{3,1,2,0:T(1,128)} copy(f32[3,1,86,512]{3,2,0,1:T(8,128)S(1)} %bitcast.29) | data formatting | bytes 1056768
  100.0 1.3 %copy.16 = f32[3,1,86,512]{3,1,2,0:T(1,128)} copy(f32[3,1,86,512]{3,2,0,1:T(8,128)S(1)} %bitcast.28) | data formatting | bytes 1056768
  101.3 28.1 %all-to-all-done.1.pieces = bf16[32,3,88,128]{3,2,1,0:T(8,128)(2,1)S(1)} async-done(((bf16[32,3,88,128]{3,2,1,0:T(8,128)(2,1)}), bf16[32,3,88,128]{3,2,1,0:T(8,128)(2,1)S(1)}, u32[]{:S(2)}, u32[]{:S(2)}) %all-to-all-start.1) | async-done | bytes 2162720 | tf_op jit(solution)/shard_map/all_to_all | solution.py:405
  129.4 1.5 %layout.1 = (bf16[2752,128]{1,0:T(8,128)(2,1)}, bf16[2752,128]{1,0:T(8,128)(2,1)}, bf16[2752,128]{1,0:T(8,128)(2,1)}) custom-call(bf16[32,3,88,128]{3,2,1,0:T(8,128)(2,1)S(1)} %all-to-all-done.1.pieces), custom_call_target="tpu_custom_call" | custom-call | tf_op jit(solution)/shard_map/layout/pallas_call | solution.py:353
  (32 shorter events, 0.7 us)
Async XLA Ops:
  0.6 13.7 %collective-permute-start = (bf16[2,2752,512]{2,1,0:T(8,128)(2,1)}, bf16[2,2752,512]{2,1,0:T(8,128)(2,1)}, u32[]{:S(2)}, u32[]{:S(2)}) collective-permute-start(bf16[2,2752,512]{2,1,0:T(8,128)(2,1)} %bitcast.20), channel_id=1, source_target_pairs={{0,4},{4,0},{8,12},{12,8},{16,20},{20,16},{24,28},{28,24},{32,36},... | collective-permute-start | bytes 16908296 | tf_op jit(solution)/shard_map/ppermute | solution.py:373
  8.5 5.9 %slice-start = ((s8[5636096]{0:T(1024)(128)(4,1)}), s8[4194304]{0:T(1024)(128)(4,1)S(1)}, s32[]{:S(2)}) async-start(s8[5636096]{0:T(1024)(128)(4,1)} %bitcast.21), calls=%async_computation.2 | async-start | bytes 8388608
  8.5 5.9 %slice-start.1 = ((s8[5636096]{0:T(1024)(128)(4,1)}), s8[1441792]{0:T(1024)(128)(4,1)S(1)}, s32[]{:S(2)}) async-start(s8[5636096]{0:T(1024)(128)(4,1)} %bitcast.21), calls=%async_computation.3 | async-start | bytes 2883584
  8.5 5.9 %copy-start.1 = (bf16[2,512,256]{2,1,0:T(8,128)(2,1)S(1)}, bf16[2,512,256]{2,1,0:T(8,128)(2,1)}, u32[]{:S(2)}) copy-start(bf16[2,512,256]{2,1,0:T(8,128)(2,1)} %get-tuple-element.43.mine) | copy-start | bytes 1572868
  8.5 5.7 %collective-permute-start.1 = (bf16[2,512,256]{2,1,0:T(8,128)(2,1)}, bf16[2,512,256]{2,1,0:T(8,128)(2,1)}, u32[]{:S(2)}, u32[]{:S(2)}) collective-permute-start(bf16[2,512,256]{2,1,0:T(8,128)(2,1)} %get-tuple-element.42), channel_id=1, source_target_pairs={{0,4},{4,0},{8,12},{12,8},{16,20},{20,16},{24,28},{28,24},{32,36},... | collective-permute-start | bytes 1572872 | tf_op jit(solution)/shard_map/ppermute | solution.py:375
  14.2 8.6 %copy-start.5 = (bf16[1,512,256]{2,1,0:T(8,128)(2,1)S(1)}, bf16[1,512,256]{2,1,0:T(8,128)(2,1)}, u32[]{:S(2)}) copy-start(bf16[1,512,256]{2,1,0:T(8,128)(2,1)} %get-tuple-element.48) | copy-start | bytes 786436
  14.2 11.1 %copy-start = (bf16[512,2752]{0,1:T(8,128)(2,1)S(1)}, bf16[512,2752]{0,1:T(8,128)(2,1)}, u32[]{:S(2)}) copy-start(bf16[512,2752]{0,1:T(8,128)(2,1)} %param.9) | copy-start | bytes 8454148
  14.3 11.1 %copy-start.2 = (bf16[1,512,256]{2,1,0:T(8,128)(2,1)S(1)}, bf16[1,512,256]{2,1,0:T(8,128)(2,1)}, u32[]{:S(2)}) copy-start(bf16[1,512,256]{2,1,0:T(8,128)(2,1)} %get-tuple-element.47.mine) | copy-start | bytes 786436
  14.3 11.1 %collective-permute-start.2 = (bf16[1,2752,512]{2,1,0:T(8,128)(2,1)}, bf16[1,2752,512]{2,1,0:T(8,128)(2,1)S(1)}, u32[]{:S(2)}, u32[]{:S(2)}) collective-permute-start(bf16[1,2752,512]{2,1,0:T(8,128)(2,1)} %bitcast.24), channel_id=1, source_target_pairs={{0,4},{4,0},{8,12},{12,8},{16,20},{20,16},{24,28},{28,24},{32,36},... | collective-permute-start | bytes 8454152 | tf_op jit(solution)/shard_map/ppermute | solution.py:381
  21.1 19.1 %collective-permute-start.5 = (bf16[2,4,4,2,88,128]{5,4,3,2,1,0:T(8,128)(2,1)S(1)}, bf16[2,4,4,2,88,128]{5,4,3,2,1,0:T(8,128)(2,1)S(1)}, u32[]{:S(2)}, u32[]{:S(2)}) collective-permute-start(bf16[2,4,4,2,88,128]{5,4,3,2,1,0:T(8,128)(2,1)S(1)} %get-tuple-element.53), channel_id=1, source_target_pairs={{0,8},{4,28},{8,0},{12,20},{16,24},{20,12},{24,16},{28,4},{32,40},... | collective-permute-start | bytes 4325384 | tf_op jit(solution)/shard_map/ppermute | solution.py:383
  22.8 2.5 %collective-permute-start.3 = (bf16[1,512,256]{2,1,0:T(8,128)(2,1)S(1)}, bf16[1,512,256]{2,1,0:T(8,128)(2,1)S(1)}, u32[]{:S(2)}, u32[]{:S(2)}) collective-permute-start(bf16[1,512,256]{2,1,0:T(8,128)(2,1)S(1)} %copy-done.5), channel_id=1, source_target_pairs={{0,4},{4,0},{8,12},{12,8},{16,20},{20,16},{24,28},{28,24},{32,36},... | collective-permute-start | bytes 786440 | tf_op jit(solution)/shard_map/ppermute | solution.py:377
  27.8 11.4 %collective-permute-start.4 = (bf16[2,4,2,2,88,128]{5,4,3,2,1,0:T(8,128)(2,1)S(1)}, bf16[2,4,2,2,88,128]{5,4,3,2,1,0:T(8,128)(2,1)S(1)}, u32[]{:S(2)}, u32[]{:S(2)}) collective-permute-start(bf16[2,4,2,2,88,128]{5,4,3,2,1,0:T(8,128)(2,1)S(1)} %get-tuple-element.50), channel_id=1, source_target_pairs={{0,32},{4,100},{8,40},{12,108},{16,48},{20,116},{24,56},{28,124},{... | collective-permute-start | bytes 2162696 | tf_op jit(solution)/shard_map/ppermute | solution.py:385
  39.3 38.0 %copy-start.3 = (f32[3,1,86,512]{3,1,2,0:T(1,128)S(1)}, f32[3,1,86,512]{3,1,2,0:T(1,128)}, u32[]{:S(2)}) copy-start(f32[3,1,86,512]{3,1,2,0:T(1,128)} %param.13) | copy-start | bytes 1585156
  39.3 38.0 %copy-start.4 = (f32[3,1,86,512]{3,1,2,0:T(1,128)S(1)}, f32[3,1,86,512]{3,1,2,0:T(1,128)}, u32[]{:S(2)}) copy-start(f32[3,1,86,512]{3,1,2,0:T(1,128)} %param.12) | copy-start | bytes 1585156
  40.6 13.5 %collective-permute-start.6 = (bf16[1,4,4,2,88,128]{5,4,3,2,1,0:T(8,128)(2,1)S(1)}, bf16[1,4,4,2,88,128]{5,4,3,2,1,0:T(8,128)(2,1)S(1)}, u32[]{:S(2)}, u32[]{:S(2)}) collective-permute-start(bf16[1,4,4,2,88,128]{5,4,3,2,1,0:T(8,128)(2,1)S(1)} %get-tuple-element.55), channel_id=1, source_target_pairs={{0,24},{4,12},{8,16},{12,4},{16,8},{20,28},{24,0},{28,20},{32,56},... | collective-permute-start | bytes 2162696 | tf_op jit(solution)/shard_map/ppermute | solution.py:390
  43.5 9.4 %collective-permute-start.10 = (bf16[1,4,2,2,88,128]{5,4,3,2,1,0:T(8,128)(2,1)S(1)}, bf16[1,4,2,2,88,128]{5,4,3,2,1,0:T(8,128)(2,1)S(1)}, u32[]{:S(2)}, u32[]{:S(2)}) collective-permute-start(bf16[1,4,2,2,88,128]{5,4,3,2,1,0:T(8,128)(2,1)S(1)} %get-tuple-element.61), channel_id=1, source_target_pairs={{0,96},{4,36},{8,104},{12,44},{16,112},{20,52},{24,120},{28,60},{3... | collective-permute-start | bytes 1081352 | tf_op jit(solution)/shard_map/ppermute | solution.py:389
  53.0 7.2 %collective-permute-start.11 = (bf16[2,2,2,88,128]{4,3,2,1,0:T(8,128)(2,1)S(1)}, bf16[2,2,2,88,128]{4,3,2,1,0:T(8,128)(2,1)S(1)}, u32[]{:S(2)}, u32[]{:S(2)}) collective-permute-start(bf16[2,2,2,88,128]{4,3,2,1,0:T(8,128)(2,1)S(1)} %get-tuple-element.63), channel_id=1, source_target_pairs={{0,8},{4,28},{8,0},{12,20},{16,24},{20,12},{24,16},{28,4},{32,40},... | collective-permute-start | bytes 540680 | tf_op jit(solution)/shard_map/ppermute | solution.py:392
  54.2 11.9 %collective-permute-start.7 = (bf16[1,4,2,88,128]{4,3,2,1,0:T(8,128)(2,1)S(1)}, bf16[1,4,2,88,128]{4,3,2,1,0:T(8,128)(2,1)S(1)}, u32[]{:S(2)}, u32[]{:S(2)}) collective-permute-start(bf16[1,4,2,88,128]{4,3,2,1,0:T(8,128)(2,1)S(1)} %get-tuple-element.57), channel_id=1, source_target_pairs={{0,96},{4,36},{8,104},{12,44},{16,112},{20,52},{24,120},{28,60},{3... | collective-permute-start | bytes 540680 | tf_op jit(solution)/shard_map/ppermute | solution.py:396
  58.6 7.4 %collective-permute-start.8 = (bf16[1,4,2,88,128]{4,3,2,1,0:T(8,128)(2,1)S(1)}, bf16[1,4,2,88,128]{4,3,2,1,0:T(8,128)(2,1)S(1)}, u32[]{:S(2)}, u32[]{:S(2)}) collective-permute-start(bf16[1,4,2,88,128]{4,3,2,1,0:T(8,128)(2,1)S(1)} %get-tuple-element.58), channel_id=1, source_target_pairs={{0,32},{4,100},{8,40},{12,108},{16,48},{20,116},{24,56},{28,124},{... | collective-permute-start | bytes 540680 | tf_op jit(solution)/shard_map/ppermute | solution.py:396
  58.6 7.4 %collective-permute-start.9 = (bf16[1,4,2,88,128]{4,3,2,1,0:T(8,128)(2,1)S(1)}, bf16[1,4,2,88,128]{4,3,2,1,0:T(8,128)(2,1)S(1)}, u32[]{:S(2)}, u32[]{:S(2)}) collective-permute-start(bf16[1,4,2,88,128]{4,3,2,1,0:T(8,128)(2,1)S(1)} %get-tuple-element.59), channel_id=1, source_target_pairs={{0,64},{4,68},{8,72},{12,76},{16,80},{20,84},{24,88},{28,92},{32,9... | collective-permute-start | bytes 540680 | tf_op jit(solution)/shard_map/ppermute | solution.py:396
  60.2 5.8 %collective-permute-start.12 = (bf16[1,2,2,88,128]{4,3,2,1,0:T(8,128)(2,1)S(1)}, bf16[1,2,2,88,128]{4,3,2,1,0:T(8,128)(2,1)S(1)}, u32[]{:S(2)}, u32[]{:S(2)}) collective-permute-start(bf16[1,2,2,88,128]{4,3,2,1,0:T(8,128)(2,1)S(1)} %get-tuple-element.65), channel_id=1, source_target_pairs={{0,24},{4,12},{8,16},{12,4},{16,8},{20,28},{24,0},{28,20},{32,56},... | collective-permute-start | bytes 270344 | tf_op jit(solution)/shard_map/ppermute | solution.py:395
  66.9 19.4 %all-to-all-start = ((f32[128,1,128]{2,1,0:T(1,128)}), f32[128,1,128]{2,1,0:T(1,128)S(1)}, u32[]{:S(2)}, u32[]{:S(2)}) async-start(f32[128,1,128]{2,1,0:T(1,128)} %bitcast.9), calls=%async_computation | async-start | bytes 131072 | tf_op jit(solution)/shard_map/all_to_all | solution.py:399
  77.0 9.2 %collective-permute-start.13 = (bf16[3,88,256]{2,1,0:T(8,128)(2,1)S(1)}, bf16[3,88,256]{2,1,0:T(8,128)(2,1)S(1)}, u32[]{:S(2)}, u32[]{:S(2)}) collective-permute-start(bf16[3,88,256]{2,1,0:T(8,128)(2,1)S(1)} %get-tuple-element.68), channel_id=1, source_target_pairs={{0,4},{4,0},{8,12},{12,8},{16,20},{20,16},{24,28},{28,24},{32,36},... | collective-permute-start | bytes 405512 | tf_op jit(solution)/shard_map/ppermute | solution.py:398
  94.6 34.8 %all-to-all-start.1 = ((bf16[32,3,88,128]{3,2,1,0:T(8,128)(2,1)}), bf16[32,3,88,128]{3,2,1,0:T(8,128)(2,1)S(1)}, u32[]{:S(2)}, u32[]{:S(2)}) async-start(bf16[32,3,88,128]{3,2,1,0:T(8,128)(2,1)} %get-tuple-element.69), calls=%async_computation.1 | async-start | bytes 4325376 | tf_op jit(solution)/shard_map/all_to_all | solution.py:405

commit v8 on v7

--- a/solution.py
+++ b/solution.py
@@ -384,7 +384,6 @@
     za, zb = collect(False, hidden, hidden_there, kept_one, theirs_one)
     zr = lax.ppermute(zb, "dp", along_z(0))
     za, zb = split_sum(za, zr, 2)
-    xa, zb = lax.optimization_barrier((xa, zb))
     xa, xb = split_sum(xa, xr, 2)
     zr = lax.ppermute(zb, "dp", along_z(1))
     xr = lax.ppermute(xb, "dp", along_x(1))

time: 131 us -> 131 us (level)
    ppermute x1, waiting for transfers between devices: 0.92 us -> 10.5 us  [body(): xr = lax.ppermute(xb, 'dp', along_x(0))]
    ppermute x1, waiting for transfers between devices: 9.37 us -> 0.01 us  [body(): zr = lax.ppermute(zb, 'dp', along_z(0))]
  transfers between devices with their start and end apart: 16 -> 16, of which waited for: 8 -> 7; matrix products, arithmetic and copies ran while one was open for 3% -> 3% of each run, Pallas kernels for 17% -> 17%
where the time goes in v8:
time: 131 us
  waiting for transfers between devices  56 us (43%)
  starting transfers between devices  36.8 us (28%)
  Pallas kernels  33.4 us (25%)
  local copies, waits for them, and re-layouts  3.8 us (3%)
    all_to_all x1, waiting for transfers between devices, body(): pieces = lax.all_to_all(pieces, 'dp', 0, 0, tiled=True)  28.1 us
    pallas_call x2, Pallas kernels, project(): pl.pallas_call(functools.partial(project_kernel, first, steps, window), i...  12.9 us
    ppermute x1, waiting for transfers between devices, body(): xr = lax.ppermute(xb, 'dp', along_x(0))  10.5 us
    all_to_all x1, starting transfers between devices, body(): squares = lax.all_to_all(squares, ('dp', 'tensor'), 0, 0, tiled=True)  10.5 us
    pallas_call x2, Pallas kernels, collect(): pl.pallas_call(functools.partial(collect_kernel, x_first), grid=(N_Z,), i...  9.11 us
    pallas_call x1, Pallas kernels, update(): pl.pallas_call(functools.partial(update_kernel, limit_sq), grid=(steps,),...  8.32 us
    all_to_all x1, waiting for transfers between devices, body(): squares = lax.all_to_all(squares, ('dp', 'tensor'), 0, 0, tiled=True)  7.96 us
    ppermute x3, starting transfers between devices, body(): lax.ppermute(by_x[r], 'dp', direct_z(r))  6.01 us
  transfers between devices with their start and end apart: 16, of which 7 were waited for; matrix products, arithmetic and copies ran while one was open for 3% of the time, Pallas kernels for 17%

profile of v8, /device:TPU:0, one launch (start us, length us, event | category | flops | bytes accessed | tf_op | source)
XLA Modules:
  0.0 131.0 jit_solution(2536969686902664028)
XLA Ops:
  0.7 7.7 %project.2 = (bf16[2,512,256]{2,1,0:T(8,128)(2,1)}, bf16[2,512,256]{2,1,0:T(8,128)(2,1)}) custom-call(bf16[512,4096]{1,0:T(8,128)(2,1)} %x_hbm.2, bf16[3,4096,512]{2,1,0:T(8,128)(2,1)} %b_hbm.5), custom_call_target="tpu_custom_call" | custom-call | flops 4294967296 | bytes 12582912 | tf_op jit(solution)/shard_map/project/pallas_call | solution.py:124
  8.5 0.6 collective-permute-start.1
  9.1 5.1 %project.3 = (bf16[1,512,256]{2,1,0:T(8,128)(2,1)}, bf16[1,512,256]{2,1,0:T(8,128)(2,1)}) custom-call(bf16[512,4096]{1,0:T(8,128)(2,1)} %x_hbm.3, bf16[3,4096,512]{2,1,0:T(8,128)(2,1)} %b_hbm.5), custom_call_target="tpu_custom_call" | custom-call | flops 2147483648 | bytes 8388608 | tf_op jit(solution)/shard_map/project/pallas_call | solution.py:124
  14.4 6.7 %collect.2 = (bf16[2,4,4,2,88,128]{5,4,3,2,1,0:T(8,128)(2,1)S(1)}, bf16[2,4,4,2,88,128]{5,4,3,2,1,0:T(8,128)(2,1)S(1)}) custom-call(bf16[2,2752,512]{2,1,0:T(8,128)(2,1)S(1)} %bitcast.23, bf16[2,2752,512]{2,1,0:T(8,128)(2,1)} %collective-permute-done.h, bf16[2,512,256]{2,1,0:T(8,128)(2,1)S(1)} %copy-done.1, bf16[2,512,256]{2,1,0:T(8,128)(2,1)} %collective-permute-done.1.theirs), custom_call_target="tpu_custom_call" | custom-call | flops 2885681152 | bytes 14090240 | tf_op jit(solution)/shard_map/collect/pallas_call | solution.py:198
  21.1 1.7 %collective-permute-start.2 = (bf16[2,4,4,2,88,128]{5,4,3,2,1,0:T(8,128)(2,1)S(1)}, bf16[2,4,4,2,88,128]{5,4,3,2,1,0:T(8,128)(2,1)S(1)}, u32[]{:S(2)}, u32[]{:S(2)}) collective-permute-start(bf16[2,4,4,2,88,128]{5,4,3,2,1,0:T(8,128)(2,1)S(1)} %get-tuple-element.44), channel_id=1, source_target_pairs={{0,8},{4,28},{8,0},{12,20},{16,24},{20,12},{24,16},{28,4},{32,40},... | collective-permute-start | bytes 4325384 | tf_op jit(solution)/shard_map/ppermute | solution.py:383
  22.8 1.4 %collective-permute-start.8 = (bf16[1,512,256]{2,1,0:T(8,128)(2,1)S(1)}, bf16[1,512,256]{2,1,0:T(8,128)(2,1)S(1)}, u32[]{:S(2)}, u32[]{:S(2)}) collective-permute-start(bf16[1,512,256]{2,1,0:T(8,128)(2,1)S(1)} %copy-done.5), channel_id=1, source_target_pairs={{0,4},{4,0},{8,12},{12,8},{16,20},{20,16},{24,28},{28,24},{32,36},... | collective-permute-start | bytes 786440 | tf_op jit(solution)/shard_map/ppermute | solution.py:377
  24.2 1.2 collective-permute-done.8.theirs
  25.4 2.4 %collect.3 = (bf16[2,4,2,2,88,128]{5,4,3,2,1,0:T(8,128)(2,1)S(1)}, bf16[2,4,2,2,88,128]{5,4,3,2,1,0:T(8,128)(2,1)S(1)}) custom-call(bf16[1,2752,512]{2,1,0:T(8,128)(2,1)S(1)} %bitcast.25, bf16[1,2752,512]{2,1,0:T(8,128)(2,1)S(1)} %collective-permute-done.7.h, bf16[1,512,256]{2,1,0:T(8,128)(2,1)S(1)} %copy-done.2, ...), custom_call_target="tpu_custom_call" | custom-call | flops 1442840576 | bytes 7045120 | tf_op jit(solution)/shard_map/collect/pallas_call | solution.py:198
  27.8 2.0 %collective-permute-start.9 = (bf16[2,4,2,2,88,128]{5,4,3,2,1,0:T(8,128)(2,1)S(1)}, bf16[2,4,2,2,88,128]{5,4,3,2,1,0:T(8,128)(2,1)S(1)}, u32[]{:S(2)}, u32[]{:S(2)}) collective-permute-start(bf16[2,4,2,2,88,128]{5,4,3,2,1,0:T(8,128)(2,1)S(1)} %get-tuple-element.55), channel_id=1, source_target_pairs={{0,32},{4,100},{8,40},{12,108},{16,48},{20,116},{24,56},{28,124},{... | collective-permute-start | bytes 2162696 | tf_op jit(solution)/shard_map/ppermute | solution.py:385
  29.7 10.5 %collective-permute-done.2.recv = bf16[2,4,4,2,88,128]{5,4,3,2,1,0:T(8,128)(2,1)S(1)} collective-permute-done((bf16[2,4,4,2,88,128]{5,4,3,2,1,0:T(8,128)(2,1)S(1)}, bf16[2,4,4,2,88,128]{5,4,3,2,1,0:T(8,128)(2,1)S(1)}, u32[]{:S(2)}, u32[]{:S(2)}) %collective-permute-start.2) | collective-permute-done | bytes 1441824 | tf_op jit(solution)/shard_map/ppermute | solution.py:383
  40.2 0.3 split_sum.5
  40.6 2.9 %collective-permute-start.3 = (bf16[1,4,4,2,88,128]{5,4,3,2,1,0:T(8,128)(2,1)S(1)}, bf16[1,4,4,2,88,128]{5,4,3,2,1,0:T(8,128)(2,1)S(1)}, u32[]{:S(2)}, u32[]{:S(2)}) collective-permute-start(bf16[1,4,4,2,88,128]{5,4,3,2,1,0:T(8,128)(2,1)S(1)} %get-tuple-element.46), channel_id=1, source_target_pairs={{0,24},{4,12},{8,16},{12,4},{16,8},{20,28},{24,0},{28,20},{32,56},... | collective-permute-start | bytes 2162696 | tf_op jit(solution)/shard_map/ppermute | solution.py:389
  43.5 0.2 split_sum.7
  43.7 4.1 %collective-permute-start.10 = (bf16[1,4,2,2,88,128]{5,4,3,2,1,0:T(8,128)(2,1)S(1)}, bf16[1,4,2,2,88,128]{5,4,3,2,1,0:T(8,128)(2,1)S(1)}, u32[]{:S(2)}, u32[]{:S(2)}) collective-permute-start(bf16[1,4,2,2,88,128]{5,4,3,2,1,0:T(8,128)(2,1)S(1)} %get-tuple-element.57), channel_id=1, source_target_pairs={{0,96},{4,36},{8,104},{12,44},{16,112},{20,52},{24,120},{28,60},{3... | collective-permute-start | bytes 1081352 | tf_op jit(solution)/shard_map/ppermute | solution.py:388
  47.8 5.4 %collective-permute-done.10 = bf16[1,4,2,2,88,128]{5,4,3,2,1,0:T(8,128)(2,1)S(1)} collective-permute-done((bf16[1,4,2,2,88,128]{5,4,3,2,1,0:T(8,128)(2,1)S(1)}, bf16[1,4,2,2,88,128]{5,4,3,2,1,0:T(8,128)(2,1)S(1)}, u32[]{:S(2)}, u32[]{:S(2)}) %collective-permute-start.10) | collective-permute-done | bytes 360480 | tf_op jit(solution)/shard_map/ppermute | solution.py:388
  53.3 0.3 collective-permute-start.11
  53.6 0.2 collective-permute-done.3
  53.8 0.2 split_sum.6
  54.0 4.5 %collective-permute-start.4 = (bf16[1,4,2,88,128]{4,3,2,1,0:T(8,128)(2,1)S(1)}, bf16[1,4,2,88,128]{4,3,2,1,0:T(8,128)(2,1)S(1)}, u32[]{:S(2)}, u32[]{:S(2)}) collective-permute-start(bf16[1,4,2,88,128]{4,3,2,1,0:T(8,128)(2,1)S(1)} %get-tuple-element.48), channel_id=1, source_target_pairs={{0,96},{4,36},{8,104},{12,44},{16,112},{20,52},{24,120},{28,60},{3... | collective-permute-start | bytes 540680 | tf_op jit(solution)/shard_map/ppermute | solution.py:395
  58.4 1.6 %collective-permute-start.6 = (bf16[1,4,2,88,128]{4,3,2,1,0:T(8,128)(2,1)S(1)}, bf16[1,4,2,88,128]{4,3,2,1,0:T(8,128)(2,1)S(1)}, u32[]{:S(2)}, u32[]{:S(2)}) collective-permute-start(bf16[1,4,2,88,128]{4,3,2,1,0:T(8,128)(2,1)S(1)} %get-tuple-element.50), channel_id=1, source_target_pairs={{0,64},{4,68},{8,72},{12,76},{16,80},{20,84},{24,88},{28,92},{32,9... | collective-permute-start | bytes 540680 | tf_op jit(solution)/shard_map/ppermute | solution.py:395
  60.0 3.1 %collective-permute-start.12 = (bf16[1,2,2,88,128]{4,3,2,1,0:T(8,128)(2,1)S(1)}, bf16[1,2,2,88,128]{4,3,2,1,0:T(8,128)(2,1)S(1)}, u32[]{:S(2)}, u32[]{:S(2)}) collective-permute-start(bf16[1,2,2,88,128]{4,3,2,1,0:T(8,128)(2,1)S(1)} %get-tuple-element.61), channel_id=1, source_target_pairs={{0,24},{4,12},{8,16},{12,4},{16,8},{20,28},{24,0},{28,20},{32,56},... | collective-permute-start | bytes 270344 | tf_op jit(solution)/shard_map/ppermute | solution.py:394
  63.1 2.7 %collective-permute-done.12.refs_5_ = bf16[1,2,2,88,128]{4,3,2,1,0:T(8,128)(2,1)S(1)} collective-permute-done((bf16[1,2,2,88,128]{4,3,2,1,0:T(8,128)(2,1)S(1)}, bf16[1,2,2,88,128]{4,3,2,1,0:T(8,128)(2,1)S(1)}, u32[]{:S(2)}, u32[]{:S(2)}) %collective-permute-start.12) | collective-permute-done | bytes 90144 | tf_op jit(solution)/shard_map/ppermute | solution.py:394
  65.9 0.8 owned_sum.1
  66.7 10.5 %all-to-all-start = ((f32[128,1,128]{2,1,0:T(1,128)}), f32[128,1,128]{2,1,0:T(1,128)S(1)}, u32[]{:S(2)}, u32[]{:S(2)}) async-start(f32[128,1,128]{2,1,0:T(1,128)} %bitcast.9), calls=%async_computation | async-start | bytes 131072 | tf_op jit(solution)/shard_map/all_to_all | solution.py:398
  77.1 1.1 copy_bitcast_fusion
  78.2 8.0 %all-to-all-done = f32[128,1,128]{2,1,0:T(1,128)S(1)} async-done(((f32[128,1,128]{2,1,0:T(1,128)}), f32[128,1,128]{2,1,0:T(1,128)S(1)}, u32[]{:S(2)}, u32[]{:S(2)}) %all-to-all-start) | async-done | bytes 65568 | tf_op jit(solution)/shard_map/all_to_all | solution.py:398
  86.2 8.3 %update.1 = (f32[3,86,512]{2,1,0:T(8,128)S(1)}, f32[3,86,512]{2,1,0:T(8,128)S(1)}, bf16[32,3,88,128]{3,2,1,0:T(8,128)(2,1)}) custom-call(f32[128,128]{1,0:T(8,128)S(1)} %bitcast.32, f32[3,88,256]{2,1,0:T(8,128)S(1)} %get-tuple-element.63.mine, bf16[3,88,256]{2,1,0:T(8,128)(2,1)S(1)} %collective-permute-done.13.recv, f32[3,86,512]{2,1,0:T(8,128)} %get-tuple-element.82.first, ...), custom_call_target="tpu_custom_call" | custom-call | tf_op jit(solution)/shard_map/update/pallas_call | solution.py:318
  94.5 4.1 %all-to-all-start.1 = ((bf16[32,3,88,128]{3,2,1,0:T(8,128)(2,1)}), bf16[32,3,88,128]{3,2,1,0:T(8,128)(2,1)S(1)}, u32[]{:S(2)}, u32[]{:S(2)}) async-start(bf16[32,3,88,128]{3,2,1,0:T(8,128)(2,1)} %get-tuple-element.65), calls=%async_computation.1 | async-start | bytes 4325376 | tf_op jit(solution)/shard_map/all_to_all | solution.py:404
  98.6 1.3 %copy.15 = f32[3,1,86,512]{3,1,2,0:T(1,128)} copy(f32[3,1,86,512]{3,2,0,1:T(8,128)S(1)} %bitcast.29) | data formatting | bytes 1056768
  99.9 1.3 %copy.16 = f32[3,1,86,512]{3,1,2,0:T(1,128)} copy(f32[3,1,86,512]{3,2,0,1:T(8,128)S(1)} %bitcast.28) | data formatting | bytes 1056768
  101.3 28.1 %all-to-all-done.1.pieces = bf16[32,3,88,128]{3,2,1,0:T(8,128)(2,1)S(1)} async-done(((bf16[32,3,88,128]{3,2,1,0:T(8,128)(2,1)}), bf16[32,3,88,128]{3,2,1,0:T(8,128)(2,1)S(1)}, u32[]{:S(2)}, u32[]{:S(2)}) %all-to-all-start.1) | async-done | bytes 2162720 | tf_op jit(solution)/shard_map/all_to_all | solution.py:404
  129.3 1.5 %layout.1 = (bf16[2752,128]{1,0:T(8,128)(2,1)}, bf16[2752,128]{1,0:T(8,128)(2,1)}, bf16[2752,128]{1,0:T(8,128)(2,1)}) custom-call(bf16[32,3,88,128]{3,2,1,0:T(8,128)(2,1)S(1)} %all-to-all-done.1.pieces), custom_call_target="tpu_custom_call" | custom-call | tf_op jit(solution)/shard_map/layout/pallas_call | solution.py:353
  (32 shorter events, 0.4 us)
Async XLA Ops:
  0.6 13.7 %collective-permute-start = (bf16[2,2752,512]{2,1,0:T(8,128)(2,1)}, bf16[2,2752,512]{2,1,0:T(8,128)(2,1)}, u32[]{:S(2)}, u32[]{:S(2)}) collective-permute-start(bf16[2,2752,512]{2,1,0:T(8,128)(2,1)} %bitcast.20), channel_id=1, source_target_pairs={{0,4},{4,0},{8,12},{12,8},{16,20},{20,16},{24,28},{28,24},{32,36},... | collective-permute-start | bytes 16908296 | tf_op jit(solution)/shard_map/ppermute | solution.py:373
  8.5 5.9 %slice-start = ((s8[5636096]{0:T(1024)(128)(4,1)}), s8[4194304]{0:T(1024)(128)(4,1)S(1)}, s32[]{:S(2)}) async-start(s8[5636096]{0:T(1024)(128)(4,1)} %bitcast.21), calls=%async_computation.2 | async-start | bytes 8388608
  8.5 5.9 %slice-start.1 = ((s8[5636096]{0:T(1024)(128)(4,1)}), s8[1441792]{0:T(1024)(128)(4,1)S(1)}, s32[]{:S(2)}) async-start(s8[5636096]{0:T(1024)(128)(4,1)} %bitcast.21), calls=%async_computation.3 | async-start | bytes 2883584
  8.5 5.9 %copy-start.1 = (bf16[2,512,256]{2,1,0:T(8,128)(2,1)S(1)}, bf16[2,512,256]{2,1,0:T(8,128)(2,1)}, u32[]{:S(2)}) copy-start(bf16[2,512,256]{2,1,0:T(8,128)(2,1)} %get-tuple-element.41.mine) | copy-start | bytes 1572868
  8.5 5.7 %collective-permute-start.1 = (bf16[2,512,256]{2,1,0:T(8,128)(2,1)}, bf16[2,512,256]{2,1,0:T(8,128)(2,1)}, u32[]{:S(2)}, u32[]{:S(2)}) collective-permute-start(bf16[2,512,256]{2,1,0:T(8,128)(2,1)} %get-tuple-element.40), channel_id=1, source_target_pairs={{0,4},{4,0},{8,12},{12,8},{16,20},{20,16},{24,28},{28,24},{32,36},... | collective-permute-start | bytes 1572872 | tf_op jit(solution)/shard_map/ppermute | solution.py:375
  14.2 8.6 %copy-start.5 = (bf16[1,512,256]{2,1,0:T(8,128)(2,1)S(1)}, bf16[1,512,256]{2,1,0:T(8,128)(2,1)}, u32[]{:S(2)}) copy-start(bf16[1,512,256]{2,1,0:T(8,128)(2,1)} %get-tuple-element.53) | copy-start | bytes 786436
  14.2 11.1 %copy-start = (bf16[512,2752]{0,1:T(8,128)(2,1)S(1)}, bf16[512,2752]{0,1:T(8,128)(2,1)}, u32[]{:S(2)}) copy-start(bf16[512,2752]{0,1:T(8,128)(2,1)} %param.9) | copy-start | bytes 8454148
  14.3 11.1 %copy-start.2 = (bf16[1,512,256]{2,1,0:T(8,128)(2,1)S(1)}, bf16[1,512,256]{2,1,0:T(8,128)(2,1)}, u32[]{:S(2)}) copy-start(bf16[1,512,256]{2,1,0:T(8,128)(2,1)} %get-tuple-element.52.mine) | copy-start | bytes 786436
  14.3 11.1 %collective-permute-start.7 = (bf16[1,2752,512]{2,1,0:T(8,128)(2,1)}, bf16[1,2752,512]{2,1,0:T(8,128)(2,1)S(1)}, u32[]{:S(2)}, u32[]{:S(2)}) collective-permute-start(bf16[1,2752,512]{2,1,0:T(8,128)(2,1)} %bitcast.24), channel_id=1, source_target_pairs={{0,4},{4,0},{8,12},{12,8},{16,20},{20,16},{24,28},{28,24},{32,36},... | collective-permute-start | bytes 8454152 | tf_op jit(solution)/shard_map/ppermute | solution.py:381
  21.1 19.1 %collective-permute-start.2 = (bf16[2,4,4,2,88,128]{5,4,3,2,1,0:T(8,128)(2,1)S(1)}, bf16[2,4,4,2,88,128]{5,4,3,2,1,0:T(8,128)(2,1)S(1)}, u32[]{:S(2)}, u32[]{:S(2)}) collective-permute-start(bf16[2,4,4,2,88,128]{5,4,3,2,1,0:T(8,128)(2,1)S(1)} %get-tuple-element.44), channel_id=1, source_target_pairs={{0,8},{4,28},{8,0},{12,20},{16,24},{20,12},{24,16},{28,4},{32,40},... | collective-permute-start | bytes 4325384 | tf_op jit(solution)/shard_map/ppermute | solution.py:383
  22.8 2.5 %collective-permute-start.8 = (bf16[1,512,256]{2,1,0:T(8,128)(2,1)S(1)}, bf16[1,512,256]{2,1,0:T(8,128)(2,1)S(1)}, u32[]{:S(2)}, u32[]{:S(2)}) collective-permute-start(bf16[1,512,256]{2,1,0:T(8,128)(2,1)S(1)} %copy-done.5), channel_id=1, source_target_pairs={{0,4},{4,0},{8,12},{12,8},{16,20},{20,16},{24,28},{28,24},{32,36},... | collective-permute-start | bytes 786440 | tf_op jit(solution)/shard_map/ppermute | solution.py:377
  27.8 15.8 %collective-permute-start.9 = (bf16[2,4,2,2,88,128]{5,4,3,2,1,0:T(8,128)(2,1)S(1)}, bf16[2,4,2,2,88,128]{5,4,3,2,1,0:T(8,128)(2,1)S(1)}, u32[]{:S(2)}, u32[]{:S(2)}) collective-permute-start(bf16[2,4,2,2,88,128]{5,4,3,2,1,0:T(8,128)(2,1)S(1)} %get-tuple-element.55), channel_id=1, source_target_pairs={{0,32},{4,100},{8,40},{12,108},{16,48},{20,116},{24,56},{28,124},{... | collective-permute-start | bytes 2162696 | tf_op jit(solution)/shard_map/ppermute | solution.py:385
  40.6 36.6 %copy-start.3 = (f32[3,1,86,512]{3,1,2,0:T(1,128)S(1)}, f32[3,1,86,512]{3,1,2,0:T(1,128)}, u32[]{:S(2)}) copy-start(f32[3,1,86,512]{3,1,2,0:T(1,128)} %param.13) | copy-start | bytes 1585156
  40.6 36.6 %copy-start.4 = (f32[3,1,86,512]{3,1,2,0:T(1,128)S(1)}, f32[3,1,86,512]{3,1,2,0:T(1,128)}, u32[]{:S(2)}) copy-start(f32[3,1,86,512]{3,1,2,0:T(1,128)} %param.12) | copy-start | bytes 1585156
  40.6 13.2 %collective-permute-start.3 = (bf16[1,4,4,2,88,128]{5,4,3,2,1,0:T(8,128)(2,1)S(1)}, bf16[1,4,4,2,88,128]{5,4,3,2,1,0:T(8,128)(2,1)S(1)}, u32[]{:S(2)}, u32[]{:S(2)}) collective-permute-start(bf16[1,4,4,2,88,128]{5,4,3,2,1,0:T(8,128)(2,1)S(1)} %get-tuple-element.46), channel_id=1, source_target_pairs={{0,24},{4,12},{8,16},{12,4},{16,8},{20,28},{24,0},{28,20},{32,56},... | collective-permute-start | bytes 2162696 | tf_op jit(solution)/shard_map/ppermute | solution.py:389
  43.7 9.5 %collective-permute-start.10 = (bf16[1,4,2,2,88,128]{5,4,3,2,1,0:T(8,128)(2,1)S(1)}, bf16[1,4,2,2,88,128]{5,4,3,2,1,0:T(8,128)(2,1)S(1)}, u32[]{:S(2)}, u32[]{:S(2)}) collective-permute-start(bf16[1,4,2,2,88,128]{5,4,3,2,1,0:T(8,128)(2,1)S(1)} %get-tuple-element.57), channel_id=1, source_target_pairs={{0,96},{4,36},{8,104},{12,44},{16,112},{20,52},{24,120},{28,60},{3... | collective-permute-start | bytes 1081352 | tf_op jit(solution)/shard_map/ppermute | solution.py:388
  53.3 6.7 %collective-permute-start.11 = (bf16[2,2,2,88,128]{4,3,2,1,0:T(8,128)(2,1)S(1)}, bf16[2,2,2,88,128]{4,3,2,1,0:T(8,128)(2,1)S(1)}, u32[]{:S(2)}, u32[]{:S(2)}) collective-permute-start(bf16[2,2,2,88,128]{4,3,2,1,0:T(8,128)(2,1)S(1)} %get-tuple-element.59), channel_id=1, source_target_pairs={{0,8},{4,28},{8,0},{12,20},{16,24},{20,12},{24,16},{28,4},{32,40},... | collective-permute-start | bytes 540680 | tf_op jit(solution)/shard_map/ppermute | solution.py:391
  54.0 11.9 %collective-permute-start.4 = (bf16[1,4,2,88,128]{4,3,2,1,0:T(8,128)(2,1)S(1)}, bf16[1,4,2,88,128]{4,3,2,1,0:T(8,128)(2,1)S(1)}, u32[]{:S(2)}, u32[]{:S(2)}) collective-permute-start(bf16[1,4,2,88,128]{4,3,2,1,0:T(8,128)(2,1)S(1)} %get-tuple-element.48), channel_id=1, source_target_pairs={{0,96},{4,36},{8,104},{12,44},{16,112},{20,52},{24,120},{28,60},{3... | collective-permute-start | bytes 540680 | tf_op jit(solution)/shard_map/ppermute | solution.py:395
  58.4 7.4 %collective-permute-start.5 = (bf16[1,4,2,88,128]{4,3,2,1,0:T(8,128)(2,1)S(1)}, bf16[1,4,2,88,128]{4,3,2,1,0:T(8,128)(2,1)S(1)}, u32[]{:S(2)}, u32[]{:S(2)}) collective-permute-start(bf16[1,4,2,88,128]{4,3,2,1,0:T(8,128)(2,1)S(1)} %get-tuple-element.49), channel_id=1, source_target_pairs={{0,32},{4,100},{8,40},{12,108},{16,48},{20,116},{24,56},{28,124},{... | collective-permute-start | bytes 540680 | tf_op jit(solution)/shard_map/ppermute | solution.py:395
  58.4 7.4 %collective-permute-start.6 = (bf16[1,4,2,88,128]{4,3,2,1,0:T(8,128)(2,1)S(1)}, bf16[1,4,2,88,128]{4,3,2,1,0:T(8,128)(2,1)S(1)}, u32[]{:S(2)}, u32[]{:S(2)}) collective-permute-start(bf16[1,4,2,88,128]{4,3,2,1,0:T(8,128)(2,1)S(1)} %get-tuple-element.50), channel_id=1, source_target_pairs={{0,64},{4,68},{8,72},{12,76},{16,80},{20,84},{24,88},{28,92},{32,9... | collective-permute-start | bytes 540680 | tf_op jit(solution)/shard_map/ppermute | solution.py:395
  60.0 5.8 %collective-permute-start.12 = (bf16[1,2,2,88,128]{4,3,2,1,0:T(8,128)(2,1)S(1)}, bf16[1,2,2,88,128]{4,3,2,1,0:T(8,128)(2,1)S(1)}, u32[]{:S(2)}, u32[]{:S(2)}) collective-permute-start(bf16[1,2,2,88,128]{4,3,2,1,0:T(8,128)(2,1)S(1)} %get-tuple-element.61), channel_id=1, source_target_pairs={{0,24},{4,12},{8,16},{12,4},{16,8},{20,28},{24,0},{28,20},{32,56},... | collective-permute-start | bytes 270344 | tf_op jit(solution)/shard_map/ppermute | solution.py:394
  66.6 19.5 %collective-permute-start.13 = (bf16[3,88,256]{2,1,0:T(8,128)(2,1)S(1)}, bf16[3,88,256]{2,1,0:T(8,128)(2,1)S(1)}, u32[]{:S(2)}, u32[]{:S(2)}) collective-permute-start(bf16[3,88,256]{2,1,0:T(8,128)(2,1)S(1)} %get-tuple-element.64), channel_id=1, source_target_pairs={{0,4},{4,0},{8,12},{12,8},{16,20},{20,16},{24,28},{28,24},{32,36},... | collective-permute-start | bytes 405512 | tf_op jit(solution)/shard_map/ppermute | solution.py:397
  66.7 19.5 %all-to-all-start = ((f32[128,1,128]{2,1,0:T(1,128)}), f32[128,1,128]{2,1,0:T(1,128)S(1)}, u32[]{:S(2)}, u32[]{:S(2)}) async-start(f32[128,1,128]{2,1,0:T(1,128)} %bitcast.9), calls=%async_computation | async-start | bytes 131072 | tf_op jit(solution)/shard_map/all_to_all | solution.py:398
  94.5 34.8 %all-to-all-start.1 = ((bf16[32,3,88,128]{3,2,1,0:T(8,128)(2,1)}), bf16[32,3,88,128]{3,2,1,0:T(8,128)(2,1)S(1)}, u32[]{:S(2)}, u32[]{:S(2)}) async-start(bf16[32,3,88,128]{3,2,1,0:T(8,128)(2,1)} %get-tuple-element.65), calls=%async_computation.1 | async-start | bytes 4325376 | tf_op jit(solution)/shard_map/all_to_all | solution.py:404
